TPU v7x, 32 devices: a whole 2x2x4 slice. The times are simulated.
32 devices in a mesh: dp: 8 (over z, x), tensor: 4 (over y, core).
Axes of the slice: x: 2, y: 2, z: 4, core: 2. Of those that a mesh axis runs over, the one named last changes fastest.
Arguments:
- tokens: bfloat16 [4096, 2048], P('dp'), may hold values from -6 to 6
- segments: int32 [8, 512], P('dp'), may hold values from 0 to 2, as said below
- positions: int32 [8, 512], P('dp'), may hold values from 0 to 1789, as said below
- attn_gain: float32 [2048], replicated, may hold values from 0.5 to 1.5
- w_query: bfloat16 [2048, 2048], P(None, 'tensor'), may hold values from -0.125 to 0.125
- key_weight: bfloat16 [2048, 512], P(None, 'tensor'), may hold values from -0.125 to 0.125
- value_weight: bfloat16 [2048, 512], P(None, 'tensor'), may hold values from -0.125 to 0.125
- w_out: bfloat16 [2048, 2048], P('tensor'), may hold values from -1 to 1
- mlp_gain: float32 [2048], replicated, may hold values from 0.5 to 1.5
- w_gate: bfloat16 [2048, 8192], P(None, 'tensor'), may hold values from -0.125 to 0.125
- w_up: bfloat16 [2048, 8192], P(None, 'tensor'), may hold values from -0.125 to 0.125
- w_down: bfloat16 [8192, 2048], P('tensor'), may hold values from -0.0625 to 0.0625
- cotangent: bfloat16 [4096, 2048], P('dp'), may hold values from -6 to 6
Outputs:
- mixed: bfloat16 [4096, 2048], P('dp')
- grad_input: float32 [4096, 2048], P('dp')
- grad_attn_gain: float32 [2048], P('dp')
- grad_w_query: float32 [2048, 2048], P('dp', 'tensor')
- grad_w_key: float32 [2048, 512], P('dp', 'tensor')
- grad_w_value: float32 [2048, 512], P('dp', 'tensor')
- grad_w_out: float32 [2048, 2048], P('tensor', 'dp')
- grad_mlp_gain: float32 [2048], P('dp')
- grad_w_gate: float32 [2048, 8192], P('dp', 'tensor')
- grad_w_up: float32 [2048, 8192], P('dp', 'tensor')
- grad_w_down: float32 [8192, 2048], P('tensor', 'dp')
Inputs may be any that keep to these rules, and one draw needn't show every extreme that they name: `segments`: within each sequence the segment numbers start at 0, never fall, and every sequence holds three documents. positions count up by one inside each document; the second and third documents of a sequence start at 0, the first may start higher.
All inputs are finite; a program needn't handle non-finite values.
Results may differ from a plain program's by a relative error of at most 0.014.
Values sent between devices are 32-bit elements; how exact they have to be, the bound alone decides.
A program may use at most 256 MiB of HBM per device.

v0:
```python
import jax
import jax.numpy as jnp
from jax import lax
from jax.sharding import PartitionSpec as P

HEAD_SIZE = 64


EPSILON = 1e-05
MASKED = -1e30


def product(left_matrix, right_matrix):
    return jnp.dot(left_matrix, right_matrix, preferred_element_type=jnp.float32)


def over_rows(left_matrix, right_matrix):
    return lax.dot_general(
        left_matrix, right_matrix, (((0,), (0,)), ((), ())), preferred_element_type=jnp.float32
    )


def against(gradient, weight):
    return lax.dot_general(
        gradient, weight, (((1,), (1,)), ((), ())), preferred_element_type=jnp.float32
    )


def normalize(values, gain):
    norm_scale = lax.rsqrt(jnp.mean(values * values, axis=-1, keepdims=True) + EPSILON)
    return (values * norm_scale * gain, norm_scale)


def norm_backward(incoming, values, norm_scale, gain):
    weighted = incoming * gain
    inner_mean = jnp.mean(weighted * values, axis=-1, keepdims=True)
    row_grad = norm_scale * weighted - values * (norm_scale * norm_scale * norm_scale) * inner_mean
    return (row_grad, jnp.sum(incoming * values * norm_scale, axis=0))


def tables(places):
    half_dim = HEAD_SIZE // 2
    frequency = 500000.0 ** (-(jnp.arange(half_dim).astype(jnp.float32) * 2.0 / HEAD_SIZE))
    angles = places.astype(jnp.float32)[..., None] * frequency
    cosine_lookup = jnp.cos(angles)
    sine_lookup = jnp.sin(angles)
    return (
        jnp.concatenate([cosine_lookup, cosine_lookup], -1),
        jnp.concatenate([sine_lookup, sine_lookup], -1),
    )


def apply_rotary(field, cosine_lookup, sine_lookup):
    half_dim = HEAD_SIZE // 2
    turned = jnp.concatenate([-field[..., half_dim:], field[..., :half_dim]], -1)
    return field * cosine_lookup + turned * sine_lookup


def unrotate(gradient, cosine_lookup, sine_lookup):
    half_dim = HEAD_SIZE // 2
    sined = gradient * sine_lookup
    return gradient * cosine_lookup + jnp.concatenate(
        [sined[..., half_dim:], -sined[..., :half_dim]], -1
    )


def allowed_pairs(segment):
    spots = jnp.arange(segment.shape[0])
    return (spots[:, None] >= spots[None, :]) & (segment[:, None] == segment[None, :])


def scores(query_rotated, key_rotated, segment):
    raw_scores = jnp.einsum(
        "qhgd,khd->hgqk", query_rotated, key_rotated, preferred_element_type=jnp.float32
    ) * HEAD_SIZE ** (-0.5)
    return jnp.where(allowed_pairs(segment), raw_scores, MASKED)


def attend_forward(block_args):
    query_rotated, key_rotated, value_seq, segment = block_args
    masked = scores(query_rotated, key_rotated, segment)
    row_peak = jnp.max(masked, axis=-1, keepdims=True)
    log_total = row_peak + jnp.log(jnp.sum(jnp.exp(masked - row_peak), axis=-1, keepdims=True))
    attention_probs = jnp.exp(masked - log_total).astype(jnp.bfloat16)
    combined_heads = jnp.einsum(
        "ojus,sov->uojv", attention_probs, value_seq, preferred_element_type=jnp.float32
    )
    return (combined_heads, log_total)


def attend_backward(block_args):
    query_rotated, key_rotated, value_seq, segment, log_total, grad_heads = block_args
    masked = scores(query_rotated, key_rotated, segment)
    attention_probs = jnp.exp(masked - log_total)
    grad_probs = jnp.einsum(
        "qhgd,khd->hgqk", grad_heads, value_seq, preferred_element_type=jnp.float32
    )
    row_sum = jnp.sum(attention_probs * grad_probs, axis=-1, keepdims=True)
    grad_raw = jnp.where(
        allowed_pairs(segment), attention_probs * (grad_probs - row_sum), 0.0
    ).astype(jnp.bfloat16)
    factor = HEAD_SIZE ** (-0.5)
    grad_query_rot = (
        jnp.einsum("ojus,sov->uojv", grad_raw, key_rotated, preferred_element_type=jnp.float32)
        * factor
    )
    grad_key_rot = (
        jnp.einsum("hgqk,qhgd->khd", grad_raw, query_rotated, preferred_element_type=jnp.float32)
        * factor
    )
    grad_value_rot = jnp.einsum(
        "hgqk,qhgd->khd",
        attention_probs.astype(jnp.bfloat16),
        grad_heads,
        preferred_element_type=jnp.float32,
    )
    return (grad_query_rot, grad_key_rot, grad_value_rot)


def body(
    tokens,
    segments,
    positions,
    attn_gain,
    w_query,
    key_weight,
    value_weight,
    w_out,
    mlp_gain,
    w_gate,
    w_up,
    w_down,
    cotangent,
):
    inputs = tokens.astype(jnp.float32)
    row_count = inputs.shape[0]
    seq_count, seq_len = segments.shape
    query_heads = w_query.shape[1] // HEAD_SIZE
    kv_heads = key_weight.shape[1] // HEAD_SIZE
    group_size = query_heads // kv_heads
    normed_one, scale_one = normalize(inputs, attn_gain)
    normed_one = normed_one.astype(jnp.bfloat16)
    cosine_lookup, sine_lookup = tables(positions.reshape(row_count))
    cosine_lookup = cosine_lookup[:, None, :]
    sine_lookup = sine_lookup[:, None, :]
    query_projected = product(normed_one, w_query).reshape(row_count, query_heads, HEAD_SIZE)
    key_projected = product(normed_one, key_weight).reshape(row_count, kv_heads, HEAD_SIZE)
    query_rotated = (
        apply_rotary(query_projected, cosine_lookup, sine_lookup)
        .astype(jnp.bfloat16)
        .reshape(seq_count, seq_len, kv_heads, group_size, HEAD_SIZE)
    )
    key_rotated = (
        apply_rotary(key_projected, cosine_lookup, sine_lookup)
        .astype(jnp.bfloat16)
        .reshape(seq_count, seq_len, kv_heads, HEAD_SIZE)
    )
    value_projected = (
        product(normed_one, value_weight)
        .astype(jnp.bfloat16)
        .reshape(seq_count, seq_len, kv_heads, HEAD_SIZE)
    )
    combined_heads, log_totals = lax.map(
        attend_forward, (query_rotated, key_rotated, value_projected, segments)
    )
    head_outputs = combined_heads.reshape(row_count, query_heads * HEAD_SIZE).astype(jnp.bfloat16)
    attn_sum = lax.psum(product(head_outputs, w_out), "tensor")
    hidden = inputs + attn_sum
    normed_two, scale_two = normalize(hidden, mlp_gain)
    normed_two = normed_two.astype(jnp.bfloat16)
    gate_proj = product(normed_two, w_gate)
    up_proj = product(normed_two, w_up)
    sigmoid_gate = jax.nn.sigmoid(gate_proj)
    swish_gate = gate_proj * sigmoid_gate
    activation = (swish_gate * up_proj).astype(jnp.bfloat16)
    branch = lax.psum(product(activation, w_down), "tensor")
    mixed = (hidden + branch).astype(jnp.bfloat16)
    grad_w_down = over_rows(activation, cotangent)
    grad_activation = against(cotangent, w_down)
    grad_gate_in = (
        grad_activation * up_proj * sigmoid_gate * (1.0 + gate_proj * (1.0 - sigmoid_gate))
    ).astype(jnp.bfloat16)
    grad_up_in = (grad_activation * swish_gate).astype(jnp.bfloat16)
    grad_w_gate = over_rows(normed_two, grad_gate_in)
    grad_w_up = over_rows(normed_two, grad_up_in)
    grad_normed_two = lax.psum(against(grad_gate_in, w_gate) + against(grad_up_in, w_up), "tensor")
    back_two, grad_mlp_gain = norm_backward(grad_normed_two, hidden, scale_two, mlp_gain)
    grad_hidden = cotangent.astype(jnp.float32) + back_two
    grad_attn = grad_hidden.astype(jnp.bfloat16)
    grad_w_out = over_rows(head_outputs, grad_attn)
    grad_heads = (
        against(grad_attn, w_out)
        .astype(jnp.bfloat16)
        .reshape(seq_count, seq_len, kv_heads, group_size, HEAD_SIZE)
    )
    grad_query_rot, grad_key_rot, grad_value_rot = lax.map(
        attend_backward,
        (query_rotated, key_rotated, value_projected, segments, log_totals, grad_heads),
    )
    grad_query_in = (
        unrotate(
            grad_query_rot.reshape(row_count, query_heads, HEAD_SIZE), cosine_lookup, sine_lookup
        )
        .reshape(row_count, query_heads * HEAD_SIZE)
        .astype(jnp.bfloat16)
    )
    grad_key_in = (
        unrotate(grad_key_rot.reshape(row_count, kv_heads, HEAD_SIZE), cosine_lookup, sine_lookup)
        .reshape(row_count, kv_heads * HEAD_SIZE)
        .astype(jnp.bfloat16)
    )
    grad_value_in = grad_value_rot.reshape(row_count, kv_heads * HEAD_SIZE).astype(jnp.bfloat16)
    grad_w_query = over_rows(normed_one, grad_query_in)
    grad_w_key = over_rows(normed_one, grad_key_in)
    grad_w_value = over_rows(normed_one, grad_value_in)
    grad_normed_one = lax.psum(
        against(grad_query_in, w_query)
        + against(grad_key_in, key_weight)
        + against(grad_value_in, value_weight),
        "tensor",
    )
    back_one, grad_attn_gain = norm_backward(grad_normed_one, inputs, scale_one, attn_gain)
    grad_input = grad_hidden + back_one
    summed = (
        lax.psum_scatter(grad_w_query, "dp", scatter_dimension=0, tiled=True),
        lax.psum_scatter(grad_w_key, "dp", scatter_dimension=0, tiled=True),
        lax.psum_scatter(grad_w_value, "dp", scatter_dimension=0, tiled=True),
        lax.psum_scatter(grad_w_out, "dp", scatter_dimension=1, tiled=True),
        lax.psum_scatter(grad_attn_gain, "dp", scatter_dimension=0, tiled=True),
        lax.psum_scatter(grad_w_gate, "dp", scatter_dimension=0, tiled=True),
        lax.psum_scatter(grad_w_up, "dp", scatter_dimension=0, tiled=True),
        lax.psum_scatter(grad_w_down, "dp", scatter_dimension=1, tiled=True),
        lax.psum_scatter(grad_mlp_gain, "dp", scatter_dimension=0, tiled=True),
    )
    (
        grad_w_query,
        grad_w_key,
        grad_w_value,
        grad_w_out,
        grad_attn_gain,
        grad_w_gate,
        grad_w_up,
        grad_w_down,
        grad_mlp_gain,
    ) = summed
    return (
        mixed,
        grad_input,
        grad_attn_gain,
        grad_w_query,
        grad_w_key,
        grad_w_value,
        grad_w_out,
        grad_mlp_gain,
        grad_w_gate,
        grad_w_up,
        grad_w_down,
    )


def solution(mesh):
    placed = (
        P("dp", None),
        P("dp", None),
        P("dp", None),
        P(),
        P(None, "tensor"),
        P(None, "tensor"),
        P(None, "tensor"),
        P("tensor", None),
        P(),
        P(None, "tensor"),
        P(None, "tensor"),
        P("tensor", None),
        P("dp", None),
    )
    return jax.shard_map(
        body,
        mesh=mesh,
        in_specs=placed,
        out_specs=(
            P("dp", None),
            P("dp", None),
            P("dp"),
            P("dp", "tensor"),
            P("dp", "tensor"),
            P("dp", "tensor"),
            P("tensor", "dp"),
            P("dp"),
            P("dp", "tensor"),
            P("dp", "tensor"),
            P("tensor", "dp"),
        ),
        check_vma=False,
    )
```

profile of v0, /device:TPU:0, one launch (start us, length us, event | category | flops | bytes accessed | tf_op | source)
XLA Modules:
  0.0 1645.2 jit_solution(2407296407307873755)
XLA Ops:
  28.7 87.8 %all-reduce.8.cloned.1.call-done = f32[512,2048]{1,0:T(8,128)} async-done(((f32[512,2048]{1,0:T(8,128)}), f32[512,2048]{1,0:T(8,128)}) %all-reduce.8.cloned.1.call-update) | async-done | bytes 4194320 | tf_op jit(solution)/shard_map/psum | solution.py:167
  120.4 11.9 fusion.51
  132.3 6.1 fusion.52
  138.5 11.7 multiply_convert_fusion
  150.2 8.5 fusion.54
  158.7 9.5 convolution_add_fusion
  168.5 10.5 fusion.53
  179.0 75.0 %all-reduce.10.cloned.1.call-done = f32[512,2048]{1,0:T(8,128)} async-done(((f32[512,2048]{1,0:T(8,128)}), f32[512,2048]{1,0:T(8,128)}) %all-reduce.10.cloned.1.call-update) | async-done | bytes 4194320 | tf_op jit(solution)/shard_map/psum | solution.py:186
  270.9 13.4 fusion.19
  284.4 14.2 broadcast_multiply_fusion
  315.9 5.4 fusion.26
  323.0 9.8 fusion.61
  332.8 10.0 fusion.62
  344.5 9.8 fusion.63
  356.2 104.4 %all-reduce.12.cloned.1.call-done = (f32[512,2048]{1,0:T(8,128)}, f32[512,2048]{1,0:T(8,128)}) async-done(((f32[512,2048]{1,0:T(8,128)}, f32[512,2048]{1,0:T(8,128)}), (f32[512,2048]{1,0:T(8,128)}, f32[512,2048]{1,0:T(8,128)})) %all-reduce.12.cloned.1.call-update) | async-done | bytes 8388624 | tf_op jit(solution)/shard_map/psum | solution.py:176
  464.0 37.3 %all-reduce.2 = (f32[2048]{0:T(1024)S(1)}, f32[2048]{0:T(1024)S(1)}) all-reduce(f32[2048]{0:T(1024)S(1)} %get-tuple-element.54, f32[2048]{0:T(1024)S(1)} %get-tuple-element.52), channel_id=2, replica_groups=mesh['dp'=8,'tensor'=4] {'dp'}, use_global_device_ids=true, to_apply=%region_12.13.clone | all-reduce | flops 4096 | bytes 32768
  502.7 5.6 add_convert_fusion
  513.0 14.9 reduce-scatter.12.cloned.1.call-done
  527.9 66.8 %reduce-scatter.10.cloned.1.call-done = f32[256,128]{1,0:T(8,128)} async-done(((f32[2048,128]{1,0:T(8,128)}), f32[256,128]{1,0:T(8,128)}) %reduce-scatter.10.cloned.1.call-update) | async-done | bytes 131088 | tf_op jit(solution)/shard_map/reduce_scatter | solution.py:226
  594.7 91.0 %reduce-scatter.8.cloned.1.call-done = f32[256,512]{1,0:T(8,128)} async-done(((f32[2048,512]{1,0:T(8,128)}), f32[256,512]{1,0:T(8,128)}) %reduce-scatter.8.cloned.1.call-update) | async-done | bytes 524304 | tf_op jit(solution)/shard_map/reduce_scatter | solution.py:225
  685.7 92.8 %reduce-scatter.14.cloned.1.call-done = f32[512,256]{1,0:T(8,128)} async-done(((f32[512,2048]{1,0:T(8,128)}), f32[512,256]{1,0:T(8,128)}) %reduce-scatter.14.cloned.1.call-update) | async-done | bytes 524304 | tf_op jit(solution)/shard_map/reduce_scatter | solution.py:228
  778.4 286.8 %reduce-scatter.16.cloned.1.call-done = f32[256,2048]{1,0:T(8,128)} async-done(((f32[2048,2048]{1,0:T(8,128)}), f32[256,2048]{1,0:T(8,128)}) %reduce-scatter.16.cloned.1.call-update) | async-done | bytes 2097168 | tf_op jit(solution)/shard_map/reduce_scatter | solution.py:230
  1065.3 286.7 %reduce-scatter.18.cloned.1.call-done = f32[256,2048]{1,0:T(8,128)} async-done(((f32[2048,2048]{1,0:T(8,128)}), f32[256,2048]{1,0:T(8,128)}) %reduce-scatter.18.cloned.1.call-update) | async-done | bytes 2097168 | tf_op jit(solution)/shard_map/reduce_scatter | solution.py:231
  1351.9 286.0 %reduce-scatter.20.cloned.1.call-done = f32[2048,256]{1,0:T(8,128)} async-done(((f32[2048,2048]{1,0:T(8,128)}), f32[2048,256]{1,0:T(8,128)}) %reduce-scatter.20.cloned.1.call-update) | async-done | bytes 2097168 | tf_op jit(solution)/shard_map/reduce_scatter | solution.py:232
  (155 shorter events, 73.4 us)
Async XLA Ops:
  7.2 17.6 %copy-start = (bf16[512,2048]{1,0:T(8,128)(2,1)S(1)}, bf16[512,2048]{1,0:T(8,128)(2,1)}, u32[]{:S(2)}) copy-start(bf16[512,2048]{1,0:T(8,128)(2,1)} %param.20) | copy-start | bytes 6291460
  7.2 109.3 %all-reduce.8.cloned.1.call-start = ((), (), s32[]{:S(2)}) async-start(), calls=%async_computation.7 | async-start | bytes 8388608 | tf_op jit(solution)/shard_map/psum | solution.py:167
  28.1 91.8 %copy-start.27 = (f32[2048]{0:T(1024)S(1)}, f32[2048]{0:T(1024)}, u32[]{:S(2)}) copy-start(f32[2048]{0:T(1024)} %param.21) | copy-start | bytes 24580
  28.1 225.9 %all-reduce.10.cloned.1.call-start = ((), (), s32[]{:S(2)}) async-start(), calls=%async_computation.8 | async-start | bytes 8388608 | tf_op jit(solution)/shard_map/psum | solution.py:186
  119.9 12.3 copy-start.4
  120.0 12.3 slice-start.2
  120.4 11.9 copy-start.12
  168.3 292.3 %all-reduce.12.cloned.1.call-start = ((), (), s32[]{:S(2)}) async-start(), calls=%async_computation.16 | async-start | bytes 16777216 | tf_op jit(solution)/shard_map/psum | solution.py:176
  270.9 13.4 copy-start.19
  270.9 13.4 copy-start.25
  284.3 15.2 copy-start.24
  284.4 16.2 copy-start.15
  307.0 220.9 %reduce-scatter.12.cloned.1.call-start = ((), (), s32[]{:S(2)}) async-start(), calls=%async_computation.11 | async-start | bytes 1179648 | tf_op jit(solution)/shard_map/reduce_scatter | solution.py:227
  310.4 284.3 %reduce-scatter.10.cloned.1.call-start = ((), (), s32[]{:S(2)}) async-start(), calls=%async_computation.10 | async-start | bytes 1179648 | tf_op jit(solution)/shard_map/reduce_scatter | solution.py:226
  312.2 373.4 %reduce-scatter.8.cloned.1.call-start = ((), (), s32[]{:S(2)}) async-start(), calls=%async_computation.9 | async-start | bytes 4718592 | tf_op jit(solution)/shard_map/reduce_scatter | solution.py:225
  315.6 462.9 %reduce-scatter.14.cloned.1.call-start = ((), (), s32[]{:S(2)}) async-start(), calls=%async_computation.12 | async-start | bytes 4718592 | tf_op jit(solution)/shard_map/reduce_scatter | solution.py:228
  321.3 743.9 %reduce-scatter.16.cloned.1.call-start = ((), (), s32[]{:S(2)}) async-start(), calls=%async_computation.13 | async-start | bytes 18874368 | tf_op jit(solution)/shard_map/reduce_scatter | solution.py:230
  332.8 1019.2 %reduce-scatter.18.cloned.1.call-start = ((), (), s32[]{:S(2)}) async-start(), calls=%async_computation.14 | async-start | bytes 18874368 | tf_op jit(solution)/shard_map/reduce_scatter | solution.py:231
  342.9 1295.0 %reduce-scatter.20.cloned.1.call-start = ((), (), s32[]{:S(2)}) async-start(), calls=%async_computation.15 | async-start | bytes 18874368 | tf_op jit(solution)/shard_map/reduce_scatter | solution.py:232
  354.3 106.3 %copy-start.6 = (bf16[512,2048]{1,0:T(8,128)(2,1)S(1)}, bf16[512,2048]{1,0:T(8,128)(2,1)}, u32[]{:S(2)}) copy-start(bf16[512,2048]{1,0:T(8,128)(2,1)} %param.13) | copy-start | bytes 6291460
  354.3 106.3 %copy-start.26 = (f32[2048]{0:T(1024)S(1)}, f32[2048]{0:T(1024)}, u32[]{:S(2)}) copy-start(f32[2048]{0:T(1024)} %param.16) | copy-start | bytes 24580
  354.3 106.3 %copy-start.29 = (f32[512]{0:T(512)S(1)}, f32[512]{0:T(512)}, u32[]{:S(2)}) copy-start(f32[512]{0:T(512)} %copy-done.28) | copy-start | bytes 6148
  460.6 47.7 %copy-start.34 = (f32[512]{0:T(512)S(1)}, f32[512]{0:T(512)}, u32[]{:S(2)}) copy-start(f32[512]{0:T(512)} %get-tuple-element.89) | copy-start | bytes 6148
  508.3 1129.6 %copy-start.1 = (bf16[512,2048]{1,0:T(8,128)(2,1)S(1)}, bf16[512,2048]{1,0:T(8,128)(2,1)}, u32[]{:S(2)}) copy-start(bf16[512,2048]{1,0:T(8,128)(2,1)} %param.20) | copy-start | bytes 6291460
  (29 other events, 114.1 us)
Sparse Core Ops, SparseCore 0:
  28.2 88.1 all-reduce.7
  168.4 85.6 all-reduce.9
  307.2 153.3 all-reduce.11
  464.4 63.4 reduce-scatter.11
  532.1 62.4 reduce-scatter.9
  598.7 86.8 reduce-scatter.7
  690.3 88.0 reduce-scatter.13
  782.8 282.4 reduce-scatter.15
  1070.1 281.7 reduce-scatter.17
  1356.1 281.7 reduce-scatter.19
where the time goes:
time: 1650 us
  waiting for transfers between devices  1390 us (84%)
  matrix products  150 us (9%)
  blocking collectives  37.3 us (2%)
  other arithmetic  36 us (2%)
    reduce_scatter x1, waiting for transfers between devices, body(): lax.psum_scatter(grad_w_gate, 'dp', scatter_dimension=0, tiled=True)  287 us
    reduce_scatter x1, waiting for transfers between devices, body(): lax.psum_scatter(grad_w_up, 'dp', scatter_dimension=0, tiled=True)  287 us
    reduce_scatter x1, waiting for transfers between devices, body(): lax.psum_scatter(grad_w_down, 'dp', scatter_dimension=1, tiled=True)  286 us
    psum x1, waiting for transfers between devices, body(): branch = lax.psum(product(activation, w_down), 'tensor')  104 us
    reduce_scatter x1, waiting for transfers between devices, body(): lax.psum_scatter(grad_w_out, 'dp', scatter_dimension=1, tiled=True)  92.8 us
    reduce_scatter x1, waiting for transfers between devices, body(): lax.psum_scatter(grad_w_query, 'dp', scatter_dimension=0, tiled=True)  91 us
    psum x1, waiting for transfers between devices, body(): attn_sum = lax.psum(product(head_outputs, w_out), 'tensor')  87.8 us
    psum x1, waiting for transfers between devices, body(): lax.psum(against(grad_gate_in, w_gate) + against(grad_up_in, w_up), 'tens...  75 us
  transfers between devices with their start and end apart: 10, of which 10 were waited for; matrix products, arithmetic and copies ran while one was open for 4% of the time, Pallas kernels for 0%

commit v1 on v0

v1 whole, which is shorter than its diff:
```python
import jax
import jax.numpy as jnp
from jax import lax
from jax.sharding import PartitionSpec as P

HEAD_SIZE = 64
EPSILON = 1e-05
MASKED = -1e30
F32 = jnp.float32
BF16 = jnp.bfloat16


def product(left_matrix, right_matrix):
    return jnp.dot(left_matrix, right_matrix, preferred_element_type=F32)


def over_rows(left_matrix, right_matrix):
    return lax.dot_general(
        left_matrix, right_matrix, (((0,), (0,)), ((), ())), preferred_element_type=F32
    )


def against(gradient, weight):
    return lax.dot_general(
        gradient, weight, (((1,), (1,)), ((), ())), preferred_element_type=F32
    )


def narrowed(value):
    return jnp.where(value == value, value, 0.0).astype(BF16)


def swap(value, axis, bit):
    size = lax.axis_size(axis)
    return lax.ppermute(value, axis, [(i, i ^ bit) for i in range(size)])


def half_of(value, which, dim=0):
    size = value.shape[dim] // 2
    return lax.dynamic_slice_in_dim(value, which * size, size, dim)


def joined(mine, other, which):
    first = jnp.where(which == 0, mine, other)
    second = jnp.where(which == 0, other, mine)
    return jnp.concatenate([first, second], axis=0)


def tensor_sum_half(partial, core):
    total = half_of(partial, core) + swap(half_of(partial, 1 - core), "tensor", 1)
    bit = 2
    while bit < lax.axis_size("tensor"):
        total = total + swap(total, "tensor", bit)
        bit *= 2
    return total


def tables(places):
    half_dim = HEAD_SIZE // 2
    frequency = 500000.0 ** (-(jnp.arange(half_dim).astype(F32) * 2.0 / HEAD_SIZE))
    angles = places.astype(F32)[..., None] * frequency
    cosine_lookup = jnp.cos(angles)
    sine_lookup = jnp.sin(angles)
    return (
        jnp.concatenate([cosine_lookup, cosine_lookup], -1),
        jnp.concatenate([sine_lookup, sine_lookup], -1),
    )


def apply_rotary(field, cosine_lookup, sine_lookup):
    half_dim = HEAD_SIZE // 2
    turned = jnp.concatenate([-field[..., half_dim:], field[..., :half_dim]], -1)
    return field * cosine_lookup + turned * sine_lookup


def unrotate(gradient, cosine_lookup, sine_lookup):
    half_dim = HEAD_SIZE // 2
    sined = gradient * sine_lookup
    return gradient * cosine_lookup + jnp.concatenate(
        [sined[..., half_dim:], -sined[..., :half_dim]], -1
    )


def allowed_pairs(segment):
    spots = jnp.arange(segment.shape[0])
    return (spots[:, None] >= spots[None, :]) & (segment[:, None] == segment[None, :])


def scores(query_rotated, key_rotated, segment):
    raw_scores = jnp.einsum(
        "qhgd,khd->hgqk", query_rotated, key_rotated, preferred_element_type=F32
    ) * HEAD_SIZE ** (-0.5)
    return jnp.where(allowed_pairs(segment), raw_scores, MASKED)


def attend_forward(query_rotated, key_rotated, value_seq, segment):
    masked = scores(query_rotated, key_rotated, segment)
    row_peak = jnp.max(masked, axis=-1, keepdims=True)
    log_total = row_peak + jnp.log(jnp.sum(jnp.exp(masked - row_peak), axis=-1, keepdims=True))
    attention_probs = jnp.exp(masked - log_total).astype(BF16)
    combined_heads = jnp.einsum(
        "ojus,sov->uojv", attention_probs, value_seq, preferred_element_type=F32
    )
    return (combined_heads, log_total)


def attend_backward(query_rotated, key_rotated, value_seq, segment, log_total, grad_heads):
    masked = scores(query_rotated, key_rotated, segment)
    attention_probs = jnp.exp(masked - log_total)
    grad_probs = jnp.einsum("qhgd,khd->hgqk", grad_heads, value_seq, preferred_element_type=F32)
    row_sum = jnp.sum(attention_probs * grad_probs, axis=-1, keepdims=True)
    grad_raw = jnp.where(
        allowed_pairs(segment), attention_probs * (grad_probs - row_sum), 0.0
    ).astype(BF16)
    factor = HEAD_SIZE ** (-0.5)
    grad_query_rot = (
        jnp.einsum("ojus,sov->uojv", grad_raw, key_rotated, preferred_element_type=F32) * factor
    )
    grad_key_rot = (
        jnp.einsum("hgqk,qhgd->khd", grad_raw, query_rotated, preferred_element_type=F32) * factor
    )
    grad_value_rot = jnp.einsum(
        "hgqk,qhgd->khd", attention_probs.astype(BF16), grad_heads, preferred_element_type=F32
    )
    return (grad_query_rot, grad_key_rot, grad_value_rot)


def per_sequence(step, *fields):
    results = [step(*[field[s] for field in fields]) for s in range(fields[0].shape[0])]
    return [jnp.stack(parts) for parts in zip(*results)]


def body(
    tokens,
    segments,
    positions,
    attn_gain,
    w_query,
    key_weight,
    value_weight,
    w_out,
    mlp_gain,
    w_gate,
    w_up,
    w_down,
    cotangent,
):
    groups = lax.axis_size("dp")
    place = lax.axis_index("dp")
    core = lax.axis_index("tensor") % 2
    all_bits = [1 << i for i in range(groups.bit_length() - 1)]
    shared_bits = [bit for bit in (4, 1) if bit < groups]
    split_bits = [bit for bit in all_bits if bit not in shared_bits]

    def gathered(half):
        parts = [half]
        for bit in shared_bits:
            parts = parts + [swap(part, "dp", bit) for part in parts]
        others = parts[1:]
        twins = [swap(part, "tensor", 1) for part in others]
        return jnp.concatenate([narrowed(part) for part in others + twins], axis=0)

    def blocks(matrix, offsets):
        width = matrix.shape[1] // groups
        return [
            lax.dynamic_slice_in_dim(matrix, (place ^ offset) * width, width, 1)
            for offset in offsets
        ]

    def offsets_of(bits):
        found = [0]
        for bit in bits:
            found = found + [offset + bit for offset in found]
        return found

    def reduced(matrix_of, bits):
        sent = None
        for bit in bits:
            rest = bits[bits.index(bit) + 1 :]
            offsets = offsets_of(rest)
            if sent is None:
                away = matrix_of([offset ^ bit for offset in offsets])
                home = matrix_of(offsets)
            else:
                away = [sent[offset ^ bit] for offset in offsets]
                home = [sent[offset] for offset in offsets]
            came = swap(away, "dp", bit)
            sent = {offset: h + c for offset, h, c in zip(offsets, home, came)}
        return sent[0]

    inputs = tokens.astype(F32)
    row_count, width = inputs.shape
    seq_count, seq_len = segments.shape
    query_heads = w_query.shape[1] // HEAD_SIZE
    kv_heads = key_weight.shape[1] // HEAD_SIZE
    group_size = query_heads // kv_heads
    query_width, kv_width = w_query.shape[1], key_weight.shape[1]

    cotangent_half = half_of(cotangent, core).astype(F32)
    cotangent_others = gathered(cotangent_half)

    scale_one = lax.rsqrt(jnp.mean(inputs * inputs, axis=-1, keepdims=True) + EPSILON)
    normed_one = (inputs * scale_one * attn_gain).astype(BF16)
    cosine_lookup, sine_lookup = tables(positions.reshape(row_count))
    cosine_lookup = cosine_lookup[:, None, :]
    sine_lookup = sine_lookup[:, None, :]
    query_projected = product(normed_one, w_query).reshape(row_count, query_heads, HEAD_SIZE)
    key_projected = product(normed_one, key_weight).reshape(row_count, kv_heads, HEAD_SIZE)
    query_rotated = (
        apply_rotary(query_projected, cosine_lookup, sine_lookup)
        .astype(BF16)
        .reshape(seq_count, seq_len, kv_heads, group_size, HEAD_SIZE)
    )
    key_rotated = (
        apply_rotary(key_projected, cosine_lookup, sine_lookup)
        .astype(BF16)
        .reshape(seq_count, seq_len, kv_heads, HEAD_SIZE)
    )
    value_projected = (
        product(normed_one, value_weight)
        .astype(BF16)
        .reshape(seq_count, seq_len, kv_heads, HEAD_SIZE)
    )
    combined_heads, log_totals = per_sequence(
        attend_forward, query_rotated, key_rotated, value_projected, segments
    )
    head_outputs = combined_heads.reshape(row_count, query_width).astype(BF16)

    inputs_half = half_of(inputs, core)
    hidden = inputs_half + tensor_sum_half(product(head_outputs, w_out), core)
    scale_two = lax.rsqrt(jnp.mean(hidden * hidden, axis=-1, keepdims=True) + EPSILON)
    normed_half = (hidden * scale_two * mlp_gain).astype(BF16)
    normed_sent = normed_half.astype(F32)
    normed_twin = narrowed(swap(normed_sent, "tensor", 1))
    normed_two = joined(normed_half, normed_twin, core)
    normed_others = gathered(normed_sent)

    def feed_forward(normed, incoming):
        gate_proj = product(normed, w_gate)
        up_proj = product(normed, w_up)
        grad_activation = against(incoming, w_down)
        sigmoid_gate = jax.nn.sigmoid(gate_proj)
        swish_gate = gate_proj * sigmoid_gate
        activation = (swish_gate * up_proj).astype(BF16)
        grad_gate_in = (
            grad_activation * up_proj * sigmoid_gate * (1.0 + gate_proj * (1.0 - sigmoid_gate))
        ).astype(BF16)
        grad_up_in = (grad_activation * swish_gate).astype(BF16)
        return activation, grad_gate_in, grad_up_in

    activation, grad_gate_in, grad_up_in = feed_forward(normed_two, cotangent)
    grad_normed_two = tensor_sum_half(
        against(grad_gate_in, w_gate) + against(grad_up_in, w_up), core
    )
    mixed_half = hidden + tensor_sum_half(product(activation, w_down), core)
    mixed = joined(mixed_half.astype(BF16), narrowed(swap(mixed_half, "tensor", 1)), core)

    weighted = grad_normed_two * mlp_gain
    inner_mean = jnp.mean(weighted * hidden, axis=-1, keepdims=True)
    back_two = scale_two * weighted - hidden * (scale_two * scale_two * scale_two) * inner_mean
    gain_two_half = jnp.sum(grad_normed_two * hidden * scale_two, axis=0)
    grad_hidden = cotangent_half + back_two
    attn_half = grad_hidden.astype(BF16)
    attn_twin = narrowed(swap(grad_hidden, "tensor", 1))
    grad_attn = joined(attn_half, attn_twin, core)

    grad_heads = (
        against(grad_attn, w_out)
        .astype(BF16)
        .reshape(seq_count, seq_len, kv_heads, group_size, HEAD_SIZE)
    )
    grad_query_rot, grad_key_rot, grad_value_rot = per_sequence(
        attend_backward,
        query_rotated,
        key_rotated,
        value_projected,
        segments,
        log_totals,
        grad_heads,
    )
    grad_query_in = (
        unrotate(
            grad_query_rot.reshape(row_count, query_heads, HEAD_SIZE), cosine_lookup, sine_lookup
        )
        .reshape(row_count, query_width)
        .astype(BF16)
    )
    grad_key_in = (
        unrotate(grad_key_rot.reshape(row_count, kv_heads, HEAD_SIZE), cosine_lookup, sine_lookup)
        .reshape(row_count, kv_width)
        .astype(BF16)
    )
    grad_value_in = grad_value_rot.reshape(row_count, kv_width).astype(BF16)
    partial_one = (
        against(grad_query_in, w_query)
        + against(grad_key_in, key_weight)
        + against(grad_value_in, value_weight)
    )
    grad_normed_one = tensor_sum_half(partial_one, core)
    scale_one = half_of(scale_one, core)
    weighted = grad_normed_one * attn_gain
    inner_mean = jnp.mean(weighted * inputs_half, axis=-1, keepdims=True)
    back_one = scale_one * weighted - inputs_half * (scale_one * scale_one * scale_one) * inner_mean
    gain_one_half = jnp.sum(grad_normed_one * inputs_half * scale_one, axis=0)
    input_half = grad_hidden + back_one
    grad_input = joined(input_half, swap(input_half, "tensor", 1), core)

    activation_o, grad_gate_o, grad_up_o = feed_forward(normed_others, cotangent_others)

    def rows_of(left, left_others, right, right_others):
        def term(offsets):
            ours = blocks(left, offsets)
            theirs = blocks(left_others, offsets)
            return [
                over_rows(a, right) + over_rows(b, right_others) for a, b in zip(ours, theirs)
            ]

        return reduced(term, split_bits)

    def columns_of(left, left_others, right, right_others):
        def term(offsets):
            ours = blocks(right, offsets)
            theirs = blocks(right_others, offsets)
            return [
                over_rows(left, a) + over_rows(left_others, b) for a, b in zip(ours, theirs)
            ]

        return reduced(term, split_bits)

    grad_w_down = columns_of(activation, activation_o, cotangent, cotangent_others)
    grad_w_gate = rows_of(normed_two, normed_others, grad_gate_in, grad_gate_o)
    grad_w_up = rows_of(normed_two, normed_others, grad_up_in, grad_up_o)

    grad_w_out = reduced(
        lambda offsets: [over_rows(head_outputs, b) for b in blocks(grad_attn, offsets)], all_bits
    )
    projected = jnp.concatenate([grad_query_in, grad_key_in, grad_value_in], axis=1)
    grad_w_proj = reduced(
        lambda offsets: [over_rows(b, projected) for b in blocks(normed_one, offsets)], all_bits
    )
    grad_w_query = grad_w_proj[:, :query_width]
    grad_w_key = grad_w_proj[:, query_width : query_width + kv_width]
    grad_w_value = grad_w_proj[:, query_width + kv_width :]

    gains = jnp.stack([gain_one_half, gain_two_half])
    gains = gains + swap(gains, "tensor", 1)
    gains = reduced(lambda offsets: blocks(gains, offsets), all_bits)
    grad_attn_gain, grad_mlp_gain = gains[0], gains[1]
    return (
        mixed,
        grad_input,
        grad_attn_gain,
        grad_w_query,
        grad_w_key,
        grad_w_value,
        grad_w_out,
        grad_mlp_gain,
        grad_w_gate,
        grad_w_up,
        grad_w_down,
    )


def solution(mesh):
    placed = (
        P("dp", None),
        P("dp", None),
        P("dp", None),
        P(),
        P(None, "tensor"),
        P(None, "tensor"),
        P(None, "tensor"),
        P("tensor", None),
        P(),
        P(None, "tensor"),
        P(None, "tensor"),
        P("tensor", None),
        P("dp", None),
    )
    return jax.shard_map(
        body,
        mesh=mesh,
        in_specs=placed,
        out_specs=(
            P("dp", None),
            P("dp", None),
            P("dp"),
            P("dp", "tensor"),
            P("dp", "tensor"),
            P("dp", "tensor"),
            P("tensor", "dp"),
            P("dp"),
            P("dp", "tensor"),
            P("dp", "tensor"),
            P("tensor", "dp"),
        ),
        check_vma=False,
    )
```

time: 1650 us -> 705 us (0.43)
  waiting for transfers between devices: 1390 us -> 337 us
  matrix products: 150 us -> 224 us
  starting transfers between devices: 1.3 us -> 47.7 us
  blocking collectives: 37.3 us -> 0 us
  other arithmetic: 36 us -> 69.4 us
    reduce_scatter x7 -> x0, waiting for transfers between devices: 1120 us -> none  [the longest x1 287 us: body(): lax.psum_scatter(grad_w_gate, 'dp', scatter_dimension=0, tiled=True)]
    ppermute x0 -> x49, waiting for transfers between devices: none -> 337 us  [swap(): return lax.ppermute(value, axis, [(i, i ^ bit) for i in range(size)])]
    psum x3 -> x0, waiting for transfers between devices: 267 us -> none  [the longest x1 104 us: body(): branch = lax.psum(product(activation, w_down), 'tensor')]
    ppermute x0 -> x49, starting transfers between devices: none -> 47.7 us  [swap(): return lax.ppermute(value, axis, [(i, i ^ bit) for i in range(size)])]
    dot_general x8 -> x10, matrix products: 36.8 us -> 81.2 us  [the longest x9 78.3 us: product(): return jnp.dot(left_matrix, right_matrix, preferred_element_type=F32)]
    unnamed x1 -> x0, blocking collectives: 37.3 us -> none
    unnamed x2 -> x16, other arithmetic: 0.01 us -> 20.4 us
    dot_general x7 -> x8, matrix products: 35.8 us -> 53.5 us  [against(): lax.dot_general(gradient, weight, (((1,), (1,)), ((), ())), preferred_ele...]
  transfers between devices with their start and end apart: 10 -> 49, of which waited for: 10 -> 18; matrix products, arithmetic and copies ran while one was open for 4% -> 39% of each run, Pallas kernels for 0% -> 0%
where the time goes in v1:
time: 705 us; the launch traced here: 695 us
  waiting for transfers between devices  337 us (48%)
  matrix products  224 us (32%)
  other arithmetic  69.4 us (10%)
  starting transfers between devices  47.7 us (7%)
  local copies, waits for them, and re-layouts  15.7 us (2%)
    ppermute x49, waiting for transfers between devices, swap(): return lax.ppermute(value, axis, [(i, i ^ bit) for i in range(size)])  337 us
    dot_general x9, matrix products, product(): return jnp.dot(left_matrix, right_matrix, preferred_element_type=F32)  78.3 us
    dot_general x8, matrix products, against(): lax.dot_general(gradient, weight, (((1,), (1,)), ((), ())), preferred_ele...  53.5 us
    dot_general x28, matrix products, over_rows(): lax.dot_general(left_matrix, right_matrix, (((0,), (0,)), ((), ())), pref...  51.9 us
    ppermute x49, starting transfers between devices, swap(): return lax.ppermute(value, axis, [(i, i ^ bit) for i in range(size)])  47.7 us
    unnamed x16, other arithmetic  20.4 us
    dot_general x1, matrix products, attend_backward(): jnp.einsum('ojus,sov->uojv', grad_raw, key_rotated, preferred_element_typ...  14.4 us
    dot_general x1, matrix products, attend_backward(): jnp.einsum('hgqk,qhgd->khd', grad_raw, query_rotated, preferred_element_t...  14.4 us
  transfers between devices with their start and end apart: 49, of which 18 were waited for; matrix products, arithmetic and copies ran while one was open for 39% of the time, Pallas kernels for 0%

profile of v1, /device:TPU:0, one launch (start us, length us, event | category | flops | bytes accessed | tf_op | source)
XLA Modules:
  0.0 695.4 jit_solution(17901569504107320562)
XLA Ops:
  47.0 10.6 %fusion.179 = f32[512,2048]{1,0:T(8,128)} fusion(bf16[512,2048]{1,0:T(8,128)(2,1)} %param.25, bf16[2048,2048]{1,0:T(8,128)(2,1)} %param.24), kind=kOutput, calls=%fused_computation.297 | convolution fusion | flops 4294967296 | bytes 14680064 | tf_op jit(solution)/shard_map/dot_general | solution.py:24
  57.7 68.8 %collective-permute-done.40 = f32[256,2048]{1,0:T(8,128)} collective-permute-done((f32[256,2048]{1,0:T(8,128)}, f32[256,2048]{1,0:T(8,128)}, u32[]{:S(2)}, u32[]{:S(2)}) %collective-permute-start.40) | collective-permute-done | bytes 2097184 | tf_op jit(solution)/shard_map/ppermute | solution.py:35
  138.7 35.4 %collective-permute-done.42 = f32[256,2048]{1,0:T(8,128)S(1)} collective-permute-done((f32[256,2048]{1,0:T(8,128)}, f32[256,2048]{1,0:T(8,128)S(1)}, u32[]{:S(2)}, u32[]{:S(2)}) %collective-permute-start.42) | collective-permute-done | bytes 2097184 | tf_op jit(solution)/shard_map/ppermute | solution.py:35
  185.9 11.2 %multiply_convert_fusion.3 = (bf16[512,2048]{1,0:T(8,128)(2,1)S(1)}, bf16[512,2048]{1,0:T(8,128)(2,1)S(1)}, bf16[512,2048]{1,0:T(8,128)(2,1)S(1)}) fusion(f32[512,2048]{1,0:T(8,128)S(1)} %copy-done.50, f32[512,2048]{1,0:T(8,128)} %fusion.30, bf16[2048,2048]{1,0:T(8,128)(2,1)} %param.22, bf16[256,2048]{1,0:T(8,128)(2,1)S(1)} %get-tuple-element.32, ...), kind=kOutput, calls=%fused_computation.50 | convolution fusion | flops 4314890240 | bytes 25165824 | tf_op jit(solution)/shard_map/dot_general | solution.py:14
  197.1 9.5 %fusion.180 = f32[512,2048]{1,0:T(8,128)} fusion(bf16[512,2048]{1,0:T(8,128)(2,1)S(1)} %get-tuple-element.23, bf16[2048,2048]{1,0:T(8,128)(2,1)} %param.22), kind=kOutput, calls=%fused_computation.298 | convolution fusion | flops 4294967296 | bytes 14680064 | tf_op jit(solution)/shard_map/dot_general | solution.py:24
  206.6 8.8 %convolution_add_fusion = f32[512,2048]{1,0:T(8,128)S(1)} fusion(f32[512,2048]{1,0:T(8,128)} %fusion.180, bf16[512,2048]{1,0:T(8,128)(2,1)S(1)} %get-tuple-element.22, bf16[2048,2048]{1,0:T(8,128)(2,1)} %param.23), kind=kOutput, calls=%fused_computation.57 | convolution fusion | flops 4296015872 | bytes 18874368 | tf_op jit(solution)/shard_map/dot_general | solution.py:24
  217.9 6.9 fusion.178
  227.5 19.2 %fusion.184 = f32[1536,2048]{1,0:T(8,128)} fusion(bf16[1536,2048]{1,0:T(8,128)(2,1)} %fusion.42, bf16[2048,2048]{1,0:T(8,128)(2,1)} %param.24), kind=kOutput, calls=%fused_computation.302 | convolution fusion | flops 12884901888 | bytes 27262976 | tf_op jit(solution)/shard_map/dot_general | solution.py:24
  267.6 36.5 %collective-permute-done.36 = f32[256,2048]{1,0:T(8,128)} collective-permute-done((f32[256,2048]{1,0:T(8,128)}, f32[256,2048]{1,0:T(8,128)}, u32[]{:S(2)}, u32[]{:S(2)}) %collective-permute-start.36) | collective-permute-done | bytes 2097184 | tf_op jit(solution)/shard_map/ppermute | solution.py:35
  314.4 43.6 %collective-permute-done.4 = f32[256,2048]{1,0:T(8,128)S(1)} collective-permute-done((f32[256,2048]{1,0:T(8,128)S(1)}, f32[256,2048]{1,0:T(8,128)S(1)}, u32[]{:S(2)}, u32[]{:S(2)}) %collective-permute-start.4) | collective-permute-done | bytes 2097184 | tf_op jit(solution)/shard_map/ppermute | solution.py:35
  362.1 19.2 %fusion.185 = f32[1536,2048]{1,0:T(8,128)} fusion(bf16[1536,2048]{1,0:T(8,128)(2,1)} %fusion.48, bf16[2048,2048]{1,0:T(8,128)(2,1)} %param.22), kind=kOutput, calls=%fused_computation.303 | convolution fusion | flops 12884901888 | bytes 27262976 | tf_op jit(solution)/shard_map/dot_general | solution.py:14
  381.2 28.6 %multiply_convert_fusion = (bf16[1536,2048]{1,0:T(8,128)(2,1)}, bf16[1536,2048]{1,0:T(8,128)(2,1)}, bf16[1536,2048]{1,0:T(8,128)(2,1)}) fusion(f32[1536,2048]{1,0:T(8,128)} %fusion.185, f32[1536,2048]{1,0:T(8,128)} %fusion.184, bf16[1536,2048]{1,0:T(8,128)(2,1)} %fusion.48, bf16[2048,2048]{1,0:T(8,128)(2,1)} %param.23), kind=kOutput, calls=%fused_computation.1 | convolution fusion | flops 12932087808 | bytes 58720256 | tf_op jit(solution)/shard_map/dot_general | solution.py:14
  409.9 6.9 convolution_add_fusion.5
  439.7 14.4 %fusion.32 = f32[2,64,4,512]{3,1,2,0:T(8,128)} fusion(bf16[512,2,64,1]{0,2,3,1:T(8,128)(2,1)} %copy-done.36, f32[2,512,512,4]{2,1,3,0:T(8,128)} %fusion.181, f32[2,512,512,4]{2,1,3,0:T(8,128)} %copy-done.5, f32[2,4,512]{2,1,0:T(4,128)} %bitcast.238, pred[512,512]{0,1:T(8,128)(4,1)S(1)} %copy-done.19), kind=kOutput, calls=%fused_computation.108 | convolution fusion | flops 291770880 | bytes 18235392 | tf_op jit(solution)/shard_map/ojus,sov->uojv/dot_general | solution.py:117
  457.7 14.4 %broadcast_multiply_fusion = (f32[512,2,64]{0,2,1:T(8,128)}, f32[512,2,64]{0,2,1:T(8,128)}) fusion(f32[512,64]{0,1:T(8,128)} %get-tuple-element.47, bf16[512,2,4,64]{0,3,2,1:T(8,128)(2,1)} %copy-done.30, f32[2,512,512,4]{2,1,3,0:T(8,128)} %fusion.181, f32[2,512,512,4]{2,1,3,0:T(8,128)} %copy-done.5, f32[2,4,512]{2,1,0:T(4,128)} %bitcast.239, ...), kind=kOutput, calls=%fused_computation.209 | convolution fusion | flops 291574272 | bytes 18235392 | tf_op jit(solution)/shard_map/hgqk,qhgd->khd/dot_general | solution.py:120
  493.4 17.2 %collective-permute-done.47 = f32[256,2048]{1,0:T(8,128)} collective-permute-done((f32[256,2048]{1,0:T(8,128)}, f32[256,2048]{1,0:T(8,128)}, u32[]{:S(2)}, u32[]{:S(2)}) %collective-permute-start.47) | collective-permute-done | bytes 2097184 | tf_op jit(solution)/shard_map/ppermute | solution.py:35
  516.9 37.6 %collective-permute-done.48 = f32[2048,256]{1,0:T(8,128)} collective-permute-done((f32[2048,256]{1,0:T(8,128)}, f32[2048,256]{1,0:T(8,128)}, u32[]{:S(2)}, u32[]{:S(2)}) %collective-permute-start.48) | collective-permute-done | bytes 2097184 | tf_op jit(solution)/shard_map/ppermute | solution.py:35
  554.5 7.1 %fusion.8 = f32[2048,256]{1,0:T(8,128)} fusion(f32[2048,256]{1,0:T(8,128)} %collective-permute-done.48, f32[2048,256]{1,0:T(8,128)S(1)} %copy-done.16, bf16[1536,2048]{1,0:T(8,128)(2,1)} %get-tuple-element.19, bf16[1536,2048]{1,0:T(8,128)(2,1)} %fusion.42, s32[]{:T(128)S(6)} %select_n.183), kind=kOutput, calls=%fused_computation.65 | convolution fusion | flops 1611661312 | bytes 13369348 | tf_op jit(solution)/shard_map/dot_general | solution.py:18
  569.2 26.4 %collective-permute-done.28 = f32[512,256]{1,0:T(8,128)S(1)} collective-permute-done((f32[512,256]{1,0:T(8,128)S(1)}, f32[512,256]{1,0:T(8,128)S(1)}, u32[]{:S(2)}, u32[]{:S(2)}) %collective-permute-start.28) | collective-permute-done | bytes 524320 | tf_op jit(solution)/shard_map/ppermute | solution.py:35
  598.3 6.3 collective-permute-done.30
  613.3 19.6 %collective-permute-done.25 = f32[256,768]{1,0:T(8,128)S(1)} collective-permute-done((f32[256,768]{1,0:T(8,128)S(1)}, f32[256,768]{1,0:T(8,128)S(1)}, u32[]{:S(2)}, u32[]{:S(2)}) %collective-permute-start.25) | collective-permute-done | bytes 786464 | tf_op jit(solution)/shard_map/ppermute | solution.py:35
  641.1 13.5 %collective-permute-done.33 = f32[512,256]{1,0:T(8,128)S(1)} collective-permute-done((f32[512,256]{1,0:T(8,128)S(1)}, f32[512,256]{1,0:T(8,128)S(1)}, u32[]{:S(2)}, u32[]{:S(2)}) %collective-permute-start.33) | collective-permute-done | bytes 524320 | tf_op jit(solution)/shard_map/ppermute | solution.py:35
  664.2 11.0 %collective-permute-done.22 = f32[256,768]{1,0:T(8,128)S(1)} collective-permute-done((f32[256,768]{1,0:T(8,128)S(1)}, f32[256,768]{1,0:T(8,128)S(1)}, u32[]{:S(2)}, u32[]{:S(2)}) %collective-permute-start.22) | collective-permute-done | bytes 786464 | tf_op jit(solution)/shard_map/ppermute | solution.py:35
  675.3 9.7 %collective-permute-done.26 = f32[256,768]{1,0:T(8,128)S(1)} collective-permute-done((f32[256,768]{1,0:T(8,128)S(1)}, f32[256,768]{1,0:T(8,128)S(1)}, u32[]{:S(2)}, u32[]{:S(2)}) %collective-permute-start.26) | collective-permute-done | bytes 786464 | tf_op jit(solution)/shard_map/ppermute | solution.py:35
  (325 shorter events, 211.2 us)
Async XLA Ops:
  31.3 95.2 %collective-permute-start.40 = (f32[256,2048]{1,0:T(8,128)}, f32[256,2048]{1,0:T(8,128)}, u32[]{:S(2)}, u32[]{:S(2)}) collective-permute-start(f32[256,2048]{1,0:T(8,128)} %dynamic-slice_convert_fusion), channel_id=1, source_target_pairs={{0,16},{4,20},{8,24},{12,28},{16,0},{20,4},{24,8},{28,12},{1,17},{... | collective-permute-start | bytes 6291464 | tf_op jit(solution)/shard_map/ppermute | solution.py:35
  34.9 93.1 %collective-permute-start.41 = (f32[256,2048]{1,0:T(8,128)}, f32[256,2048]{1,0:T(8,128)}, u32[]{:S(2)}, u32[]{:S(2)}) collective-permute-start(f32[256,2048]{1,0:T(8,128)} %dynamic-slice_convert_fusion), channel_id=1, source_target_pairs={{0,4},{4,0},{8,12},{12,8},{16,20},{20,16},{24,28},{28,24},{1,5},{5... | collective-permute-start | bytes 6291464 | tf_op jit(solution)/shard_map/ppermute | solution.py:35
  40.3 91.0 %collective-permute-start.1 = (f32[256,2048]{1,0:T(8,128)}, f32[256,2048]{1,0:T(8,128)}, u32[]{:S(2)}, u32[]{:S(2)}) collective-permute-start(f32[256,2048]{1,0:T(8,128)} %dynamic-slice_add_fusion.3), channel_id=1, source_target_pairs={{0,2},{1,3},{2,0},{3,1},{4,6},{5,7},{6,4},{7,5},{8,10},{9,11},{10,... | collective-permute-start | bytes 6291464 | tf_op jit(solution)/shard_map/ppermute | solution.py:35
  128.0 48.7 %collective-permute-start.43 = (f32[256,2048]{1,0:T(8,128)}, f32[256,2048]{1,0:T(8,128)S(1)}, u32[]{:S(2)}, u32[]{:S(2)}) collective-permute-start(f32[256,2048]{1,0:T(8,128)} %collective-permute-done.40), channel_id=1, source_target_pairs={{0,1},{1,0},{2,3},{3,2},{4,5},{5,4},{6,7},{7,6},{8,9},{9,8},{10,11... | collective-permute-start | bytes 6291464 | tf_op jit(solution)/shard_map/ppermute | solution.py:35
  128.0 49.9 %collective-permute-start.44 = (f32[256,2048]{1,0:T(8,128)}, f32[256,2048]{1,0:T(8,128)S(1)}, u32[]{:S(2)}, u32[]{:S(2)}) collective-permute-start(f32[256,2048]{1,0:T(8,128)} %collective-permute-done.41), channel_id=1, source_target_pairs={{0,1},{1,0},{2,3},{3,2},{4,5},{5,4},{6,7},{7,6},{8,9},{9,8},{10,11... | collective-permute-start | bytes 6291464 | tf_op jit(solution)/shard_map/ppermute | solution.py:35
  138.7 117.1 %collective-permute-start.34 = (f32[256,2048]{1,0:T(8,128)}, f32[256,2048]{1,0:T(8,128)}, u32[]{:S(2)}, u32[]{:S(2)}) collective-permute-start(f32[256,2048]{1,0:T(8,128)} %get-tuple-element.15), channel_id=1, source_target_pairs={{0,16},{4,20},{8,24},{12,28},{16,0},{20,4},{24,8},{28,12},{1,17},{... | collective-permute-start | bytes 6291464 | tf_op jit(solution)/shard_map/ppermute | solution.py:35
  174.1 82.6 %collective-permute-start.35 = (f32[256,2048]{1,0:T(8,128)}, f32[256,2048]{1,0:T(8,128)}, u32[]{:S(2)}, u32[]{:S(2)}) collective-permute-start(f32[256,2048]{1,0:T(8,128)} %get-tuple-element.15), channel_id=1, source_target_pairs={{0,4},{4,0},{8,12},{12,8},{16,20},{20,16},{24,28},{28,24},{1,5},{5... | collective-permute-start | bytes 6291464 | tf_op jit(solution)/shard_map/ppermute | solution.py:35
  176.7 49.6 %collective-permute-start.45 = (f32[256,2048]{1,0:T(8,128)S(1)}, f32[256,2048]{1,0:T(8,128)S(1)}, u32[]{:S(2)}, u32[]{:S(2)}) collective-permute-start(f32[256,2048]{1,0:T(8,128)S(1)} %collective-permute-done.42), channel_id=1, source_target_pairs={{0,1},{1,0},{2,3},{3,2},{4,5},{5,4},{6,7},{7,6},{8,9},{9,8},{10,11... | collective-permute-start | bytes 6291464 | tf_op jit(solution)/shard_map/ppermute | solution.py:35
  256.5 50.4 %collective-permute-start.37 = (f32[256,2048]{1,0:T(8,128)}, f32[256,2048]{1,0:T(8,128)S(1)}, u32[]{:S(2)}, u32[]{:S(2)}) collective-permute-start(f32[256,2048]{1,0:T(8,128)} %collective-permute-done.34), channel_id=1, source_target_pairs={{0,1},{1,0},{2,3},{3,2},{4,5},{5,4},{6,7},{7,6},{8,9},{9,8},{10,11... | collective-permute-start | bytes 6291464 | tf_op jit(solution)/shard_map/ppermute | solution.py:35
  256.8 51.5 %collective-permute-start.38 = (f32[256,2048]{1,0:T(8,128)}, f32[256,2048]{1,0:T(8,128)S(1)}, u32[]{:S(2)}, u32[]{:S(2)}) collective-permute-start(f32[256,2048]{1,0:T(8,128)} %collective-permute-done.35), channel_id=1, source_target_pairs={{0,1},{1,0},{2,3},{3,2},{4,5},{5,4},{6,7},{7,6},{8,9},{9,8},{10,11... | collective-permute-start | bytes 6291464 | tf_op jit(solution)/shard_map/ppermute | solution.py:35
  266.9 91.1 %collective-permute-start.4 = (f32[256,2048]{1,0:T(8,128)S(1)}, f32[256,2048]{1,0:T(8,128)S(1)}, u32[]{:S(2)}, u32[]{:S(2)}) collective-permute-start(f32[256,2048]{1,0:T(8,128)S(1)} %dynamic-slice_add_fusion.2), channel_id=1, source_target_pairs={{0,2},{1,3},{2,0},{3,1},{4,6},{5,7},{6,4},{7,5},{8,10},{9,11},{10,... | collective-permute-start | bytes 6291464 | tf_op jit(solution)/shard_map/ppermute | solution.py:35
  304.2 56.7 %collective-permute-start.39 = (f32[256,2048]{1,0:T(8,128)}, f32[256,2048]{1,0:T(8,128)S(1)}, u32[]{:S(2)}, u32[]{:S(2)}) collective-permute-start(f32[256,2048]{1,0:T(8,128)} %collective-permute-done.36), channel_id=1, source_target_pairs={{0,1},{1,0},{2,3},{3,2},{4,5},{5,4},{6,7},{7,6},{8,9},{9,8},{10,11... | collective-permute-start | bytes 6291464 | tf_op jit(solution)/shard_map/ppermute | solution.py:35
  360.3 128.7 %collective-permute-start.5 = (f32[256,2048]{1,0:T(8,128)}, f32[256,2048]{1,0:T(8,128)}, u32[]{:S(2)}, u32[]{:S(2)}) collective-permute-start(f32[256,2048]{1,0:T(8,128)} %get-tuple-element.34), channel_id=1, source_target_pairs={{0,1},{1,0},{2,3},{3,2},{4,5},{5,4},{6,7},{7,6},{8,9},{9,8},{10,11... | collective-permute-start | bytes 6291464 | tf_op jit(solution)/shard_map/ppermute | solution.py:35
  360.3 68.4 %collective-permute-start.8 = (f32[256,2048]{1,0:T(8,128)S(1)}, f32[256,2048]{1,0:T(8,128)}, u32[]{:S(2)}, u32[]{:S(2)}) collective-permute-start(f32[256,2048]{1,0:T(8,128)S(1)} %get-tuple-element.33), channel_id=1, source_target_pairs={{0,1},{1,0},{2,3},{3,2},{4,5},{5,4},{6,7},{7,6},{8,9},{9,8},{10,11... | collective-permute-start | bytes 6291464 | tf_op jit(solution)/shard_map/ppermute | solution.py:35
  416.8 64.6 %collective-permute-start.46 = (f32[256,2048]{1,0:T(8,128)}, f32[256,2048]{1,0:T(8,128)}, u32[]{:S(2)}, u32[]{:S(2)}) collective-permute-start(f32[256,2048]{1,0:T(8,128)} %convolution_add_fusion.5), channel_id=1, source_target_pairs={{0,8},{4,12},{8,0},{12,4},{16,24},{20,28},{24,16},{28,20},{1,9},{5... | collective-permute-start | bytes 6291464 | tf_op jit(solution)/shard_map/ppermute | solution.py:35
  422.1 88.4 %collective-permute-start.47 = (f32[256,2048]{1,0:T(8,128)}, f32[256,2048]{1,0:T(8,128)}, u32[]{:S(2)}, u32[]{:S(2)}) collective-permute-start(f32[256,2048]{1,0:T(8,128)} %convolution_add_fusion.3), channel_id=1, source_target_pairs={{0,8},{4,12},{8,0},{12,4},{16,24},{20,28},{24,16},{28,20},{1,9},{5... | collective-permute-start | bytes 6291464 | tf_op jit(solution)/shard_map/ppermute | solution.py:35
  427.9 126.7 %collective-permute-start.48 = (f32[2048,256]{1,0:T(8,128)}, f32[2048,256]{1,0:T(8,128)}, u32[]{:S(2)}, u32[]{:S(2)}) collective-permute-start(f32[2048,256]{1,0:T(8,128)} %convolution_add_fusion.1), channel_id=1, source_target_pairs={{0,8},{4,12},{8,0},{12,4},{16,24},{20,28},{24,16},{28,20},{1,9},{5... | collective-permute-start | bytes 6291464 | tf_op jit(solution)/shard_map/ppermute | solution.py:35
  478.6 83.0 %collective-permute-start.9 = (f32[256,2048]{1,0:T(8,128)S(1)}, f32[256,2048]{1,0:T(8,128)S(1)}, u32[]{:S(2)}, u32[]{:S(2)}) collective-permute-start(f32[256,2048]{1,0:T(8,128)S(1)} %constant_dynamic-slice_fusion.8), channel_id=1, source_target_pairs={{0,1},{1,0},{2,3},{3,2},{4,5},{5,4},{6,7},{7,6},{8,9},{9,8},{10,11... | collective-permute-start | bytes 6291464 | tf_op jit(solution)/shard_map/ppermute | solution.py:35
  481.4 85.6 %collective-permute-start.24 = (f32[256,768]{1,0:T(8,128)S(1)}, f32[256,768]{1,0:T(8,128)S(1)}, u32[]{:S(2)}, u32[]{:S(2)}) collective-permute-start(f32[256,768]{1,0:T(8,128)S(1)} %fusion.94), channel_id=1, source_target_pairs={{0,4},{4,0},{8,12},{12,8},{16,20},{20,16},{24,28},{28,24},{1,5},{5... | collective-permute-start | bytes 2359304 | tf_op jit(solution)/shard_map/ppermute | solution.py:35
  489.1 123.1 %collective-permute-start.23 = (f32[256,768]{1,0:T(8,128)S(1)}, f32[256,768]{1,0:T(8,128)S(1)}, u32[]{:S(2)}, u32[]{:S(2)}) collective-permute-start(f32[256,768]{1,0:T(8,128)S(1)} %fusion.97), channel_id=1, source_target_pairs={{0,4},{4,0},{8,12},{12,8},{16,20},{20,16},{24,28},{28,24},{1,5},{5... | collective-permute-start | bytes 2359304 | tf_op jit(solution)/shard_map/ppermute | solution.py:35
  510.5 55.5 %collective-permute-start.31 = (f32[512,256]{1,0:T(8,128)S(1)}, f32[512,256]{1,0:T(8,128)S(1)}, u32[]{:S(2)}, u32[]{:S(2)}) collective-permute-start(f32[512,256]{1,0:T(8,128)S(1)} %fusion.79), channel_id=1, source_target_pairs={{0,4},{4,0},{8,12},{12,8},{16,20},{20,16},{24,28},{28,24},{1,5},{5... | collective-permute-start | bytes 1572872 | tf_op jit(solution)/shard_map/ppermute | solution.py:35
  561.9 73.3 %collective-permute-start.10 = (f32[256,2048]{1,0:T(8,128)S(1)}, f32[256,2048]{1,0:T(8,128)S(1)}, u32[]{:S(2)}, u32[]{:S(2)}) collective-permute-start(f32[256,2048]{1,0:T(8,128)S(1)} %dynamic-slice_add_fusion), channel_id=1, source_target_pairs={{0,2},{1,3},{2,0},{3,1},{4,6},{5,7},{6,4},{7,5},{8,10},{9,11},{10,... | collective-permute-start | bytes 6291464 | tf_op jit(solution)/shard_map/ppermute | solution.py:35
  604.6 58.6 %collective-permute-start.20 = (f32[256,768]{1,0:T(8,128)S(1)}, f32[256,768]{1,0:T(8,128)S(1)}, u32[]{:S(2)}, u32[]{:S(2)}) collective-permute-start(f32[256,768]{1,0:T(8,128)S(1)} %fusion.103), channel_id=1, source_target_pairs={{0,4},{4,0},{8,12},{12,8},{16,20},{20,16},{24,28},{28,24},{1,5},{5... | collective-permute-start | bytes 2359304 | tf_op jit(solution)/shard_map/ppermute | solution.py:35
  637.5 54.6 %collective-permute-start.11 = (f32[256,2048]{1,0:T(8,128)S(1)}, f32[256,2048]{1,0:T(8,128)S(1)}, u32[]{:S(2)}, u32[]{:S(2)}) collective-permute-start(f32[256,2048]{1,0:T(8,128)S(1)} %subtract_add_fusion), channel_id=1, source_target_pairs={{0,1},{1,0},{2,3},{3,2},{4,5},{5,4},{6,7},{7,6},{8,9},{9,8},{10,11... | collective-permute-start | bytes 6291464 | tf_op jit(solution)/shard_map/ppermute | solution.py:35
  (88 other events, 1310.4 us)

commit v2 on v1

--- a/solution.py
+++ b/solution.py
@@ -1,6 +1,10 @@
+import functools
+
 import jax
 import jax.numpy as jnp
 from jax import lax
+from jax.experimental import pallas as pl
+from jax.experimental.pallas import tpu as pltpu
 from jax.sharding import PartitionSpec as P
 
 HEAD_SIZE = 64
@@ -128,6 +132,625 @@
 def per_sequence(step, *fields):
     results = [step(*[field[s] for field in fields]) for s in range(fields[0].shape[0])]
     return [jnp.stack(parts) for parts in zip(*results)]
+
+
+MESH = pl.DeviceIdType.MESH
+CHUNKS = 4
+TILE = 256
+ROWS = 16
+
+
+def flip(index, bit):
+    return index + bit * (1 - 2 * ((index // bit) % 2))
+
+
+def loop(count, step):
+    lax.fori_loop(0, count, lambda i, carry: (step(i), carry)[1], 0)
+
+
+def middle_kernel(
+    heads_ref,
+    w_out_ref,
+    tokens_ref,
+    cot_ref,
+    cot_half_ref,
+    gain_ref,
+    w_gate_ref,
+    w_up_ref,
+    w_down_ref,
+    query_ref,
+    keys_ref,
+    values_ref,
+    log_total_ref,
+    segment_column_ref,
+    segment_row_ref,
+    cosine_ref,
+    sine_ref,
+    grad_hidden_out,
+    grad_attn_out,
+    projected_out,
+    grad_attn_far,
+    projected_far,
+    mixed_half_out,
+    mixed_twin_out,
+    normed_out,
+    activation_out,
+    grad_gate_out,
+    grad_up_out,
+    gain_out,
+    cot_others,
+    normed_others,
+    gate_w,
+    up_w,
+    down_w,
+    cot,
+    hidden,
+    normed,
+    normed_sent,
+    normed_twin,
+    act,
+    gg,
+    gu,
+    away,
+    mine,
+    core_in,
+    y_in,
+    local_sem,
+    core_send,
+    core_recv,
+    y_send,
+    y_recv,
+    cot_send,
+    cot_recv,
+    n_send,
+    n_recv,
+    twin_send,
+    twin_recv,
+    end_send,
+    end_recv,
+    hidden_send,
+    hidden_recv,
+    far_send,
+    far_recv,
+):
+    dp, tensor = lax.axis_index("dp"), lax.axis_index("tensor")
+    core = tensor % 2
+    twin_id = (dp, flip(tensor, 1))
+    y_id = (dp, flip(tensor, 2))
+    x_id = (flip(dp, 1), tensor)
+    z_id = (flip(dp, 4), tensor)
+    far_id = (flip(dp, 2), tensor)
+    heads = gg.at[:, pl.ds(0, heads_ref.shape[1])]
+    tok = gu.at[pl.ds(0, hidden.shape[0])]
+    half, width = hidden.shape
+    hidden_units = gate_w.shape[1]
+    chunk = half // CHUNKS
+    my_row = pl.multiple_of(core * half, half)
+    twin_row = pl.multiple_of((1 - core) * half, half)
+
+    def remote(src, dst, send, recv, device):
+        return pltpu.make_async_remote_copy(
+            src_ref=src, dst_ref=dst, send_sem=send, recv_sem=recv,
+            device_id=device, device_id_type=MESH,
+        )
+
+    loads = {
+        "heads": pltpu.make_async_copy(heads_ref, heads, local_sem.at[0]),
+        "w_out": pltpu.make_async_copy(w_out_ref, act, local_sem.at[1]),
+        "tok": pltpu.make_async_copy(tokens_ref.at[pl.ds(my_row, half)], tok, local_sem.at[2]),
+        "cot": pltpu.make_async_copy(cot_ref, cot, local_sem.at[3]),
+        "gate": pltpu.make_async_copy(w_gate_ref, gate_w, local_sem.at[4]),
+        "up": pltpu.make_async_copy(w_up_ref, up_w, local_sem.at[5]),
+        "down": pltpu.make_async_copy(w_down_ref, down_w, local_sem.at[6]),
+    }
+    for name in loads:
+        loads[name].start()
+
+    barrier = pltpu.get_barrier_semaphore()
+    for device in (twin_id, y_id, x_id, z_id, far_id):
+        pl.semaphore_signal(barrier, inc=1, device_id=device, device_id_type=MESH)
+    pl.semaphore_wait(barrier, 5)
+
+    def rows(k):
+        return pl.ds(pl.multiple_of(k * chunk, chunk), chunk)
+
+    def from_x(source, slots, k, send, recv):
+        return remote(source.at[rows(k)], slots.at[0, rows(k)], send.at[0, k], recv.at[0, k], x_id)
+
+    def from_z(source, slots, k, send, recv):
+        return remote(source.at[rows(k)], slots.at[1, rows(k)], send.at[1, k], recv.at[1, k], z_id)
+
+    def from_zx(slots, k, send, recv):
+        return remote(
+            slots.at[1, rows(k)], slots.at[2, rows(k)], send.at[2, k], recv.at[2, k], x_id
+        )
+
+    def to_twin(slots, which, slot):
+        return remote(
+            slots.at[slot], slots.at[3 + slot],
+            twin_send.at[which, slot], twin_recv.at[which, slot], twin_id,
+        )
+
+    def send_z(source, slots, k, send, recv):
+        from_z(source, slots, k, send, recv).start()
+        from_z(source, slots, k + 1, send, recv).start()
+
+    def relay(source, slots, k, send, recv):
+        for i in (k, k + 1):
+            from_z(source, slots, i, send, recv).wait_recv()
+            from_zx(slots, i, send, recv).start()
+            from_z(source, slots, i, send, recv).wait_send()
+
+    send_z(cot_half_ref, cot_others, 0, cot_send, cot_recv)
+    for k in range(CHUNKS):
+        from_x(cot_half_ref, cot_others, k, cot_send, cot_recv).start()
+
+    loads["heads"].wait()
+    loads["w_out"].wait()
+
+    def project(into, first_row):
+        def step(j):
+            columns = pl.ds(pl.multiple_of(j * TILE, TILE), TILE)
+            into[:, columns] = jnp.dot(
+                heads[pl.ds(first_row, half), :], act[:, columns], preferred_element_type=F32
+            )
+
+        loop(width // TILE, step)
+
+    def core_copy(which, window, k):
+        return remote(
+            away.at[window], core_in.at[which].at[window],
+            core_send.at[which, k], core_recv.at[which, k], twin_id,
+        )
+
+    def y_copy(which, window, k):
+        return remote(
+            mine.at[which % 2].at[window], y_in.at[which % 2].at[window],
+            y_send.at[which, k], y_recv.at[which, k], y_id,
+        )
+
+    everything = slice(None)
+    row_windows = [(rows(k), everything) for k in range(CHUNKS)]
+
+    def column_window(j):
+        return (everything, pl.ds(pl.multiple_of(j * TILE, TILE), TILE))
+
+    project(away, twin_row)
+    for k in range(CHUNKS):
+        core_copy(0, row_windows[k], k).start()
+    project(mine.at[0], my_row)
+    for k in range(CHUNKS):
+        core_copy(0, row_windows[k], k).wait_recv()
+
+        def add(i, k=k):
+            window = pl.ds(pl.multiple_of(k * chunk + i * ROWS, ROWS), ROWS)
+            mine[0, window, :] = mine[0, window, :] + core_in[0, window, :]
+
+        loop(chunk // ROWS, add)
+        y_copy(0, row_windows[k], k).start()
+
+    loads["tok"].wait()
+    gain = gain_ref[...]
+    for k in range(CHUNKS):
+        y_copy(0, row_windows[k], k).wait_recv()
+
+        def normalize_rows(i, k=k):
+            offset = pl.multiple_of(k * chunk + i * ROWS, ROWS)
+            window = pl.ds(offset, ROWS)
+            values = tok[window, :].astype(F32) + (mine[0, window, :] + y_in[0, window, :])
+            scale = lax.rsqrt(jnp.mean(values * values, axis=-1, keepdims=True) + EPSILON)
+            rounded = (values * scale * gain).astype(BF16)
+            hidden[window, :] = values
+            normed[pl.ds(pl.multiple_of(my_row + offset, ROWS), ROWS), :] = rounded
+            normed_sent[window, :] = rounded.astype(F32)
+
+        loop(chunk // ROWS, normalize_rows)
+        remote(
+            normed_sent.at[rows(k)], normed_twin.at[rows(k)],
+            n_send.at[3, k], n_recv.at[3, k], twin_id,
+        ).start()
+        if k == 2:
+            relay(cot_half_ref, cot_others, 0, cot_send, cot_recv)
+            send_z(cot_half_ref, cot_others, 2, cot_send, cot_recv)
+        from_x(normed_sent, normed_others, k, n_send, n_recv).start()
+    for k in range(CHUNKS):
+        remote(
+            normed_sent.at[rows(k)], normed_twin.at[rows(k)],
+            n_send.at[3, k], n_recv.at[3, k], twin_id,
+        ).wait_recv()
+
+        def take(i, k=k):
+            offset = pl.multiple_of(k * chunk + i * ROWS, ROWS)
+            normed[pl.ds(pl.multiple_of(twin_row + offset, ROWS), ROWS), :] = normed_twin[
+                pl.ds(offset, ROWS), :
+            ].astype(BF16)
+
+        loop(chunk // ROWS, take)
+
+    for name in ("cot", "gate", "up", "down"):
+        loads[name].wait()
+
+    def units(j):
+        columns = pl.ds(pl.multiple_of(j * TILE, TILE), TILE)
+        gate = jnp.dot(normed[...], gate_w[:, columns], preferred_element_type=F32)
+        up = jnp.dot(normed[...], up_w[:, columns], preferred_element_type=F32)
+        back = lax.dot_general(
+            cot[...], down_w[columns, :], (((1,), (1,)), ((), ())), preferred_element_type=F32
+        )
+        sigmoid = jax.nn.sigmoid(gate)
+        swish = gate * sigmoid
+        act[:, columns] = (swish * up).astype(BF16)
+        gg[:, columns] = (back * up * sigmoid * (1.0 + gate * (1.0 - sigmoid))).astype(BF16)
+        gu[:, columns] = (back * swish).astype(BF16)
+
+    loop(hidden_units // TILE, units)
+
+    tiles = width // TILE
+    for k in range(CHUNKS):
+        core_copy(0, row_windows[k], k).wait_send()
+
+    def column_sums(which, tile_product, forwarded=True):
+        def produce(j):
+            value = tile_product(j)
+            columns = pl.ds(pl.multiple_of(j * TILE, TILE), TILE)
+            away[:, columns] = value[0]
+            mine[which % 2, :, columns] = value[1]
+            core_copy(which, column_window(j), j).start()
+
+        def forward(j):
+            core_copy(which, column_window(j), j).wait_recv()
+            columns = pl.ds(pl.multiple_of(j * TILE, TILE), TILE)
+            mine[which % 2, :, columns] = (
+                mine[which % 2, :, columns] + core_in[which, :, columns]
+            )
+            if forwarded:
+                y_copy(which, column_window(j), j).start()
+
+        produce(0)
+
+        def step(j):
+            produce(j + 1)
+            forward(j)
+
+        loop(tiles - 1, step)
+        forward(tiles - 1)
+
+    def halves(dot_of):
+        return dot_of(pl.ds(twin_row, half)), dot_of(pl.ds(my_row, half))
+
+    transposed = (((1,), (1,)), ((), ()))
+
+    def back_tile(j):
+        columns = pl.ds(pl.multiple_of(j * TILE, TILE), TILE)
+        return halves(
+            lambda part: lax.dot_general(
+                gg[part, :], gate_w[columns, :], transposed, preferred_element_type=F32
+            )
+            + lax.dot_general(
+                gu[part, :], up_w[columns, :], transposed, preferred_element_type=F32
+            )
+        )
+
+    def branch_tile(j):
+        columns = pl.ds(pl.multiple_of(j * TILE, TILE), TILE)
+        return halves(
+            lambda part: jnp.dot(act[part, :], down_w[:, columns], preferred_element_type=F32)
+        )
+
+    column_sums(1, back_tile)
+    stores = [
+        pltpu.make_async_copy(normed, normed_out, local_sem.at[7]),
+        pltpu.make_async_copy(act, activation_out, local_sem.at[8]),
+        pltpu.make_async_copy(gg, grad_gate_out, local_sem.at[9]),
+        pltpu.make_async_copy(gu, grad_up_out, local_sem.at[10]),
+    ]
+    for store in stores:
+        store.start()
+    relay(cot_half_ref, cot_others, 2, cot_send, cot_recv)
+    send_z(normed_sent, normed_others, 0, n_send, n_recv)
+    loop(tiles, lambda j: core_copy(1, column_window(j), j).wait_send())
+    for k in range(CHUNKS):
+        y_copy(0, row_windows[k], k).wait_send()
+    column_sums(2, branch_tile, forwarded=False)
+    for k in range(CHUNKS):
+        from_x(cot_half_ref, cot_others, k, cot_send, cot_recv).wait_recv()
+    to_twin(cot_others, 0, 0).start()
+    to_twin(cot_others, 0, 1).start()
+
+    for store in stores:
+        store.wait()
+    operands = [
+        pltpu.make_async_copy(query_ref, act.at[:, pl.ds(0, 512)], local_sem.at[0]),
+        pltpu.make_async_copy(keys_ref, act.at[:, pl.ds(1024, 512)], local_sem.at[1]),
+        pltpu.make_async_copy(values_ref, act.at[:, pl.ds(1536, 512)], local_sem.at[2]),
+        pltpu.make_async_copy(w_out_ref, gate_w.at[pl.ds(0, 512)], local_sem.at[3]),
+    ]
+    for operand in operands:
+        operand.start()
+
+    loop(tiles, lambda j: y_copy(1, column_window(j), j).wait_recv())
+    loop(tiles, lambda j: y_copy(2, column_window(j), j).start())
+    gain_out[...] = jnp.zeros_like(gain_out)
+
+    def hidden_copy(k):
+        return remote(
+            core_in.at[0, rows(k)], normed_twin.at[rows(k)],
+            hidden_send.at[k], hidden_recv.at[k], twin_id,
+        )
+
+    for k in range(CHUNKS):
+
+        def norm_rows(i, k=k):
+            offset = pl.multiple_of(k * chunk + i * ROWS, ROWS)
+            window = pl.ds(offset, ROWS)
+            incoming = mine[1, window, :] + y_in[1, window, :]
+            values = hidden[window, :]
+            scale = lax.rsqrt(jnp.mean(values * values, axis=-1, keepdims=True) + EPSILON)
+            weighted = incoming * gain
+            inner = jnp.mean(weighted * values, axis=-1, keepdims=True)
+            back = scale * weighted - values * (scale * scale * scale) * inner
+            here = pl.ds(pl.multiple_of(my_row + offset, ROWS), ROWS)
+            total = cot[here, :].astype(F32) + back
+            core_in[0, window, :] = total
+            normed[here, :] = total.astype(BF16)
+            gain_out[...] = gain_out[...] + jnp.sum(
+                incoming * values * scale, axis=0, keepdims=True
+            )
+
+        loop(chunk // ROWS, norm_rows)
+        hidden_copy(k).start()
+    hidden_store = pltpu.make_async_copy(core_in.at[0], grad_hidden_out, local_sem.at[4])
+    hidden_store.start()
+    relay(normed_sent, normed_others, 0, n_send, n_recv)
+    send_z(normed_sent, normed_others, 2, n_send, n_recv)
+    for k in range(CHUNKS):
+        hidden_copy(k).wait_recv()
+
+        def take_hidden(i, k=k):
+            offset = pl.multiple_of(k * chunk + i * ROWS, ROWS)
+            normed[pl.ds(pl.multiple_of(twin_row + offset, ROWS), ROWS), :] = normed_twin[
+                pl.ds(offset, ROWS), :
+            ].astype(BF16)
+
+        loop(chunk // ROWS, take_hidden)
+    grad_attn_store = pltpu.make_async_copy(normed, grad_attn_out, local_sem.at[5])
+    grad_attn_store.start()
+
+    def far_columns(b):
+        z_low = (dp // 2) % 2
+        return pl.ds(pl.multiple_of(b * 1024 + (1 - z_low) * 512, 512), 512)
+
+    def far_copies():
+        copies = []
+        for b in range(2):
+            kept = pl.ds(b * 512, 512)
+            copies.append(remote(
+                core_in.at[0, :, far_columns(b)], grad_attn_far.at[0, :, kept],
+                far_send.at[b], far_recv.at[b], far_id,
+            ))
+            copies.append(remote(
+                normed_twin.at[:, far_columns(b)], grad_attn_far.at[1, :, kept],
+                far_send.at[2 + b], far_recv.at[2 + b], far_id,
+            ))
+        return copies
+
+    for copy in far_copies():
+        copy.start()
+
+    for operand in operands:
+        operand.wait()
+
+    def head_tile(j):
+        columns = pl.ds(pl.multiple_of(j * TILE, TILE), TILE)
+        act[:, pl.ds(pl.multiple_of(512 + j * TILE, TILE), TILE)] = lax.dot_general(
+            normed[...], gate_w[columns, :], transposed, preferred_element_type=F32
+        ).astype(BF16)
+
+    loop(512 // TILE, head_tile)
+    sums = y_in.at[1]
+    sums[:, pl.ds(0, 1024)] = jnp.zeros((TILE, 1024), F32)
+
+    def gather_into(offset, kv, value):
+        for part in range(value.shape[0] // TILE):
+            columns = pl.ds(pl.multiple_of(offset + kv * 256 + part * 128, 128), 128)
+            sums[:, columns] = sums[:, columns] + value[part * TILE : (part + 1) * TILE]
+
+    factor = HEAD_SIZE ** (-0.5)
+    lane = lax.broadcasted_iota(jnp.int32, (TILE, 128), 1)
+
+    def unrotate_tile(value, window):
+        turned = jnp.where(
+            lane % 64 < 32, pltpu.roll(value, 96, 1), pltpu.roll(value, 32, 1)
+        )
+        return value * cosine_ref[window, :] + turned * sine_ref[window, :]
+
+    def put(block, column, value):
+        rounded = value.astype(BF16)
+        gu[pl.ds(block * TILE, TILE), pl.ds(column, 128)] = rounded
+        core_in[1, :, pl.ds(block * 1024 + column, 128)] = rounded.astype(F32)
+
+    def pair(p):
+        kv = p // 2
+        column = pl.multiple_of(p * 128, 128)
+        for block in range(2):
+            keys_seen = (block + 1) * TILE
+            window = pl.ds(block * TILE, TILE)
+            seen = pl.ds(0, keys_seen)
+            queries = act[window, pl.ds(column, 128)]
+            upstream = act[window, pl.ds(pl.multiple_of(512 + column, 128), 128)]
+            key_place = lax.broadcasted_iota(jnp.int32, (keys_seen, TILE), 0)
+            query_place = lax.broadcasted_iota(jnp.int32, (keys_seen, TILE), 1) + block * TILE
+            allowed = (key_place <= query_place) & (
+                segment_column_ref[seen, :] == segment_row_ref[:, window]
+            )
+            query_grad = jnp.zeros((TILE, 128), F32)
+            for side in range(2):
+                padded = pl.multiple_of((kv * 2 + side) * 128, 128)
+                keys = act[seen, pl.ds(pl.multiple_of(1024 + padded, 128), 128)]
+                vals = act[seen, pl.ds(pl.multiple_of(1536 + padded, 128), 128)]
+                raw = lax.dot_general(
+                    keys, queries, transposed, preferred_element_type=F32
+                ) * factor
+                log_total = log_total_ref[pl.ds(2 * p + side, 1), window]
+                probs = jnp.exp(jnp.where(allowed, raw - log_total, MASKED))
+                grad_probs = lax.dot_general(
+                    vals, upstream, transposed, preferred_element_type=F32
+                )
+                row_sum = jnp.sum(probs * grad_probs, axis=0, keepdims=True)
+                grad_raw = (probs * (grad_probs - row_sum)).astype(BF16)
+                query_grad = query_grad + lax.dot_general(
+                    grad_raw, keys, (((0,), (0,)), ((), ())), preferred_element_type=F32
+                )
+                own = (lax.broadcasted_iota(jnp.int32, (keys_seen, 128), 1) // 64) == side
+                gather_into(0, kv, jnp.where(
+                    own, jnp.dot(grad_raw, queries, preferred_element_type=F32), 0.0
+                ))
+                gather_into(512, kv, jnp.where(
+                    own, jnp.dot(probs.astype(BF16), upstream, preferred_element_type=F32), 0.0
+                ))
+            put(block, column, unrotate_tile(query_grad * factor, window))
+
+    loop(4, pair)
+
+    def both(offset, block):
+        def folded(kv):
+            value = sums[:, pl.ds(offset + kv * 256 + block * 128, 128)]
+            return value + pltpu.roll(value, 64, 1)
+
+        return jnp.where(lane < 64, folded(0), folded(1))
+
+    for block in range(2):
+        window = pl.ds(block * TILE, TILE)
+        put(block, 512, unrotate_tile(both(0, block) * factor, window))
+        put(block, 640, both(512, block))
+    projected_store = pltpu.make_async_copy(
+        gu.at[:, pl.ds(0, 768)], projected_out, local_sem.at[6]
+    )
+    projected_store.start()
+
+    def projected_copy(b):
+        window = (everything, pl.ds(b * 1024, 768))
+        return remote(
+            core_in.at[1].at[window], projected_far.at[window],
+            far_send.at[4 + b], far_recv.at[4 + b], far_id,
+        )
+
+    projected_copy(0).start()
+    projected_copy(1).start()
+
+    for k in range(CHUNKS):
+        from_x(normed_sent, normed_others, k, n_send, n_recv).wait_recv()
+    to_twin(normed_others, 1, 0).start()
+    for k in range(CHUNKS):
+        from_zx(cot_others, k, cot_send, cot_recv).wait_recv()
+    to_twin(cot_others, 0, 2).start()
+    relay(normed_sent, normed_others, 2, n_send, n_recv)
+    to_twin(normed_others, 1, 1).start()
+
+    loop(tiles, lambda j: y_copy(2, column_window(j), j).wait_recv())
+    loop(tiles, lambda j: y_copy(2, column_window(j), j).wait_send())
+
+    def mixed_rows(i):
+        window = pl.ds(pl.multiple_of(i * ROWS, ROWS), ROWS)
+        mine[0, window, :] = hidden[window, :] + (mine[0, window, :] + y_in[0, window, :])
+
+    loop(half // ROWS, mixed_rows)
+    mixed_copy = remote(
+        mine.at[0], mixed_twin_out, end_send.at[1], end_recv.at[1], twin_id
+    )
+    mixed_copy.start()
+    mixed_store = pltpu.make_async_copy(mine.at[0], mixed_half_out, local_sem.at[12])
+    mixed_store.start()
+    for k in range(CHUNKS):
+        from_zx(normed_others, k, n_send, n_recv).wait_recv()
+    to_twin(normed_others, 1, 2).start()
+
+    for store in (hidden_store, grad_attn_store, projected_store, mixed_store):
+        store.wait()
+    mixed_copy.wait()
+    for copy in far_copies() + [projected_copy(0), projected_copy(1)]:
+        copy.wait()
+    for k in range(CHUNKS):
+        hidden_copy(k).wait_send()
+        from_x(cot_half_ref, cot_others, k, cot_send, cot_recv).wait_send()
+        from_x(normed_sent, normed_others, k, n_send, n_recv).wait_send()
+        from_zx(cot_others, k, cot_send, cot_recv).wait_send()
+        from_zx(normed_others, k, n_send, n_recv).wait_send()
+        remote(
+            normed_sent.at[rows(k)], normed_twin.at[rows(k)],
+            n_send.at[3, k], n_recv.at[3, k], twin_id,
+        ).wait_send()
+    loop(tiles, lambda j: y_copy(1, column_window(j), j).wait_send())
+    loop(tiles, lambda j: core_copy(2, column_window(j), j).wait_send())
+    for slot in range(3):
+        to_twin(cot_others, 0, slot).wait()
+        to_twin(normed_others, 1, slot).wait()
+
+
+def middle(
+    heads, w_out, tokens, cotangent, cotangent_half, gain, w_gate, w_up, w_down,
+    query, keys, values, log_total, segment, cosine, sine,
+):
+    row_count, width = tokens.shape
+    half = row_count // 2
+    hidden_units = w_gate.shape[1]
+    tiles = width // TILE
+    hbm = pl.BlockSpec(memory_space=pl.ANY)
+    vmem = pl.BlockSpec(memory_space=pltpu.VMEM)
+    wide = jax.ShapeDtypeStruct((half, width), F32)
+    units = jax.ShapeDtypeStruct((row_count, hidden_units), BF16)
+    dma = pltpu.SemaphoreType.DMA
+    return pl.pallas_call(
+        middle_kernel,
+        out_shape=(
+            wide,
+            jax.ShapeDtypeStruct((row_count, width), BF16),
+            jax.ShapeDtypeStruct((row_count, 768), BF16),
+            jax.ShapeDtypeStruct((2, half, width // 2), F32),
+            wide,
+            wide, wide,
+            jax.ShapeDtypeStruct((row_count, width), BF16),
+            units, units, units,
+            jax.ShapeDtypeStruct((1, width), F32),
+            jax.ShapeDtypeStruct((6, half, width), F32),
+            jax.ShapeDtypeStruct((6, half, width), F32),
+        ),
+        in_specs=[hbm, hbm, hbm, hbm, hbm, vmem, hbm, hbm, hbm, hbm, hbm, hbm] + [vmem] * 5,
+        out_specs=(hbm,) * 11 + (vmem,) + (hbm,) * 2,
+        scratch_shapes=[
+            pltpu.VMEM(w_gate.shape, BF16),
+            pltpu.VMEM(w_up.shape, BF16),
+            pltpu.VMEM(w_down.shape, BF16),
+            pltpu.VMEM((row_count, width), BF16),
+            pltpu.VMEM((half, width), F32),
+            pltpu.VMEM((row_count, width), BF16),
+            pltpu.VMEM((half, width), F32),
+            pltpu.VMEM((half, width), F32),
+            pltpu.VMEM((row_count, hidden_units), BF16),
+            pltpu.VMEM((row_count, hidden_units), BF16),
+            pltpu.VMEM((row_count, hidden_units), BF16),
+            pltpu.VMEM((half, width), F32),
+            pltpu.VMEM((2, half, width), F32),
+            pltpu.VMEM((3, half, width), F32),
+            pltpu.VMEM((2, half, width), F32),
+            dma((13,)),
+            dma((3, tiles)), dma((3, tiles)), dma((3, tiles)), dma((3, tiles)),
+            dma((3, CHUNKS)), dma((3, CHUNKS)),
+            dma((4, CHUNKS)), dma((4, CHUNKS)),
+            dma((2, 3)), dma((2, 3)),
+            dma((2,)), dma((2,)),
+            dma((CHUNKS,)), dma((CHUNKS,)),
+            dma((6,)), dma((6,)),
+        ],
+        compiler_params=pltpu.CompilerParams(
+            collective_id=0, has_side_effects=True, vmem_limit_bytes=64 * 1024 * 1024
+        ),
+        name="feed_forward",
+    )(
+        heads, w_out, tokens, cotangent, cotangent_half, gain.reshape(1, width),
+        w_gate, w_up, w_down, query, keys, values, log_total,
+        segment.reshape(row_count, 1), segment.reshape(1, row_count), cosine, sine,
+    )
 
 
 def body(
@@ -152,14 +775,6 @@
     shared_bits = [bit for bit in (4, 1) if bit < groups]
     split_bits = [bit for bit in all_bits if bit not in shared_bits]
 
-    def gathered(half):
-        parts = [half]
-        for bit in shared_bits:
-            parts = parts + [swap(part, "dp", bit) for part in parts]
-        others = parts[1:]
-        twins = [swap(part, "tensor", 1) for part in others]
-        return jnp.concatenate([narrowed(part) for part in others + twins], axis=0)
-
     def blocks(matrix, offsets):
         width = matrix.shape[1] // groups
         return [
@@ -196,9 +811,6 @@
     group_size = query_heads // kv_heads
     query_width, kv_width = w_query.shape[1], key_weight.shape[1]
 
-    cotangent_half = half_of(cotangent, core).astype(F32)
-    cotangent_others = gathered(cotangent_half)
-
     scale_one = lax.rsqrt(jnp.mean(inputs * inputs, axis=-1, keepdims=True) + EPSILON)
     normed_one = (inputs * scale_one * attn_gain).astype(BF16)
     cosine_lookup, sine_lookup = tables(positions.reshape(row_count))
@@ -227,13 +839,55 @@
     head_outputs = combined_heads.reshape(row_count, query_width).astype(BF16)
 
     inputs_half = half_of(inputs, core)
-    hidden = inputs_half + tensor_sum_half(product(head_outputs, w_out), core)
-    scale_two = lax.rsqrt(jnp.mean(hidden * hidden, axis=-1, keepdims=True) + EPSILON)
-    normed_half = (hidden * scale_two * mlp_gain).astype(BF16)
-    normed_sent = normed_half.astype(F32)
-    normed_twin = narrowed(swap(normed_sent, "tensor", 1))
-    normed_two = joined(normed_half, normed_twin, core)
-    normed_others = gathered(normed_sent)
+    cotangent_half = half_of(cotangent, core).astype(F32)
+    def padded(heads):
+        zeros = jnp.zeros((row_count, HEAD_SIZE), BF16)
+        parts = []
+        for h in range(kv_heads):
+            parts += [heads[0, :, h], zeros, zeros, heads[0, :, h]]
+        return jnp.concatenate(parts, axis=1)
+
+    z_low = (place // 2) % 2
+
+    def near(matrix, which):
+        parts = matrix.reshape(matrix.shape[0], 2, 2, -1)
+        return lax.dynamic_index_in_dim(parts, which, 2, False).reshape(matrix.shape[0], -1)
+
+    heads_far = narrowed(swap(head_outputs.astype(F32), "dp", 2))
+    normed_one_far = narrowed(swap(near(normed_one, 1 - z_low).astype(F32), "dp", 2))
+    lanes = jnp.arange(128) % HEAD_SIZE
+    cosine_tile = jnp.concatenate([cosine_lookup[:, 0], cosine_lookup[:, 0]], axis=1)
+    sine_tile = jnp.concatenate([sine_lookup[:, 0], sine_lookup[:, 0]], axis=1)
+    sine_tile = jnp.where(lanes < HEAD_SIZE // 2, sine_tile, -sine_tile)
+    (
+        grad_hidden,
+        grad_attn,
+        projected,
+        grad_attn_far,
+        projected_far,
+        mixed_half,
+        mixed_twin,
+        normed_two,
+        activation,
+        grad_gate_in,
+        grad_up_in,
+        gain_two_half,
+        cotangent_others,
+        normed_others,
+    ) = middle(
+        head_outputs, w_out, tokens, cotangent, cotangent_half, mlp_gain, w_gate, w_up, w_down,
+        query_rotated.reshape(row_count, query_width), padded(key_rotated),
+        padded(value_projected), log_totals.reshape(query_heads, row_count), segments,
+        cosine_tile, sine_tile,
+    )
+    gain_two_half = gain_two_half[0]
+    mixed = joined(mixed_half, mixed_twin, core).astype(BF16)
+    cotangent_others = cotangent_others.reshape(-1, width).astype(BF16)
+    normed_others = normed_others.reshape(-1, width).astype(BF16)
+    grad_attn_far = joined(grad_attn_far[0], grad_attn_far[1], core).astype(BF16)
+    projected_far = jnp.concatenate(
+        [projected_far[:, :768], projected_far[:, 1024:1792]], axis=0
+    ).astype(BF16)
 
     def feed_forward(normed, incoming):
         gate_proj = product(normed, w_gate)
@@ -248,53 +902,8 @@
         grad_up_in = (grad_activation * swish_gate).astype(BF16)
         return activation, grad_gate_in, grad_up_in
 
-    activation, grad_gate_in, grad_up_in = feed_forward(normed_two, cotangent)
-    grad_normed_two = tensor_sum_half(
-        against(grad_gate_in, w_gate) + against(grad_up_in, w_up), core
-    )
-    mixed_half = hidden + tensor_sum_half(product(activation, w_down), core)
-    mixed = joined(mixed_half.astype(BF16), narrowed(swap(mixed_half, "tensor", 1)), core)
-
-    weighted = grad_normed_two * mlp_gain
-    inner_mean = jnp.mean(weighted * hidden, axis=-1, keepdims=True)
-    back_two = scale_two * weighted - hidden * (scale_two * scale_two * scale_two) * inner_mean
-    gain_two_half = jnp.sum(grad_normed_two * hidden * scale_two, axis=0)
-    grad_hidden = cotangent_half + back_two
-    attn_half = grad_hidden.astype(BF16)
-    attn_twin = narrowed(swap(grad_hidden, "tensor", 1))
-    grad_attn = joined(attn_half, attn_twin, core)
-
-    grad_heads = (
-        against(grad_attn, w_out)
-        .astype(BF16)
-        .reshape(seq_count, seq_len, kv_heads, group_size, HEAD_SIZE)
-    )
-    grad_query_rot, grad_key_rot, grad_value_rot = per_sequence(
-        attend_backward,
-        query_rotated,
-        key_rotated,
-        value_projected,
-        segments,
-        log_totals,
-        grad_heads,
-    )
-    grad_query_in = (
-        unrotate(
-            grad_query_rot.reshape(row_count, query_heads, HEAD_SIZE), cosine_lookup, sine_lookup
-        )
-        .reshape(row_count, query_width)
-        .astype(BF16)
-    )
-    grad_key_in = (
-        unrotate(grad_key_rot.reshape(row_count, kv_heads, HEAD_SIZE), cosine_lookup, sine_lookup)
-        .reshape(row_count, kv_width)
-        .astype(BF16)
-    )
-    grad_value_in = grad_value_rot.reshape(row_count, kv_width).astype(BF16)
-    partial_one = (
-        against(grad_query_in, w_query)
-        + against(grad_key_in, key_weight)
-        + against(grad_value_in, value_weight)
+    partial_one = against(
+        projected, jnp.concatenate([w_query, key_weight, value_weight], axis=1)
     )
     grad_normed_one = tensor_sum_half(partial_one, core)
     scale_one = half_of(scale_one, core)
@@ -331,13 +940,25 @@
     grad_w_gate = rows_of(normed_two, normed_others, grad_gate_in, grad_gate_o)
     grad_w_up = rows_of(normed_two, normed_others, grad_up_in, grad_up_o)
 
-    grad_w_out = reduced(
-        lambda offsets: [over_rows(head_outputs, b) for b in blocks(grad_attn, offsets)], all_bits
-    )
-    projected = jnp.concatenate([grad_query_in, grad_key_in, grad_value_in], axis=1)
-    grad_w_proj = reduced(
-        lambda offsets: [over_rows(b, projected) for b in blocks(normed_one, offsets)], all_bits
-    )
+    out_part = over_rows(head_outputs, near(grad_attn, z_low)) + over_rows(
+        heads_far, grad_attn_far
+    )
+    proj_part = over_rows(near(normed_one, z_low), projected) + over_rows(
+        normed_one_far, projected_far
+    )
+    x_low, z_high = place % 2, place // 4
+    width_out = width // groups
+
+    def reduced_far(parts):
+        column = lambda which: lax.dynamic_index_in_dim(parts, which, 1, False)
+        parts = column(x_low) + swap(column(1 - x_low), "dp", 1)
+        piece = lambda which: lax.dynamic_index_in_dim(parts, which, 0, False)
+        return piece(z_high) + swap(piece(1 - z_high), "dp", 4)
+
+    grad_w_out = reduced_far(
+        out_part.reshape(query_width, 2, 2, width_out).transpose(1, 2, 0, 3)
+    )
+    grad_w_proj = reduced_far(proj_part.reshape(2, 2, width_out, -1))
     grad_w_query = grad_w_proj[:, :query_width]
     grad_w_key = grad_w_proj[:, query_width : query_width + kv_width]
     grad_w_value = grad_w_proj[:, query_width + kv_width :]
@@ -361,6 +982,237 @@
     )
 
 
+def general_body(
+    tokens,
+    segments,
+    positions,
+    attn_gain,
+    w_query,
+    key_weight,
+    value_weight,
+    w_out,
+    mlp_gain,
+    w_gate,
+    w_up,
+    w_down,
+    cotangent,
+):
+    groups = lax.axis_size("dp")
+    place = lax.axis_index("dp")
+    core = lax.axis_index("tensor") % 2
+    all_bits = [1 << i for i in range(groups.bit_length() - 1)]
+    shared_bits = [bit for bit in (4, 1) if bit < groups]
+    split_bits = [bit for bit in all_bits if bit not in shared_bits]
+
+    def gathered(half):
+        parts = [half]
+        for bit in shared_bits:
+            parts = parts + [swap(part, "dp", bit) for part in parts]
+        others = parts[1:]
+        twins = [swap(part, "tensor", 1) for part in others]
+        return jnp.concatenate([narrowed(part) for part in others + twins], axis=0)
+
+    def blocks(matrix, offsets):
+        width = matrix.shape[1] // groups
+        return [
+            lax.dynamic_slice_in_dim(matrix, (place ^ offset) * width, width, 1)
+            for offset in offsets
+        ]
+
+    def offsets_of(bits):
+        found = [0]
+        for bit in bits:
+            found = found + [offset + bit for offset in found]
+        return found
+
+    def reduced(matrix_of, bits):
+        sent = None
+        for bit in bits:
+            rest = bits[bits.index(bit) + 1 :]
+            offsets = offsets_of(rest)
+            if sent is None:
+                away = matrix_of([offset ^ bit for offset in offsets])
+                home = matrix_of(offsets)
+            else:
+                away = [sent[offset ^ bit] for offset in offsets]
+                home = [sent[offset] for offset in offsets]
+            came = swap(away, "dp", bit)
+            sent = {offset: h + c for offset, h, c in zip(offsets, home, came)}
+        return sent[0]
+
+    inputs = tokens.astype(F32)
+    row_count, width = inputs.shape
+    seq_count, seq_len = segments.shape
+    query_heads = w_query.shape[1] // HEAD_SIZE
+    kv_heads = key_weight.shape[1] // HEAD_SIZE
+    group_size = query_heads // kv_heads
+    query_width, kv_width = w_query.shape[1], key_weight.shape[1]
+
+    cotangent_half = half_of(cotangent, core).astype(F32)
+    cotangent_others = gathered(cotangent_half)
+
+    scale_one = lax.rsqrt(jnp.mean(inputs * inputs, axis=-1, keepdims=True) + EPSILON)
+    normed_one = (inputs * scale_one * attn_gain).astype(BF16)
+    cosine_lookup, sine_lookup = tables(positions.reshape(row_count))
+    cosine_lookup = cosine_lookup[:, None, :]
+    sine_lookup = sine_lookup[:, None, :]
+    query_projected = product(normed_one, w_query).reshape(row_count, query_heads, HEAD_SIZE)
+    key_projected = product(normed_one, key_weight).reshape(row_count, kv_heads, HEAD_SIZE)
+    query_rotated = (
+        apply_rotary(query_projected, cosine_lookup, sine_lookup)
+        .astype(BF16)
+        .reshape(seq_count, seq_len, kv_heads, group_size, HEAD_SIZE)
+    )
+    key_rotated = (
+        apply_rotary(key_projected, cosine_lookup, sine_lookup)
+        .astype(BF16)
+        .reshape(seq_count, seq_len, kv_heads, HEAD_SIZE)
+    )
+    value_projected = (
+        product(normed_one, value_weight)
+        .astype(BF16)
+        .reshape(seq_count, seq_len, kv_heads, HEAD_SIZE)
+    )
+    combined_heads, log_totals = per_sequence(
+        attend_forward, query_rotated, key_rotated, value_projected, segments
+    )
+    head_outputs = combined_heads.reshape(row_count, query_width).astype(BF16)
+
+    inputs_half = half_of(inputs, core)
+    hidden = inputs_half + tensor_sum_half(product(head_outputs, w_out), core)
+    scale_two = lax.rsqrt(jnp.mean(hidden * hidden, axis=-1, keepdims=True) + EPSILON)
+    normed_half = (hidden * scale_two * mlp_gain).astype(BF16)
+    normed_sent = normed_half.astype(F32)
+    normed_twin = narrowed(swap(normed_sent, "tensor", 1))
+    normed_two = joined(normed_half, normed_twin, core)
+    normed_others = gathered(normed_sent)
+
+    def feed_forward(normed, incoming):
+        gate_proj = product(normed, w_gate)
+        up_proj = product(normed, w_up)
+        grad_activation = against(incoming, w_down)
+        sigmoid_gate = jax.nn.sigmoid(gate_proj)
+        swish_gate = gate_proj * sigmoid_gate
+        activation = (swish_gate * up_proj).astype(BF16)
+        grad_gate_in = (
+            grad_activation * up_proj * sigmoid_gate * (1.0 + gate_proj * (1.0 - sigmoid_gate))
+        ).astype(BF16)
+        grad_up_in = (grad_activation * swish_gate).astype(BF16)
+        return activation, grad_gate_in, grad_up_in
+
+    activation, grad_gate_in, grad_up_in = feed_forward(normed_two, cotangent)
+    grad_normed_two = tensor_sum_half(
+        against(grad_gate_in, w_gate) + against(grad_up_in, w_up), core
+    )
+    mixed_half = hidden + tensor_sum_half(product(activation, w_down), core)
+    mixed = joined(mixed_half.astype(BF16), narrowed(swap(mixed_half, "tensor", 1)), core)
+
+    weighted = grad_normed_two * mlp_gain
+    inner_mean = jnp.mean(weighted * hidden, axis=-1, keepdims=True)
+    back_two = scale_two * weighted - hidden * (scale_two * scale_two * scale_two) * inner_mean
+    gain_two_half = jnp.sum(grad_normed_two * hidden * scale_two, axis=0)
+    grad_hidden = cotangent_half + back_two
+    attn_half = grad_hidden.astype(BF16)
+    attn_twin = narrowed(swap(grad_hidden, "tensor", 1))
+    grad_attn = joined(attn_half, attn_twin, core)
+
+    grad_heads = (
+        against(grad_attn, w_out)
+        .astype(BF16)
+        .reshape(seq_count, seq_len, kv_heads, group_size, HEAD_SIZE)
+    )
+    grad_query_rot, grad_key_rot, grad_value_rot = per_sequence(
+        attend_backward,
+        query_rotated,
+        key_rotated,
+        value_projected,
+        segments,
+        log_totals,
+        grad_heads,
+    )
+    grad_query_in = (
+        unrotate(
+            grad_query_rot.reshape(row_count, query_heads, HEAD_SIZE), cosine_lookup, sine_lookup
+        )
+        .reshape(row_count, query_width)
+        .astype(BF16)
+    )
+    grad_key_in = (
+        unrotate(grad_key_rot.reshape(row_count, kv_heads, HEAD_SIZE), cosine_lookup, sine_lookup)
+        .reshape(row_count, kv_width)
+        .astype(BF16)
+    )
+    grad_value_in = grad_value_rot.reshape(row_count, kv_width).astype(BF16)
+    partial_one = (
+        against(grad_query_in, w_query)
+        + against(grad_key_in, key_weight)
+        + against(grad_value_in, value_weight)
+    )
+    grad_normed_one = tensor_sum_half(partial_one, core)
+    scale_one = half_of(scale_one, core)
+    weighted = grad_normed_one * attn_gain
+    inner_mean = jnp.mean(weighted * inputs_half, axis=-1, keepdims=True)
+    back_one = scale_one * weighted - inputs_half * (scale_one * scale_one * scale_one) * inner_mean
+    gain_one_half = jnp.sum(grad_normed_one * inputs_half * scale_one, axis=0)
+    input_half = grad_hidden + back_one
+    grad_input = joined(input_half, swap(input_half, "tensor", 1), core)
+
+    activation_o, grad_gate_o, grad_up_o = feed_forward(normed_others, cotangent_others)
+
+    def rows_of(left, left_others, right, right_others):
+        def term(offsets):
+            ours = blocks(left, offsets)
+            theirs = blocks(left_others, offsets)
+            return [
+                over_rows(a, right) + over_rows(b, right_others) for a, b in zip(ours, theirs)
+            ]
+
+        return reduced(term, split_bits)
+
+    def columns_of(left, left_others, right, right_others):
+        def term(offsets):
+            ours = blocks(right, offsets)
+            theirs = blocks(right_others, offsets)
+            return [
+                over_rows(left, a) + over_rows(left_others, b) for a, b in zip(ours, theirs)
+            ]
+
+        return reduced(term, split_bits)
+
+    grad_w_down = columns_of(activation, activation_o, cotangent, cotangent_others)
+    grad_w_gate = rows_of(normed_two, normed_others, grad_gate_in, grad_gate_o)
+    grad_w_up = rows_of(normed_two, normed_others, grad_up_in, grad_up_o)
+
+    grad_w_out = reduced(
+        lambda offsets: [over_rows(head_outputs, b) for b in blocks(grad_attn, offsets)], all_bits
+    )
+    projected = jnp.concatenate([grad_query_in, grad_key_in, grad_value_in], axis=1)
+    grad_w_proj = reduced(
+        lambda offsets: [over_rows(b, projected) for b in blocks(normed_one, offsets)], all_bits
+    )
+    grad_w_query = grad_w_proj[:, :query_width]
+    grad_w_key = grad_w_proj[:, query_width : query_width + kv_width]
+    grad_w_value = grad_w_proj[:, query_width + kv_width :]
+
+    gains = jnp.stack([gain_one_half, gain_two_half])
+    gains = gains + swap(gains, "tensor", 1)
+    gains = reduced(lambda offsets: blocks(gains, offsets), all_bits)
+    grad_attn_gain, grad_mlp_gain = gains[0], gains[1]
+    return (
+        mixed,
+        grad_input,
+        grad_attn_gain,
+        grad_w_query,
+        grad_w_key,
+        grad_w_value,
+        grad_w_out,
+        grad_mlp_gain,
+        grad_w_gate,
+        grad_w_up,
+        grad_w_down,
+    )
+
+
 def solution(mesh):
     placed = (
         P("dp", None),
@@ -377,8 +1229,9 @@
         P("tensor", None),
         P("dp", None),
     )
+    fits = mesh.shape["dp"] == 8 and mesh.shape["tensor"] == 4
     return jax.shard_map(
-        body,
+        body if fits else general_body,
         mesh=mesh,
         in_specs=placed,
         out_specs=(

time: 705 us -> 623 us (0.88)
  waiting for transfers between devices: 337 us -> 76.3 us
  Pallas kernels: 0 us -> 247 us
  matrix products: 224 us -> 139 us
  local copies, waits for them, and re-layouts: 15.7 us -> 59.1 us
  starting transfers between devices: 47.7 us -> 28.9 us
  other arithmetic: 69.4 us -> 60 us
    ppermute x49 -> x20, waiting for transfers between devices: 337 us -> 76.3 us  [swap(): return lax.ppermute(value, axis, [(i, i ^ bit) for i in range(size)])]
    pallas_call x0 -> x1, Pallas kernels: none -> 247 us  [middle(): pl.pallas_call(middle_kernel, out_shape=(wide, jax.ShapeDtypeStruct((row_...]
    dot_general x4 -> x0, matrix products: 36.3 us -> none  [the longest x1 14.4 us: attend_backward(): jnp.einsum('ojus,sov->uojv', grad_raw, key_rotated, preferred_element_typ...]
    dot_general x8 -> x2, matrix products: 53.5 us -> 25.3 us  [against(): lax.dot_general(gradient, weight, (((1,), (1,)), ((), ())), preferred_ele...]
    dot_general x9 -> x5, matrix products: 78.3 us -> 51.4 us  [product(): return jnp.dot(left_matrix, right_matrix, preferred_element_type=F32)]
    convert_element_type x3 -> x4, other arithmetic: 3.66 us -> 24.4 us  [the longest x1 10.5 us: body(): cotangent_others = cotangent_others.reshape(-1, width).astype(BF16)]
    unnamed x16 -> x2, other arithmetic: 20.4 us -> 0.01 us
    ppermute x49 -> x20, starting transfers between devices: 47.7 us -> 28.9 us  [swap(): return lax.ppermute(value, axis, [(i, i ^ bit) for i in range(size)])]
  transfers between devices with their start and end apart: 49 -> 20, of which waited for: 18 -> 5; matrix products, arithmetic and copies ran while one was open for 39% -> 38% of each run, Pallas kernels for 0% -> 40%
where the time goes in v2:
time: 623 us; the launch traced here: 612 us
  Pallas kernels  247 us (40%)
  matrix products  139 us (22%)
  waiting for transfers between devices  76.3 us (12%)
  other arithmetic  60 us (10%)
  local copies, waits for them, and re-layouts  59.1 us (9%)
  starting transfers between devices  28.9 us (5%)
    pallas_call x1, Pallas kernels, middle(): pl.pallas_call(middle_kernel, out_shape=(wide, jax.ShapeDtypeStruct((row_...  247 us
    ppermute x20, waiting for transfers between devices, swap(): return lax.ppermute(value, axis, [(i, i ^ bit) for i in range(size)])  76.3 us
    dot_general x16, matrix products, over_rows(): lax.dot_general(left_matrix, right_matrix, (((0,), (0,)), ((), ())), pref...  58.6 us
    dot_general x5, matrix products, product(): return jnp.dot(left_matrix, right_matrix, preferred_element_type=F32)  51.4 us
    ppermute x20, starting transfers between devices, swap(): return lax.ppermute(value, axis, [(i, i ^ bit) for i in range(size)])  28.9 us
    dot_general x2, matrix products, against(): lax.dot_general(gradient, weight, (((1,), (1,)), ((), ())), preferred_ele...  25.3 us
    unnamed x137, local copies, waits for them, and re-layouts  19.3 us
  transfers between devices with their start and end apart: 20, of which 5 were waited for; matrix products, arithmetic and copies ran while one was open for 38% of the time, Pallas kernels for 40%

profile of v2, /device:TPU:0, one launch (start us, length us, event | category | flops | bytes accessed | tf_op | source)
XLA Modules:
  0.0 612.2 jit_solution(18404133955556210061)
XLA Ops:
  8.7 7.2 %convert_reduce_fusion = f32[512,2,512]{2,1,0:T(2,128)S(1)} fusion(bf16[512,2,2,512]{3,2,1,0:T(2,128)(2,1)S(1)} %reshape.193, s32[]{:T(128)S(6)} %select_n.177), kind=kLoop, calls=%fused_computation.33 | loop fusion | flops 524288 | bytes 3145732 | tf_op jit(solution)/shard_map/convert_element_type | solution.py:857
  63.9 246.9 %feed_forward.1 = (f32[256,2048]{1,0:T(8,128)}, bf16[512,2048]{1,0:T(8,128)(2,1)}, bf16[512,768]{1,0:T(8,128)(2,1)}, f32[2,256,1024]{2,1,0:T(8,128)}, f32[256,20...) custom-call(bf16[512,512]{1,0:T(8,128)(2,1)} %copy.71.heads_ref, ...), custom_call_target="tpu_custom_call" | custom-call | tf_op jit(solution)/shard_map/feed_forward/pallas_call | solution.py:703
  310.8 6.0 fusion.4
  320.0 5.6 convert_element_type.117
  325.6 10.5 %convert_element_type.119 = bf16[6,256,2048]{2,1,0:T(8,128)(2,1)} convert(f32[6,256,2048]{2,1,0:T(8,128)} %get-tuple-element.36) | non-fusion elementwise | flops 3145728 | bytes 18874368 | tf_op jit(solution)/shard_map/convert_element_type | solution.py:885
  336.1 19.3 %fusion.99 = f32[1536,2048]{1,0:T(8,128)} fusion(bf16[1536,2048]{1,0:T(8,128)(2,1)} %bitcast.136, bf16[2048,2048]{1,0:T(8,128)(2,1)} %w_down_ref.1), kind=kOutput, calls=%fused_computation.177 | convolution fusion | flops 12884901888 | bytes 27262976 | tf_op jit(solution)/shard_map/dot_general | solution.py:28
  355.4 17.1 %fusion.100 = f32[1536,2048]{1,0:T(8,128)} fusion(bf16[1536,2048]{1,0:T(8,128)(2,1)S(1)} %bitcast.124, bf16[2048,2048]{1,0:T(8,128)(2,1)} %w_gate_ref.1), kind=kOutput, calls=%fused_computation.178 | convolution fusion | flops 12884901888 | bytes 27262976 | tf_op jit(solution)/shard_map/dot_general | solution.py:18
  372.5 27.6 %multiply_convert_fusion = (bf16[1536,2048]{1,0:T(8,128)(2,1)}, bf16[1536,2048]{1,0:T(8,128)(2,1)}, bf16[1536,2048]{1,0:T(8,128)(2,1)S(1)}) fusion(f32[1536,2048]{1,0:T(8,128)} %fusion.100, f32[1536,2048]{1,0:T(8,128)} %fusion.99, bf16[1536,2048]{1,0:T(8,128)(2,1)} %bitcast.125, bf16[2048,2048]{1,0:T(8,128)(2,1)} %w_up_ref.1), kind=kOutput, calls=%fused_computation | convolution fusion | flops 12932087808 | bytes 58720256 | tf_op jit(solution)/shard_map/dot_general | solution.py:18
  400.1 3.7 fusion.32
  416.1 6.4 %fusion.38 = f32[256,2048]{1,0:T(8,128)} fusion(bf16[1536,2048]{1,0:T(8,128)(2,1)} %get-tuple-element.42, bf16[1536,2048]{1,0:T(8,128)(2,1)} %bitcast.128, s32[]{:T(128)S(6)} %select_n.166), kind=kOutput, calls=%fused_computation.82 | convolution fusion | flops 1610612736 | bytes 9175044 | tf_op jit(solution)/shard_map/dot_general | solution.py:22
  422.5 4.2 fusion.36
  426.8 3.8 constant_dynamic-slice_fusion.4
  439.1 3.5 constant_dynamic-slice_fusion.3
  442.6 6.0 copy.89
  453.5 5.1 fusion.28
  463.9 4.6 fusion.30
  490.1 14.7 %collective-permute-done.15 = f32[2,512,256]{2,0,1:T(2,128)} collective-permute-done((f32[2,512,256]{2,0,1:T(2,128)}, f32[2,512,256]{2,0,1:T(2,128)}, u32[]{:S(2)}, u32[]{:S(2)}) %collective-permute-start.15) | collective-permute-done | bytes 1048608 | tf_op jit(solution)/shard_map/ppermute | solution.py:39
  509.2 4.0 collective-permute-start.16
  517.8 4.0 fusion.11
  521.8 4.0 fusion.12
  525.7 31.7 %collective-permute-done.19 = f32[2048,256]{1,0:T(8,128)S(1)} collective-permute-done((f32[2048,256]{1,0:T(8,128)}, f32[2048,256]{1,0:T(8,128)S(1)}, u32[]{:S(2)}, u32[]{:S(2)}) %collective-permute-start.19) | collective-permute-done | bytes 2097184 | tf_op jit(solution)/shard_map/ppermute | solution.py:39
  568.2 5.3 collective-permute-start.13
  578.0 11.3 %collective-permute-done.6 = f32[2,256]{1,0:T(2,128)S(1)} collective-permute-done((f32[2,256]{1,0:T(2,128)S(1)}, f32[2,256]{1,0:T(2,128)S(1)}, u32[]{:S(2)}, u32[]{:S(2)}) %collective-permute-start.6) | collective-permute-done | bytes 2080 | tf_op jit(solution)/shard_map/ppermute | solution.py:39
  589.4 17.3 %collective-permute-done.10 = f32[2,256]{1,0:T(2,128)S(1)} collective-permute-done((f32[2,256]{1,0:T(2,128)S(1)}, f32[2,256]{1,0:T(2,128)S(1)}, u32[]{:S(2)}, u32[]{:S(2)}) %collective-permute-start.10) | collective-permute-done | bytes 2080 | tf_op jit(solution)/shard_map/ppermute | solution.py:39
  (258 shorter events, 141.0 us)
Async XLA Ops:
  17.6 491.6 %collective-permute-start.11 = (f32[512,1024]{1,0:T(8,128)}, f32[512,1024]{1,0:T(8,128)}, u32[]{:S(2)}, u32[]{:S(2)}) collective-permute-start(f32[512,1024]{1,0:T(8,128)} %bitcast.55), channel_id=1, source_target_pairs={{0,8},{4,12},{8,0},{12,4},{16,24},{20,28},{24,16},{28,20},{1,9},{5... | collective-permute-start | bytes 6291464 | tf_op jit(solution)/shard_map/ppermute | solution.py:39
  42.7 426.6 %collective-permute-start.14 = (f32[512,512]{0,1:T(8,128)}, f32[512,512]{0,1:T(8,128)}, u32[]{:S(2)}, u32[]{:S(2)}) collective-permute-start(f32[512,512]{0,1:T(8,128)} %bitcast_convert_fusion), channel_id=1, source_target_pairs={{0,8},{4,12},{8,0},{12,4},{16,24},{20,28},{24,16},{28,20},{1,9},{5... | collective-permute-start | bytes 3145736 | tf_op jit(solution)/shard_map/ppermute | solution.py:39
  319.9 165.7 %collective-permute-start = (f32[256,2048]{1,0:T(8,128)}, f32[256,2048]{1,0:T(8,128)}, u32[]{:S(2)}, u32[]{:S(2)}) collective-permute-start(f32[256,2048]{1,0:T(8,128)} %constant_dynamic-slice_fusion.13), channel_id=1, source_target_pairs={{0,1},{1,0},{2,3},{3,2},{4,5},{5,4},{6,7},{7,6},{8,9},{9,8},{10,11... | collective-permute-start | bytes 6291464 | tf_op jit(solution)/shard_map/ppermute | solution.py:39
  407.3 108.9 %collective-permute-start.18 = (f32[256,2048]{1,0:T(8,128)}, f32[256,2048]{1,0:T(8,128)}, u32[]{:S(2)}, u32[]{:S(2)}) collective-permute-start(f32[256,2048]{1,0:T(8,128)} %convolution_add_fusion.2), channel_id=1, source_target_pairs={{0,8},{4,12},{8,0},{12,4},{16,24},{20,28},{24,16},{28,20},{1,9},{5... | collective-permute-start | bytes 6291464 | tf_op jit(solution)/shard_map/ppermute | solution.py:39
  416.1 105.7 %collective-permute-start.17 = (f32[256,2048]{1,0:T(8,128)}, f32[256,2048]{1,0:T(8,128)}, u32[]{:S(2)}, u32[]{:S(2)}) collective-permute-start(f32[256,2048]{1,0:T(8,128)} %convolution_add_fusion.4), channel_id=1, source_target_pairs={{0,8},{4,12},{8,0},{12,4},{16,24},{20,28},{24,16},{28,20},{1,9},{5... | collective-permute-start | bytes 6291464 | tf_op jit(solution)/shard_map/ppermute | solution.py:39
  479.2 25.6 %collective-permute-start.15 = (f32[2,512,256]{2,0,1:T(2,128)}, f32[2,512,256]{2,0,1:T(2,128)}, u32[]{:S(2)}, u32[]{:S(2)}) collective-permute-start(f32[2,512,256]{2,0,1:T(2,128)} %bitcast.117), channel_id=1, source_target_pairs={{0,4},{4,0},{8,12},{12,8},{16,20},{20,16},{24,28},{28,24},{1,5},{5... | collective-permute-start | bytes 3145736 | tf_op jit(solution)/shard_map/ppermute | solution.py:39
  485.6 71.8 %collective-permute-start.19 = (f32[2048,256]{1,0:T(8,128)}, f32[2048,256]{1,0:T(8,128)S(1)}, u32[]{:S(2)}, u32[]{:S(2)}) collective-permute-start(f32[2048,256]{1,0:T(8,128)} %convolution_add_fusion), channel_id=1, source_target_pairs={{0,8},{4,12},{8,0},{12,4},{16,24},{20,28},{24,16},{28,20},{1,9},{5... | collective-permute-start | bytes 6291464 | tf_op jit(solution)/shard_map/ppermute | solution.py:39
  504.8 55.8 %collective-permute-start.1 = (f32[256,2048]{1,0:T(8,128)S(1)}, f32[256,2048]{1,0:T(8,128)S(1)}, u32[]{:S(2)}, u32[]{:S(2)}) collective-permute-start(f32[256,2048]{1,0:T(8,128)S(1)} %dynamic-slice_add_fusion), channel_id=1, source_target_pairs={{0,2},{1,3},{2,0},{3,1},{4,6},{5,7},{6,4},{7,5},{8,10},{9,11},{10,... | collective-permute-start | bytes 6291464 | tf_op jit(solution)/shard_map/ppermute | solution.py:39
  509.2 64.8 %collective-permute-start.16 = (f32[512,256]{1,0:T(8,128)S(1)}, f32[512,256]{1,0:T(8,128)S(1)}, u32[]{:S(2)}, u32[]{:S(2)}) collective-permute-start(f32[512,256]{1,0:T(8,128)S(1)} %bitcast.154), channel_id=1, source_target_pairs={{0,16},{4,20},{8,24},{12,28},{16,0},{20,4},{24,8},{28,12},{1,17},{... | collective-permute-start | bytes 1572872 | tf_op jit(solution)/shard_map/ppermute | solution.py:39
  516.2 48.9 %collective-permute-start.12 = (f32[2,256,768]{2,1,0:T(8,128)S(1)}, f32[2,256,768]{2,1,0:T(8,128)S(1)}, u32[]{:S(2)}, u32[]{:S(2)}) collective-permute-start(f32[2,256,768]{2,1,0:T(8,128)S(1)} %dynamic-slice_bitcast_fusion), channel_id=1, source_target_pairs={{0,4},{4,0},{8,12},{12,8},{16,20},{20,16},{24,28},{28,24},{1,5},{5... | collective-permute-start | bytes 4718600 | tf_op jit(solution)/shard_map/ppermute | solution.py:39
  521.7 35.7 %copy-start.9 = (bf16[512,2048]{1,0:T(8,128)(2,1)S(1)}, bf16[512,2048]{1,0:T(8,128)(2,1)}, u32[]{:S(2)}) copy-start(bf16[512,2048]{1,0:T(8,128)(2,1)} %get-tuple-element.38) | copy-start | bytes 6291460
  521.7 35.7 %copy-start.37 = (f32[2048,256]{1,0:T(8,128)S(1)}, f32[2048,256]{1,0:T(8,128)}, u32[]{:S(2)}) copy-start(f32[2048,256]{1,0:T(8,128)} %fusion.30) | copy-start | bytes 6291460
  525.7 34.8 %copy-start.7 = (f32[512,2048]{1,0:T(8,128)S(1)}, f32[512,2048]{1,0:T(8,128)}, u32[]{:S(2)}) copy-start(f32[512,2048]{1,0:T(8,128)} %convert_element_type.97) | copy-start | bytes 12582916
  525.7 34.8 %copy-start.52 = (f32[2048]{0:T(1024)S(1)}, f32[2048]{0:T(1024)}, u32[]{:S(2)}) copy-start(f32[2048]{0:T(1024)} %param.16) | copy-start | bytes 24580
  561.3 1.7 collective-permute-start.3
  562.9 46.1 %collective-permute-start.2 = (f32[256,2048]{1,0:T(8,128)S(1)}, f32[256,2048]{1,0:T(8,128)S(1)}, u32[]{:S(2)}, u32[]{:S(2)}) collective-permute-start(f32[256,2048]{1,0:T(8,128)S(1)} %subtract_add_fusion), channel_id=1, source_target_pairs={{0,1},{1,0},{2,3},{3,2},{4,5},{5,4},{6,7},{7,6},{8,9},{9,8},{10,11... | collective-permute-start | bytes 6291464 | tf_op jit(solution)/shard_map/ppermute | solution.py:39
  563.0 3.8 collective-permute-start.8
  564.6 3.6 collective-permute-start.5
  565.3 8.2 %collective-permute-start.7 = (f32[2,256]{1,0:T(2,128)S(1)}, f32[2,256]{1,0:T(2,128)S(1)}, u32[]{:S(2)}, u32[]{:S(2)}) collective-permute-start(f32[2,256]{1,0:T(2,128)S(1)} %get-tuple-element.70), channel_id=1, source_target_pairs={{0,4},{4,0},{8,12},{12,8},{16,20},{20,16},{24,28},{28,24},{1,5},{5... | collective-permute-start | bytes 6152 | tf_op jit(solution)/shard_map/ppermute | solution.py:39
  568.1 5.9 collective-permute-start.9
  568.2 39.0 %collective-permute-start.13 = (f32[256,768]{1,0:T(8,128)S(1)}, f32[256,768]{1,0:T(8,128)S(1)}, u32[]{:S(2)}, u32[]{:S(2)}) collective-permute-start(f32[256,768]{1,0:T(8,128)S(1)} %dynamic-slice_bitcast_fusion.2), channel_id=1, source_target_pairs={{0,16},{4,20},{8,24},{12,28},{16,0},{20,4},{24,8},{28,12},{1,17},{... | collective-permute-start | bytes 2359304 | tf_op jit(solution)/shard_map/ppermute | solution.py:39
  573.5 4.5 collective-permute-start.4
  574.0 15.3 %collective-permute-start.6 = (f32[2,256]{1,0:T(2,128)S(1)}, f32[2,256]{1,0:T(2,128)S(1)}, u32[]{:S(2)}, u32[]{:S(2)}) collective-permute-start(f32[2,256]{1,0:T(2,128)S(1)} %get-tuple-element.72), channel_id=1, source_target_pairs={{0,8},{4,12},{8,0},{12,4},{16,24},{20,28},{24,16},{28,20},{1,9},{5... | collective-permute-start | bytes 6152 | tf_op jit(solution)/shard_map/ppermute | solution.py:39
  574.1 32.6 %collective-permute-start.10 = (f32[2,256]{1,0:T(2,128)S(1)}, f32[2,256]{1,0:T(2,128)S(1)}, u32[]{:S(2)}, u32[]{:S(2)}) collective-permute-start(f32[2,256]{1,0:T(2,128)S(1)} %fusion.78), channel_id=1, source_target_pairs={{0,16},{4,20},{8,24},{12,28},{16,0},{20,4},{24,8},{28,12},{1,17},{... | collective-permute-start | bytes 6152 | tf_op jit(solution)/shard_map/ppermute | solution.py:39
  (60 other events, 243.6 us)

commit v3 on v2

--- a/solution.py
+++ b/solution.py
@@ -14,26 +14,6 @@
 BF16 = jnp.bfloat16
 
 
-def product(left_matrix, right_matrix):
-    return jnp.dot(left_matrix, right_matrix, preferred_element_type=F32)
-
-
-def over_rows(left_matrix, right_matrix):
-    return lax.dot_general(
-        left_matrix, right_matrix, (((0,), (0,)), ((), ())), preferred_element_type=F32
-    )
-
-
-def against(gradient, weight):
-    return lax.dot_general(
-        gradient, weight, (((1,), (1,)), ((), ())), preferred_element_type=F32
-    )
-
-
-def narrowed(value):
-    return jnp.where(value == value, value, 0.0).astype(BF16)
-
-
 def swap(value, axis, bit):
     size = lax.axis_size(axis)
     return lax.ppermute(value, axis, [(i, i ^ bit) for i in range(size)])
@@ -50,90 +30,6 @@
     return jnp.concatenate([first, second], axis=0)
 
 
-def tensor_sum_half(partial, core):
-    total = half_of(partial, core) + swap(half_of(partial, 1 - core), "tensor", 1)
-    bit = 2
-    while bit < lax.axis_size("tensor"):
-        total = total + swap(total, "tensor", bit)
-        bit *= 2
-    return total
-
-
-def tables(places):
-    half_dim = HEAD_SIZE // 2
-    frequency = 500000.0 ** (-(jnp.arange(half_dim).astype(F32) * 2.0 / HEAD_SIZE))
-    angles = places.astype(F32)[..., None] * frequency
-    cosine_lookup = jnp.cos(angles)
-    sine_lookup = jnp.sin(angles)
-    return (
-        jnp.concatenate([cosine_lookup, cosine_lookup], -1),
-        jnp.concatenate([sine_lookup, sine_lookup], -1),
-    )
-
-
-def apply_rotary(field, cosine_lookup, sine_lookup):
-    half_dim = HEAD_SIZE // 2
-    turned = jnp.concatenate([-field[..., half_dim:], field[..., :half_dim]], -1)
-    return field * cosine_lookup + turned * sine_lookup
-
-
-def unrotate(gradient, cosine_lookup, sine_lookup):
-    half_dim = HEAD_SIZE // 2
-    sined = gradient * sine_lookup
-    return gradient * cosine_lookup + jnp.concatenate(
-        [sined[..., half_dim:], -sined[..., :half_dim]], -1
-    )
-
-
-def allowed_pairs(segment):
-    spots = jnp.arange(segment.shape[0])
-    return (spots[:, None] >= spots[None, :]) & (segment[:, None] == segment[None, :])
-
-
-def scores(query_rotated, key_rotated, segment):
-    raw_scores = jnp.einsum(
-        "qhgd,khd->hgqk", query_rotated, key_rotated, preferred_element_type=F32
-    ) * HEAD_SIZE ** (-0.5)
-    return jnp.where(allowed_pairs(segment), raw_scores, MASKED)
-
-
-def attend_forward(query_rotated, key_rotated, value_seq, segment):
-    masked = scores(query_rotated, key_rotated, segment)
-    row_peak = jnp.max(masked, axis=-1, keepdims=True)
-    log_total = row_peak + jnp.log(jnp.sum(jnp.exp(masked - row_peak), axis=-1, keepdims=True))
-    attention_probs = jnp.exp(masked - log_total).astype(BF16)
-    combined_heads = jnp.einsum(
-        "ojus,sov->uojv", attention_probs, value_seq, preferred_element_type=F32
-    )
-    return (combined_heads, log_total)
-
-
-def attend_backward(query_rotated, key_rotated, value_seq, segment, log_total, grad_heads):
-    masked = scores(query_rotated, key_rotated, segment)
-    attention_probs = jnp.exp(masked - log_total)
-    grad_probs = jnp.einsum("qhgd,khd->hgqk", grad_heads, value_seq, preferred_element_type=F32)
-    row_sum = jnp.sum(attention_probs * grad_probs, axis=-1, keepdims=True)
-    grad_raw = jnp.where(
-        allowed_pairs(segment), attention_probs * (grad_probs - row_sum), 0.0
-    ).astype(BF16)
-    factor = HEAD_SIZE ** (-0.5)
-    grad_query_rot = (
-        jnp.einsum("ojus,sov->uojv", grad_raw, key_rotated, preferred_element_type=F32) * factor
-    )
-    grad_key_rot = (
-        jnp.einsum("hgqk,qhgd->khd", grad_raw, query_rotated, preferred_element_type=F32) * factor
-    )
-    grad_value_rot = jnp.einsum(
-        "hgqk,qhgd->khd", attention_probs.astype(BF16), grad_heads, preferred_element_type=F32
-    )
-    return (grad_query_rot, grad_key_rot, grad_value_rot)
-
-
-def per_sequence(step, *fields):
-    results = [step(*[field[s] for field in fields]) for s in range(fields[0].shape[0])]
-    return [jnp.stack(parts) for parts in zip(*results)]
-
-
 MESH = pl.DeviceIdType.MESH
 CHUNKS = 4
 TILE = 256
@@ -149,23 +45,29 @@
 
 
 def middle_kernel(
-    heads_ref,
+    w_query_ref,
+    w_key_ref,
+    w_value_ref,
     w_out_ref,
     tokens_ref,
     cot_ref,
     cot_half_ref,
+    gain_one_ref,
     gain_ref,
     w_gate_ref,
     w_up_ref,
     w_down_ref,
-    query_ref,
-    keys_ref,
-    values_ref,
-    log_total_ref,
     segment_column_ref,
     segment_row_ref,
     cosine_ref,
     sine_ref,
+    normed_one_out,
+    heads_out,
+    query_ref,
+    keys_ref,
+    values_ref,
+    normed_one_far,
+    heads_far,
     grad_hidden_out,
     grad_attn_out,
     projected_out,
@@ -212,6 +114,7 @@
     hidden_recv,
     far_send,
     far_recv,
+    log_total_ref,
 ):
     dp, tensor = lax.axis_index("dp"), lax.axis_index("tensor")
     core = tensor % 2
@@ -220,13 +123,18 @@
     x_id = (flip(dp, 1), tensor)
     z_id = (flip(dp, 4), tensor)
     far_id = (flip(dp, 2), tensor)
-    heads = gg.at[:, pl.ds(0, heads_ref.shape[1])]
-    tok = gu.at[pl.ds(0, hidden.shape[0])]
     half, width = hidden.shape
     hidden_units = gate_w.shape[1]
     chunk = half // CHUNKS
     my_row = pl.multiple_of(core * half, half)
     twin_row = pl.multiple_of((1 - core) * half, half)
+    row_count = 2 * half
+    query_width = w_query_ref.shape[1]
+    tiles = width // TILE
+    transposed = (((1,), (1,)), ((), ()))
+    z_low = (dp // 2) % 2
+    heads = gg.at[:, pl.ds(0, query_width)]
+    tok = gu
 
     def remote(src, dst, send, recv, device):
         return pltpu.make_async_remote_copy(
@@ -235,15 +143,23 @@
         )
 
     loads = {
-        "heads": pltpu.make_async_copy(heads_ref, heads, local_sem.at[0]),
-        "w_out": pltpu.make_async_copy(w_out_ref, act, local_sem.at[1]),
-        "tok": pltpu.make_async_copy(tokens_ref.at[pl.ds(my_row, half)], tok, local_sem.at[2]),
-        "cot": pltpu.make_async_copy(cot_ref, cot, local_sem.at[3]),
-        "gate": pltpu.make_async_copy(w_gate_ref, gate_w, local_sem.at[4]),
+        "tok": pltpu.make_async_copy(tokens_ref, tok, local_sem.at[0]),
+        "query": pltpu.make_async_copy(
+            w_query_ref, gate_w.at[:, pl.ds(0, query_width)], local_sem.at[1]
+        ),
+        "key": pltpu.make_async_copy(
+            w_key_ref, gate_w.at[:, pl.ds(query_width, 128)], local_sem.at[2]
+        ),
+        "value": pltpu.make_async_copy(
+            w_value_ref, gate_w.at[:, pl.ds(query_width + 128, 128)], local_sem.at[3]
+        ),
+        "w_out": pltpu.make_async_copy(w_out_ref, cot, local_sem.at[4]),
         "up": pltpu.make_async_copy(w_up_ref, up_w, local_sem.at[5]),
         "down": pltpu.make_async_copy(w_down_ref, down_w, local_sem.at[6]),
+        "gate": pltpu.make_async_copy(w_gate_ref, gate_w, local_sem.at[7]),
+        "cot": pltpu.make_async_copy(cot_ref, cot, local_sem.at[8]),
     }
-    for name in loads:
+    for name in ("tok", "query", "key", "value", "w_out", "up", "down"):
         loads[name].start()
 
     barrier = pltpu.get_barrier_semaphore()
@@ -285,14 +201,140 @@
     for k in range(CHUNKS):
         from_x(cot_half_ref, cot_others, k, cot_send, cot_recv).start()
 
-    loads["heads"].wait()
+    def far_columns(b):
+        return pl.ds(pl.multiple_of(b * 1024 + (1 - z_low) * 512, 512), 512)
+
+    gain_one = gain_one_ref[...]
+    loads["tok"].wait()
+
+    def first_norm(i):
+        window = pl.ds(pl.multiple_of(i * ROWS, ROWS), ROWS)
+        values = tok[window, :].astype(F32)
+        scale = lax.rsqrt(jnp.mean(values * values, axis=-1, keepdims=True) + EPSILON)
+        normed[window, :] = (values * scale * gain_one).astype(BF16)
+
+    loop(row_count // ROWS, first_norm)
+    normed_one_store = pltpu.make_async_copy(normed, normed_one_out, local_sem.at[9])
+    normed_one_store.start()
+
+    def stage_far(i):
+        window = pl.ds(pl.multiple_of(i * ROWS, ROWS), ROWS)
+        here = pl.ds(pl.multiple_of(my_row + i * ROWS, ROWS), ROWS)
+        for b in range(2):
+            core_in[2, window, pl.ds(b * 512, 512)] = normed[here, far_columns(b)].astype(F32)
+
+    loop(half // ROWS, stage_far)
+    early = pl.ds(0, 1024)
+    normed_one_copy = remote(
+        core_in.at[2, :, early], normed_one_far.at[0], far_send.at[0], far_recv.at[0], far_id
+    )
+    normed_one_copy.start()
+
+    lane = lax.broadcasted_iota(jnp.int32, (TILE, 128), 1)
+    factor = HEAD_SIZE ** (-0.5)
+    everything = slice(None)
+
+    def turn(value):
+        return jnp.where(lane % 64 < 32, pltpu.roll(value, 96, 1), pltpu.roll(value, 32, 1))
+
+    def rotate_tile(value, window):
+        return value * cosine_ref[window, :] - turn(value) * sine_ref[window, :]
+
+    def unrotate_tile(value, window):
+        return value * cosine_ref[window, :] + turn(value) * sine_ref[window, :]
+
+    for name in ("query", "key", "value"):
+        loads[name].wait()
+    for block in range(2):
+        window = pl.ds(block * TILE, TILE)
+
+        def query_tile(j, window=window):
+            projection = jnp.dot(
+                normed[window, :],
+                gate_w[:, pl.ds(pl.multiple_of(j * TILE, TILE), TILE)],
+                preferred_element_type=F32,
+            )
+            for part in range(2):
+                act[window, pl.ds(pl.multiple_of(j * TILE + part * 128, 128), 128)] = rotate_tile(
+                    projection[:, part * 128 : (part + 1) * 128], window
+                ).astype(BF16)
+
+        loop(query_width // TILE, query_tile)
+        projection = jnp.dot(
+            normed[window, :], gate_w[:, pl.ds(query_width, TILE)], preferred_element_type=F32
+        )
+        for base, value in (
+            (1024, rotate_tile(projection[:, :128], window)),
+            (1536, projection[:, 128:]),
+        ):
+            other = pltpu.roll(value, 64, 1)
+            halves_of = (
+                jnp.where(lane < 64, value, 0.0),
+                jnp.where(lane >= 64, other, 0.0),
+                jnp.where(lane < 64, other, 0.0),
+                jnp.where(lane >= 64, value, 0.0),
+            )
+            for i, padded in enumerate(halves_of):
+                act[window, pl.ds(base + i * 128, 128)] = padded.astype(BF16)
+    normed_one_store.wait()
+    loads["gate"].start()
+    keeps = [
+        pltpu.make_async_copy(act.at[:, pl.ds(0, 512)], query_ref, local_sem.at[0]),
+        pltpu.make_async_copy(act.at[:, pl.ds(1024, 512)], keys_ref, local_sem.at[1]),
+        pltpu.make_async_copy(act.at[:, pl.ds(1536, 512)], values_ref, local_sem.at[2]),
+    ]
+    for keep in keeps:
+        keep.start()
+
+    def allowed_of(block):
+        keys_seen = (block + 1) * TILE
+        window = pl.ds(block * TILE, TILE)
+        key_place = lax.broadcasted_iota(jnp.int32, (keys_seen, TILE), 0)
+        query_place = lax.broadcasted_iota(jnp.int32, (keys_seen, TILE), 1) + block * TILE
+        return (key_place <= query_place) & (
+            segment_column_ref[pl.ds(0, keys_seen), :] == segment_row_ref[:, window]
+        )
+
+    def forward_pair(p):
+        kv = p // 2
+        column = pl.multiple_of(p * 128, 128)
+        for block in range(2):
+            window = pl.ds(block * TILE, TILE)
+            seen = pl.ds(0, (block + 1) * TILE)
+            queries = act[window, pl.ds(column, 128)]
+            allowed = allowed_of(block)
+            result = jnp.zeros((TILE, 128), F32)
+            for side in range(2):
+                padded = pl.multiple_of((kv * 2 + side) * 128, 128)
+                keys = act[seen, pl.ds(pl.multiple_of(1024 + padded, 128), 128)]
+                vals = act[seen, pl.ds(pl.multiple_of(1536 + padded, 128), 128)]
+                raw = jnp.where(
+                    allowed,
+                    lax.dot_general(keys, queries, transposed, preferred_element_type=F32)
+                    * factor,
+                    MASKED,
+                )
+                peak = jnp.max(raw, axis=0, keepdims=True)
+                lifted = jnp.exp(raw - peak)
+                summed = jnp.sum(lifted, axis=0, keepdims=True)
+                log_total_ref[pl.ds(2 * p + side, 1), window] = peak + jnp.log(summed)
+                result = result + lax.dot_general(
+                    (lifted * (1.0 / summed)).astype(BF16), vals, (((0,), (0,)), ((), ())),
+                    preferred_element_type=F32,
+                )
+            heads[window, pl.ds(column, 128)] = result.astype(BF16)
+
+    loop(4, forward_pair)
+    heads_store = pltpu.make_async_copy(heads, heads_out, local_sem.at[3])
+    heads_store.start()
+
     loads["w_out"].wait()
 
     def project(into, first_row):
         def step(j):
             columns = pl.ds(pl.multiple_of(j * TILE, TILE), TILE)
             into[:, columns] = jnp.dot(
-                heads[pl.ds(first_row, half), :], act[:, columns], preferred_element_type=F32
+                heads[pl.ds(first_row, half), :], cot[:, columns], preferred_element_type=F32
             )
 
         loop(width // TILE, step)
@@ -309,7 +351,6 @@
             y_send.at[which, k], y_recv.at[which, k], y_id,
         )
 
-    everything = slice(None)
     row_windows = [(rows(k), everything) for k in range(CHUNKS)]
 
     def column_window(j):
@@ -319,6 +360,7 @@
     for k in range(CHUNKS):
         core_copy(0, row_windows[k], k).start()
     project(mine.at[0], my_row)
+    loads["cot"].start()
     for k in range(CHUNKS):
         core_copy(0, row_windows[k], k).wait_recv()
 
@@ -329,7 +371,17 @@
         loop(chunk // ROWS, add)
         y_copy(0, row_windows[k], k).start()
 
-    loads["tok"].wait()
+    def stage_heads(i):
+        window = pl.ds(pl.multiple_of(i * ROWS, ROWS), ROWS)
+        for b in range(2):
+            here = pl.ds(pl.multiple_of(b * half + i * ROWS, ROWS), ROWS)
+            mine[1, window, pl.ds(b * 512, 512)] = heads[here, :].astype(F32)
+
+    loop(half // ROWS, stage_heads)
+    heads_copy = remote(
+        mine.at[1, :, early], heads_far, far_send.at[1], far_recv.at[1], far_id
+    )
+    heads_copy.start()
     gain = gain_ref[...]
     for k in range(CHUNKS):
         y_copy(0, row_windows[k], k).wait_recv()
@@ -337,7 +389,8 @@
         def normalize_rows(i, k=k):
             offset = pl.multiple_of(k * chunk + i * ROWS, ROWS)
             window = pl.ds(offset, ROWS)
-            values = tok[window, :].astype(F32) + (mine[0, window, :] + y_in[0, window, :])
+            own = tok[pl.ds(pl.multiple_of(my_row + offset, ROWS), ROWS), :].astype(F32)
+            values = own + (mine[0, window, :] + y_in[0, window, :])
             scale = lax.rsqrt(jnp.mean(values * values, axis=-1, keepdims=True) + EPSILON)
             rounded = (values * scale * gain).astype(BF16)
             hidden[window, :] = values
@@ -369,6 +422,8 @@
 
     for name in ("cot", "gate", "up", "down"):
         loads[name].wait()
+    for keep in keeps + [heads_store]:
+        keep.wait()
 
     def units(j):
         columns = pl.ds(pl.multiple_of(j * TILE, TILE), TILE)
@@ -385,9 +440,14 @@
 
     loop(hidden_units // TILE, units)
 
-    tiles = width // TILE
     for k in range(CHUNKS):
         core_copy(0, row_windows[k], k).wait_send()
+    normed_one_copy.wait()
+    heads_copy.wait()
+    normed_one_twin = remote(
+        normed_one_far.at[0], normed_one_far.at[1], far_send.at[2], far_recv.at[2], twin_id
+    )
+    normed_one_twin.start()
 
     def column_sums(which, tile_product, forwarded=True):
         def produce(j):
@@ -417,8 +477,6 @@
 
     def halves(dot_of):
         return dot_of(pl.ds(twin_row, half)), dot_of(pl.ds(my_row, half))
-
-    transposed = (((1,), (1,)), ((), ()))
 
     def back_tile(j):
         columns = pl.ds(pl.multiple_of(j * TILE, TILE), TILE)
@@ -516,25 +574,14 @@
     grad_attn_store = pltpu.make_async_copy(normed, grad_attn_out, local_sem.at[5])
     grad_attn_store.start()
 
-    def far_columns(b):
-        z_low = (dp // 2) % 2
-        return pl.ds(pl.multiple_of(b * 1024 + (1 - z_low) * 512, 512), 512)
-
-    def far_copies():
-        copies = []
-        for b in range(2):
-            kept = pl.ds(b * 512, 512)
-            copies.append(remote(
-                core_in.at[0, :, far_columns(b)], grad_attn_far.at[0, :, kept],
-                far_send.at[b], far_recv.at[b], far_id,
-            ))
-            copies.append(remote(
-                normed_twin.at[:, far_columns(b)], grad_attn_far.at[1, :, kept],
-                far_send.at[2 + b], far_recv.at[2 + b], far_id,
-            ))
-        return copies
-
-    for copy in far_copies():
+    hidden_far = [
+        remote(
+            core_in.at[0, :, far_columns(b)], grad_attn_far.at[0, :, pl.ds(b * 512, 512)],
+            far_send.at[3 + b], far_recv.at[3 + b], far_id,
+        )
+        for b in range(2)
+    ]
+    for copy in hidden_far:
         copy.start()
 
     for operand in operands:
@@ -555,19 +602,10 @@
             columns = pl.ds(pl.multiple_of(offset + kv * 256 + part * 128, 128), 128)
             sums[:, columns] = sums[:, columns] + value[part * TILE : (part + 1) * TILE]
 
-    factor = HEAD_SIZE ** (-0.5)
-    lane = lax.broadcasted_iota(jnp.int32, (TILE, 128), 1)
-
-    def unrotate_tile(value, window):
-        turned = jnp.where(
-            lane % 64 < 32, pltpu.roll(value, 96, 1), pltpu.roll(value, 32, 1)
-        )
-        return value * cosine_ref[window, :] + turned * sine_ref[window, :]
-
     def put(block, column, value):
         rounded = value.astype(BF16)
         gu[pl.ds(block * TILE, TILE), pl.ds(column, 128)] = rounded
-        core_in[1, :, pl.ds(block * 1024 + column, 128)] = rounded.astype(F32)
+        core_in[1, :, pl.ds(block * 768 + column, 128)] = rounded.astype(F32)
 
     def pair(p):
         kv = p // 2
@@ -578,11 +616,7 @@
             seen = pl.ds(0, keys_seen)
             queries = act[window, pl.ds(column, 128)]
             upstream = act[window, pl.ds(pl.multiple_of(512 + column, 128), 128)]
-            key_place = lax.broadcasted_iota(jnp.int32, (keys_seen, TILE), 0)
-            query_place = lax.broadcasted_iota(jnp.int32, (keys_seen, TILE), 1) + block * TILE
-            allowed = (key_place <= query_place) & (
-                segment_column_ref[seen, :] == segment_row_ref[:, window]
-            )
+            allowed = allowed_of(block)
             query_grad = jnp.zeros((TILE, 128), F32)
             for side in range(2):
                 padded = pl.multiple_of((kv * 2 + side) * 128, 128)
@@ -628,15 +662,16 @@
     )
     projected_store.start()
 
-    def projected_copy(b):
-        window = (everything, pl.ds(b * 1024, 768))
-        return remote(
-            core_in.at[1].at[window], projected_far.at[window],
-            far_send.at[4 + b], far_recv.at[4 + b], far_id,
-        )
-
-    projected_copy(0).start()
-    projected_copy(1).start()
+    projected_copy = remote(
+        core_in.at[1, :, pl.ds(0, 1536)], projected_far, far_send.at[5], far_recv.at[5], far_id
+    )
+    projected_copy.start()
+    for copy in hidden_far:
+        copy.wait_recv()
+    hidden_far_twin = remote(
+        grad_attn_far.at[0], grad_attn_far.at[1], far_send.at[7], far_recv.at[7], twin_id
+    )
+    hidden_far_twin.start()
 
     for k in range(CHUNKS):
         from_x(normed_sent, normed_others, k, n_send, n_recv).wait_recv()
@@ -668,7 +703,9 @@
     for store in (hidden_store, grad_attn_store, projected_store, mixed_store):
         store.wait()
     mixed_copy.wait()
-    for copy in far_copies() + [projected_copy(0), projected_copy(1)]:
+    for copy in hidden_far:
+        copy.wait_send()
+    for copy in (hidden_far_twin, normed_one_twin, projected_copy):
         copy.wait()
     for k in range(CHUNKS):
         hidden_copy(k).wait_send()
@@ -688,8 +725,8 @@
 
 
 def middle(
-    heads, w_out, tokens, cotangent, cotangent_half, gain, w_gate, w_up, w_down,
-    query, keys, values, log_total, segment, cosine, sine,
+    w_query, w_key, w_value, w_out, tokens, cotangent, cotangent_half, gain_one, gain,
+    w_gate, w_up, w_down, segment, cosine, sine,
 ):
     row_count, width = tokens.shape
     half = row_count // 2
@@ -699,15 +736,20 @@
     vmem = pl.BlockSpec(memory_space=pltpu.VMEM)
     wide = jax.ShapeDtypeStruct((half, width), F32)
     units = jax.ShapeDtypeStruct((row_count, hidden_units), BF16)
+    square = jax.ShapeDtypeStruct((row_count, 512), BF16)
     dma = pltpu.SemaphoreType.DMA
     return pl.pallas_call(
         middle_kernel,
         out_shape=(
+            jax.ShapeDtypeStruct((row_count, width), BF16),
+            square, square, square, square,
+            jax.ShapeDtypeStruct((2, half, width // 2), F32),
+            jax.ShapeDtypeStruct((half, width // 2), F32),
             wide,
             jax.ShapeDtypeStruct((row_count, width), BF16),
             jax.ShapeDtypeStruct((row_count, 768), BF16),
             jax.ShapeDtypeStruct((2, half, width // 2), F32),
-            wide,
+            jax.ShapeDtypeStruct((half, 2 * 768), F32),
             wide, wide,
             jax.ShapeDtypeStruct((row_count, width), BF16),
             units, units, units,
@@ -715,8 +757,8 @@
             jax.ShapeDtypeStruct((6, half, width), F32),
             jax.ShapeDtypeStruct((6, half, width), F32),
         ),
-        in_specs=[hbm, hbm, hbm, hbm, hbm, vmem, hbm, hbm, hbm, hbm, hbm, hbm] + [vmem] * 5,
-        out_specs=(hbm,) * 11 + (vmem,) + (hbm,) * 2,
+        in_specs=[hbm] * 7 + [vmem] * 2 + [hbm] * 3 + [vmem] * 4,
+        out_specs=(hbm,) * 18 + (vmem,) + (hbm,) * 2,
         scratch_shapes=[
             pltpu.VMEM(w_gate.shape, BF16),
             pltpu.VMEM(w_up.shape, BF16),
@@ -740,16 +782,521 @@
             dma((2, 3)), dma((2, 3)),
             dma((2,)), dma((2,)),
             dma((CHUNKS,)), dma((CHUNKS,)),
-            dma((6,)), dma((6,)),
+            dma((8,)), dma((8,)),
+            pltpu.VMEM((8, row_count), F32),
         ],
         compiler_params=pltpu.CompilerParams(
             collective_id=0, has_side_effects=True, vmem_limit_bytes=64 * 1024 * 1024
         ),
         name="feed_forward",
     )(
-        heads, w_out, tokens, cotangent, cotangent_half, gain.reshape(1, width),
-        w_gate, w_up, w_down, query, keys, values, log_total,
+        w_query, w_key, w_value, w_out, tokens, cotangent, cotangent_half,
+        gain_one.reshape(1, width), gain.reshape(1, width), w_gate, w_up, w_down,
         segment.reshape(row_count, 1), segment.reshape(1, row_count), cosine, sine,
+    )
+
+
+def last_kernel(
+    normed_others_ref,
+    cot_others_ref,
+    normed_ref,
+    cot_ref,
+    act_ref,
+    gg_ref,
+    gu_ref,
+    w_gate_ref,
+    w_up_ref,
+    w_down_ref,
+    projected_ref,
+    projected_far_ref,
+    w_query_ref,
+    w_key_ref,
+    w_value_ref,
+    heads_ref,
+    grad_attn_ref,
+    grad_attn_far_ref,
+    normed_one_ref,
+    normed_one_far_ref,
+    heads_far_ref,
+    grad_hidden_ref,
+    tokens_ref,
+    gain_ref,
+    kept_out,
+    sent_out,
+    came_out,
+    out_mine,
+    out_came,
+    proj_mine,
+    proj_came,
+    input_half_out,
+    input_twin_out,
+    gain_out,
+    normed,
+    cot,
+    normed_t,
+    cot_t,
+    units,
+    gate_w,
+    up_w,
+    down_w,
+    total,
+    staged,
+    core_in,
+    y_in,
+    w_proj,
+    tok,
+    heads,
+    grad_attn,
+    normed_one,
+    projected,
+    out_part,
+    proj_part,
+    out_x,
+    proj_x,
+    own_columns,
+    far_staged,
+    far_heads,
+    load_sem,
+    piece_sem,
+    weight_sem,
+    unit_sem,
+    store_sem,
+    row_send,
+    row_recv,
+    core_send,
+    core_recv,
+    y_send,
+    y_recv,
+    x_send,
+    x_recv,
+    z_send,
+    z_recv,
+    end_send,
+    end_recv,
+):
+    dp, tensor = lax.axis_index("dp"), lax.axis_index("tensor")
+    core = tensor % 2
+    x_low, z_low, z_high = dp % 2, (dp // 2) % 2, dp // 4
+    twin_id = (dp, flip(tensor, 1))
+    y_id = (dp, flip(tensor, 2))
+    x_id = (flip(dp, 1), tensor)
+    z_id = (flip(dp, 4), tensor)
+    far_id = (flip(dp, 2), tensor)
+    half, width = tok.shape
+    row_count = 2 * half
+    tiles = width // TILE
+    my_row = pl.multiple_of(core * half, half)
+    twin_row = pl.multiple_of((1 - core) * half, half)
+    everything = slice(None)
+    transposed = (((1,), (1,)), ((), ()))
+    over = (((0,), (0,)), ((), ()))
+
+    def remote(src, dst, send, recv, device):
+        return pltpu.make_async_remote_copy(
+            src_ref=src, dst_ref=dst, send_sem=send, recv_sem=recv,
+            device_id=device, device_id_type=MESH,
+        )
+
+    def tile_of(j):
+        return pl.ds(pl.multiple_of(j * TILE, TILE), TILE)
+
+    away_block = tile_of(flip(dp, 2))
+    home_block = tile_of(dp)
+    near = [
+        pl.ds(pl.multiple_of(b * 1024 + z_low * 512, 512), 512) for b in range(2)
+    ]
+    loads = [
+        pltpu.make_async_copy(normed_ref.at[:, away_block], own_columns.at[0], load_sem.at[0]),
+        pltpu.make_async_copy(normed_ref.at[:, home_block], own_columns.at[1], load_sem.at[1]),
+        pltpu.make_async_copy(cot_ref.at[:, away_block], own_columns.at[2], load_sem.at[2]),
+        pltpu.make_async_copy(cot_ref.at[:, home_block], own_columns.at[3], load_sem.at[3]),
+        pltpu.make_async_copy(w_query_ref, w_proj.at[:, pl.ds(0, 512)], load_sem.at[4]),
+        pltpu.make_async_copy(w_key_ref, w_proj.at[:, pl.ds(512, 128)], load_sem.at[5]),
+        pltpu.make_async_copy(w_value_ref, w_proj.at[:, pl.ds(640, 128)], load_sem.at[6]),
+        pltpu.make_async_copy(tokens_ref.at[pl.ds(my_row, half)], tok, load_sem.at[7]),
+        pltpu.make_async_copy(heads_ref, heads.at[0], load_sem.at[8]),
+        pltpu.make_async_copy(
+            grad_attn_ref.at[:, near[0]], grad_attn.at[0, :, pl.ds(0, 512)], load_sem.at[9]
+        ),
+        pltpu.make_async_copy(
+            grad_attn_ref.at[:, near[1]], grad_attn.at[0, :, pl.ds(512, 512)], load_sem.at[10]
+        ),
+        pltpu.make_async_copy(
+            normed_one_ref.at[:, near[0]], normed_one.at[0, :, pl.ds(0, 512)], load_sem.at[11]
+        ),
+        pltpu.make_async_copy(
+            normed_one_ref.at[:, near[1]], normed_one.at[0, :, pl.ds(512, 512)], load_sem.at[12]
+        ),
+        pltpu.make_async_copy(projected_ref, projected.at[0], load_sem.at[13]),
+    ]
+
+    def piece_load(i, slot):
+        source = normed_others_ref.at[i] if i < 6 else cot_others_ref.at[i - 6]
+        return pltpu.make_async_copy(source, staged.at[slot], piece_sem.at[slot])
+
+    def weight_loads(j, slot):
+        return [
+            pltpu.make_async_copy(
+                w_gate_ref.at[:, tile_of(j)], gate_w.at[slot], weight_sem.at[slot, 0]
+            ),
+            pltpu.make_async_copy(
+                w_up_ref.at[:, tile_of(j)], up_w.at[slot], weight_sem.at[slot, 1]
+            ),
+            pltpu.make_async_copy(
+                w_down_ref.at[tile_of(j), :], down_w.at[slot], weight_sem.at[slot, 2]
+            ),
+        ]
+
+    piece_load(0, 0).start()
+    piece_load(1, 1).start()
+    for load in loads[:4]:
+        load.start()
+    for load in weight_loads(0, 0):
+        load.start()
+
+    barrier = pltpu.get_barrier_semaphore()
+    for device in (twin_id, y_id, x_id, z_id, far_id):
+        pl.semaphore_signal(barrier, inc=1, device_id=device, device_id_type=MESH)
+    pl.semaphore_wait(barrier, 5)
+
+    for i in range(12):
+        piece_load(i, i % 2).wait()
+        rows_to, turned_to = (normed, normed_t) if i < 6 else (cot, cot_t)
+        base = (i % 6) * half
+
+        def convert(r, i=i, rows_to=rows_to, base=base):
+            window = pl.ds(pl.multiple_of(r * ROWS, ROWS), ROWS)
+            rows_to[pl.ds(pl.multiple_of(base + r * ROWS, ROWS), ROWS), :] = staged[
+                i % 2, window, :
+            ].astype(BF16)
+
+        loop(half // ROWS, convert)
+        for part, block in enumerate((away_block, home_block)):
+            turned_to[pl.ds(part * TILE, TILE), pl.ds(row_count + base, half)] = (
+                staged[i % 2, :, block].T.astype(BF16)
+            )
+        if i + 2 < 12:
+            piece_load(i + 2, i % 2).start()
+    for part in range(4):
+        loads[part].wait()
+        turned_to = (normed_t, cot_t)[part // 2]
+        turned_to[pl.ds((part % 2) * TILE, TILE), pl.ds(0, row_count)] = (
+            own_columns[part].astype(F32).T.astype(BF16)
+        )
+
+    for load in loads[4:]:
+        load.start()
+    far_loads = (
+        [
+            pltpu.make_async_copy(
+                grad_attn_far_ref.at[s], staged.at[0, :, pl.ds(s * 1024, 1024)], piece_sem.at[s]
+            )
+            for s in range(2)
+        ]
+        + [
+            pltpu.make_async_copy(
+                normed_one_far_ref.at[s], staged.at[1, :, pl.ds(s * 1024, 1024)],
+                piece_sem.at[2 + s],
+            )
+            for s in range(2)
+        ]
+        + [
+            pltpu.make_async_copy(projected_far_ref, far_staged, piece_sem.at[4]),
+            pltpu.make_async_copy(heads_far_ref, far_heads, piece_sem.at[5]),
+        ]
+    )
+    for load in far_loads:
+        load.start()
+
+    def row_copy(j):
+        window = (everything, everything, tile_of(j))
+        return remote(
+            sent_out.at[window], came_out.at[window], row_send.at[j], row_recv.at[j], far_id
+        )
+
+    def stores(j, slot):
+        return [
+            pltpu.make_async_copy(
+                total.at[slot, :, pl.ds(0, TILE)], sent_out.at[:, :, tile_of(j)],
+                store_sem.at[slot, 0],
+            ),
+            pltpu.make_async_copy(
+                total.at[slot, :, pl.ds(TILE, TILE)], kept_out.at[:, :, tile_of(j)],
+                store_sem.at[slot, 1],
+            ),
+        ]
+
+    def unit_loads(j):
+        return [
+            pltpu.make_async_copy(
+                source.at[:, tile_of(j)], units.at[i, pl.ds(0, row_count)], unit_sem.at[i]
+            )
+            for i, source in enumerate((gg_ref, gu_ref, act_ref))
+        ]
+
+    def feed_forward_tile(j):
+        slot = j % 2
+        for load in weight_loads(j, slot):
+            load.wait()
+
+        @pl.when(j + 1 < tiles)
+        def _():
+            for load in weight_loads(j + 1, 1 - slot):
+                load.start()
+
+        for load in unit_loads(j):
+            load.start()
+
+        def block(m):
+            rows = pl.ds(pl.multiple_of(m * 512, 512), 512)
+            to = pl.ds(pl.multiple_of(row_count + m * 512, 512), 512)
+            gate = jnp.dot(normed[rows, :], gate_w[slot], preferred_element_type=F32)
+            up = jnp.dot(normed[rows, :], up_w[slot], preferred_element_type=F32)
+            back = lax.dot_general(
+                cot[rows, :], down_w[slot], transposed, preferred_element_type=F32
+            )
+            sigmoid = jax.nn.sigmoid(gate)
+            swish = gate * sigmoid
+            units[2, to, :] = (swish * up).astype(BF16)
+            units[0, to, :] = (back * up * sigmoid * (1.0 + gate * (1.0 - sigmoid))).astype(BF16)
+            units[1, to, :] = (back * swish).astype(BF16)
+
+        loop(normed.shape[0] // 512, block)
+        for load in unit_loads(j):
+            load.wait()
+
+        @pl.when(j >= 1)
+        def _():
+            for store in stores(j - 1, 1 - slot):
+                store.wait()
+            row_copy(j - 1).start()
+
+        total[slot, 0] = jnp.dot(normed_t[...], units[0], preferred_element_type=F32)
+        total[slot, 1] = jnp.dot(normed_t[...], units[1], preferred_element_type=F32)
+        total[slot, 2] = jnp.dot(cot_t[...], units[2], preferred_element_type=F32)
+        for store in stores(j, slot):
+            store.start()
+
+    def x_copies(slot):
+        return [
+            remote(out_part.at[0, slot], out_x.at[slot], x_send.at[0, slot],
+                   x_recv.at[0, slot], x_id),
+            remote(proj_part.at[0, slot], proj_x.at[slot], x_send.at[1, slot],
+                   x_recv.at[1, slot], x_id),
+        ]
+
+    def attention_parts():
+        for load in far_loads + loads[8:]:
+            load.wait()
+
+        def convert(r):
+            window = pl.ds(pl.multiple_of(r * ROWS, ROWS), ROWS)
+            for s in range(2):
+                start = my_row if s == 0 else twin_row
+                here = pl.ds(pl.multiple_of(start + r * ROWS, ROWS), ROWS)
+                grad_attn[1, here, :] = staged[0, window, pl.ds(s * 1024, 1024)].astype(BF16)
+                normed_one[1, here, :] = staged[1, window, pl.ds(s * 1024, 1024)].astype(BF16)
+                there = pl.ds(pl.multiple_of(s * half + r * ROWS, ROWS), ROWS)
+                projected[1, there, :] = far_staged[window, pl.ds(s * 768, 768)].astype(BF16)
+                heads[1, there, :] = far_heads[window, pl.ds(s * 512, 512)].astype(BF16)
+
+        loop(half // ROWS, convert)
+        for side in range(2):
+            x_at = 1 - x_low if side == 0 else x_low
+            for slot in range(2):
+                z_at = 1 - z_high if slot == 0 else z_high
+                columns = pl.ds(pl.multiple_of(z_at * 512 + x_at * 256, 256), 256)
+                out_part[side, slot] = lax.dot_general(
+                    heads[0], grad_attn[0, :, columns], over, preferred_element_type=F32
+                ) + lax.dot_general(
+                    heads[1], grad_attn[1, :, columns], over, preferred_element_type=F32
+                )
+                proj_part[side, slot] = lax.dot_general(
+                    normed_one[0, :, columns], projected[0], over, preferred_element_type=F32
+                ) + lax.dot_general(
+                    normed_one[1, :, columns], projected[1], over, preferred_element_type=F32
+                )
+                if side == 0:
+                    for copy in x_copies(slot):
+                        copy.start()
+
+    def core_copy(j):
+        window = (everything, tile_of(j))
+        return remote(
+            staged.at[0].at[window], core_in.at[window], core_send.at[j], core_recv.at[j], twin_id
+        )
+
+    def y_copy(j):
+        window = (everything, tile_of(j))
+        return remote(
+            staged.at[1].at[window], y_in.at[window], y_send.at[j], y_recv.at[j], y_id
+        )
+
+    def attention_sums():
+        for load in loads[4:8]:
+            load.wait()
+
+        def produce(j):
+            weight = w_proj[tile_of(j), :]
+            for slot, start in ((0, twin_row), (1, my_row)):
+                staged[slot, :, tile_of(j)] = lax.dot_general(
+                    projected[0, pl.ds(start, half), :], weight, transposed,
+                    preferred_element_type=F32,
+                )
+            core_copy(j).start()
+
+        def forward(j):
+            core_copy(j).wait_recv()
+            staged[1, :, tile_of(j)] = staged[1, :, tile_of(j)] + core_in[:, tile_of(j)]
+            y_copy(j).start()
+
+        produce(0)
+
+        def step(j):
+            produce(j + 1)
+            forward(j)
+
+        loop(tiles - 1, step)
+        forward(tiles - 1)
+        loop(tiles, lambda j: core_copy(j).wait_send())
+
+    def step(j):
+        feed_forward_tile(j)
+
+        @pl.when(j == 1)
+        def _():
+            attention_parts()
+            attention_sums()
+
+    loop(tiles, step)
+    hidden_load = pltpu.make_async_copy(grad_hidden_ref, core_in, load_sem.at[0])
+    hidden_load.start()
+    for store in stores(tiles - 1, (tiles - 1) % 2):
+        store.wait()
+    row_copy(tiles - 1).start()
+
+    def z_copies():
+        return [
+            remote(out_part.at[1, 0], out_came, z_send.at[0], z_recv.at[0], z_id),
+            remote(proj_part.at[1, 0], proj_came, z_send.at[1], z_recv.at[1], z_id),
+        ]
+
+    for slot in range(2):
+        for copy in x_copies(slot):
+            copy.wait_recv()
+        out_part[1, slot] = out_part[1, slot] + out_x[slot]
+        proj_part[1, slot] = proj_part[1, slot] + proj_x[slot]
+        if slot == 0:
+            for copy in z_copies():
+                copy.start()
+    part_stores = [
+        pltpu.make_async_copy(out_part.at[1, 1], out_mine, load_sem.at[1]),
+        pltpu.make_async_copy(proj_part.at[1, 1], proj_mine, load_sem.at[2]),
+    ]
+    for store in part_stores:
+        store.start()
+
+    gain = gain_ref[...]
+    gain_out[...] = jnp.zeros_like(gain_out)
+    hidden_load.wait()
+    loop(tiles, lambda j: y_copy(j).wait_recv())
+
+    def norm_rows(i):
+        window = pl.ds(pl.multiple_of(i * ROWS, ROWS), ROWS)
+        incoming = staged[1, window, :] + y_in[window, :]
+        values = tok[window, :].astype(F32)
+        scale = lax.rsqrt(jnp.mean(values * values, axis=-1, keepdims=True) + EPSILON)
+        weighted = incoming * gain
+        inner = jnp.mean(weighted * values, axis=-1, keepdims=True)
+        back = scale * weighted - values * (scale * scale * scale) * inner
+        staged[0, window, :] = core_in[window, :] + back
+        gain_out[...] = gain_out[...] + jnp.sum(
+            incoming * values * scale, axis=0, keepdims=True
+        )
+
+    loop(half // ROWS, norm_rows)
+    input_copy = remote(
+        staged.at[0], input_twin_out, end_send.at[0], end_recv.at[0], twin_id
+    )
+    input_copy.start()
+    input_store = pltpu.make_async_copy(staged.at[0], input_half_out, load_sem.at[3])
+    input_store.start()
+
+    for store in part_stores + [input_store]:
+        store.wait()
+    input_copy.wait()
+    for slot in range(2):
+        for copy in x_copies(slot):
+            copy.wait_send()
+    loop(tiles, lambda j: y_copy(j).wait_send())
+    for copy in z_copies():
+        copy.wait()
+    loop(tiles, lambda j: row_copy(j).wait())
+
+
+def last(
+    normed_others, cot_others, normed, cot, act, gg, gu, w_gate, w_up, w_down,
+    projected, projected_far, w_query, w_key, w_value, heads, grad_attn, grad_attn_far,
+    normed_one, normed_one_far, heads_far, grad_hidden, tokens, gain,
+):
+    row_count, width = tokens.shape
+    half = row_count // 2
+    tiles = width // TILE
+    hidden_units = w_gate.shape[1]
+    hbm = pl.BlockSpec(memory_space=pl.ANY)
+    vmem = pl.BlockSpec(memory_space=pltpu.VMEM)
+    wide = jax.ShapeDtypeStruct((half, width), F32)
+    triple = jax.ShapeDtypeStruct((3, TILE, hidden_units), F32)
+    out_block = jax.ShapeDtypeStruct((512, TILE), F32)
+    proj_block = jax.ShapeDtypeStruct((TILE, 768), F32)
+    dma = pltpu.SemaphoreType.DMA
+    return pl.pallas_call(
+        last_kernel,
+        out_shape=(
+            triple, triple, triple, out_block, out_block, proj_block, proj_block, wide, wide,
+            jax.ShapeDtypeStruct((1, width), F32),
+        ),
+        in_specs=[hbm] * 23 + [vmem],
+        out_specs=(hbm,) * 9 + (vmem,),
+        scratch_shapes=[
+            pltpu.VMEM((6 * half, width), BF16),
+            pltpu.VMEM((6 * half, width), BF16),
+            pltpu.VMEM((2 * TILE, row_count + 6 * half), BF16),
+            pltpu.VMEM((2 * TILE, row_count + 6 * half), BF16),
+            pltpu.VMEM((3, row_count + 6 * half, TILE), BF16),
+            pltpu.VMEM((2, width, TILE), BF16),
+            pltpu.VMEM((2, width, TILE), BF16),
+            pltpu.VMEM((2, TILE, width), BF16),
+            pltpu.VMEM((2, 3, 2 * TILE, TILE), F32),
+            pltpu.VMEM((2, half, width), F32),
+            pltpu.VMEM((half, width), F32),
+            pltpu.VMEM((half, width), F32),
+            pltpu.VMEM((width, 768), BF16),
+            pltpu.VMEM((half, width), BF16),
+            pltpu.VMEM((2, row_count, 512), BF16),
+            pltpu.VMEM((2, row_count, 1024), BF16),
+            pltpu.VMEM((2, row_count, 1024), BF16),
+            pltpu.VMEM((2, row_count, 768), BF16),
+            pltpu.VMEM((2, 2, 512, TILE), F32),
+            pltpu.VMEM((2, 2, TILE, 768), F32),
+            pltpu.VMEM((2, 512, TILE), F32),
+            pltpu.VMEM((2, TILE, 768), F32),
+            pltpu.VMEM((4, row_count, TILE), BF16),
+            pltpu.VMEM((half, 2 * 768), F32),
+            pltpu.VMEM((half, 1024), F32),
+            dma((14,)), dma((6,)), dma((2, 3)), dma((3,)), dma((2, 2)),
+            dma((tiles,)), dma((tiles,)),
+            dma((tiles,)), dma((tiles,)), dma((tiles,)), dma((tiles,)),
+            dma((2, 2)), dma((2, 2)), dma((2,)), dma((2,)), dma((1,)), dma((1,)),
+        ],
+        compiler_params=pltpu.CompilerParams(
+            collective_id=1, has_side_effects=True, vmem_limit_bytes=64 * 1024 * 1024
+        ),
+        name="weight_gradients",
+    )(
+        normed_others, cot_others, normed, cot, act, gg, gu, w_gate, w_up, w_down,
+        projected, projected_far, w_query, w_key, w_value, heads, grad_attn, grad_attn_far,
+        normed_one, normed_one_far, heads_far, grad_hidden, tokens, gain.reshape(1, width),
     )
 
 
@@ -803,63 +1350,21 @@
             sent = {offset: h + c for offset, h, c in zip(offsets, home, came)}
         return sent[0]
 
-    inputs = tokens.astype(F32)
-    row_count, width = inputs.shape
-    seq_count, seq_len = segments.shape
-    query_heads = w_query.shape[1] // HEAD_SIZE
-    kv_heads = key_weight.shape[1] // HEAD_SIZE
-    group_size = query_heads // kv_heads
+    row_count, width = tokens.shape
     query_width, kv_width = w_query.shape[1], key_weight.shape[1]
-
-    scale_one = lax.rsqrt(jnp.mean(inputs * inputs, axis=-1, keepdims=True) + EPSILON)
-    normed_one = (inputs * scale_one * attn_gain).astype(BF16)
-    cosine_lookup, sine_lookup = tables(positions.reshape(row_count))
-    cosine_lookup = cosine_lookup[:, None, :]
-    sine_lookup = sine_lookup[:, None, :]
-    query_projected = product(normed_one, w_query).reshape(row_count, query_heads, HEAD_SIZE)
-    key_projected = product(normed_one, key_weight).reshape(row_count, kv_heads, HEAD_SIZE)
-    query_rotated = (
-        apply_rotary(query_projected, cosine_lookup, sine_lookup)
-        .astype(BF16)
-        .reshape(seq_count, seq_len, kv_heads, group_size, HEAD_SIZE)
-    )
-    key_rotated = (
-        apply_rotary(key_projected, cosine_lookup, sine_lookup)
-        .astype(BF16)
-        .reshape(seq_count, seq_len, kv_heads, HEAD_SIZE)
-    )
-    value_projected = (
-        product(normed_one, value_weight)
-        .astype(BF16)
-        .reshape(seq_count, seq_len, kv_heads, HEAD_SIZE)
-    )
-    combined_heads, log_totals = per_sequence(
-        attend_forward, query_rotated, key_rotated, value_projected, segments
-    )
-    head_outputs = combined_heads.reshape(row_count, query_width).astype(BF16)
-
-    inputs_half = half_of(inputs, core)
-    cotangent_half = half_of(cotangent, core).astype(F32)
-    def padded(heads):
-        zeros = jnp.zeros((row_count, HEAD_SIZE), BF16)
-        parts = []
-        for h in range(kv_heads):
-            parts += [heads[0, :, h], zeros, zeros, heads[0, :, h]]
-        return jnp.concatenate(parts, axis=1)
-
-    z_low = (place // 2) % 2
-
-    def near(matrix, which):
-        parts = matrix.reshape(matrix.shape[0], 2, 2, -1)
-        return lax.dynamic_index_in_dim(parts, which, 2, False).reshape(matrix.shape[0], -1)
-
-    heads_far = narrowed(swap(head_outputs.astype(F32), "dp", 2))
-    normed_one_far = narrowed(swap(near(normed_one, 1 - z_low).astype(F32), "dp", 2))
-    lanes = jnp.arange(128) % HEAD_SIZE
-    cosine_tile = jnp.concatenate([cosine_lookup[:, 0], cosine_lookup[:, 0]], axis=1)
-    sine_tile = jnp.concatenate([sine_lookup[:, 0], sine_lookup[:, 0]], axis=1)
-    sine_tile = jnp.where(lanes < HEAD_SIZE // 2, sine_tile, -sine_tile)
+    half_dim = HEAD_SIZE // 2
+    frequency = 500000.0 ** (-(jnp.arange(half_dim).astype(F32) * 2.0 / HEAD_SIZE))
+    angles = positions.reshape(row_count, 1).astype(F32) * jnp.tile(frequency, 4)
+    cosine_tile = jnp.cos(angles)
+    sine_tile = jnp.sin(angles) * jnp.where(jnp.arange(128) % HEAD_SIZE < half_dim, 1.0, -1.0)
     (
+        normed_one,
+        head_outputs,
+        _,
+        _,
+        _,
+        normed_one_far,
+        heads_far,
         grad_hidden,
         grad_attn,
         projected,
@@ -875,90 +1380,36 @@
         cotangent_others,
         normed_others,
     ) = middle(
-        head_outputs, w_out, tokens, cotangent, cotangent_half, mlp_gain, w_gate, w_up, w_down,
-        query_rotated.reshape(row_count, query_width), padded(key_rotated),
-        padded(value_projected), log_totals.reshape(query_heads, row_count), segments,
-        cosine_tile, sine_tile,
+        w_query, key_weight, value_weight, w_out, tokens, cotangent,
+        half_of(cotangent, core).astype(F32), attn_gain, mlp_gain, w_gate, w_up, w_down,
+        segments, cosine_tile, sine_tile,
     )
     gain_two_half = gain_two_half[0]
     mixed = joined(mixed_half, mixed_twin, core).astype(BF16)
-    cotangent_others = cotangent_others.reshape(-1, width).astype(BF16)
-    normed_others = normed_others.reshape(-1, width).astype(BF16)
-    grad_attn_far = joined(grad_attn_far[0], grad_attn_far[1], core).astype(BF16)
-    projected_far = jnp.concatenate(
-        [projected_far[:, :768], projected_far[:, 1024:1792]], axis=0
-    ).astype(BF16)
-
-    def feed_forward(normed, incoming):
-        gate_proj = product(normed, w_gate)
-        up_proj = product(normed, w_up)
-        grad_activation = against(incoming, w_down)
-        sigmoid_gate = jax.nn.sigmoid(gate_proj)
-        swish_gate = gate_proj * sigmoid_gate
-        activation = (swish_gate * up_proj).astype(BF16)
-        grad_gate_in = (
-            grad_activation * up_proj * sigmoid_gate * (1.0 + gate_proj * (1.0 - sigmoid_gate))
-        ).astype(BF16)
-        grad_up_in = (grad_activation * swish_gate).astype(BF16)
-        return activation, grad_gate_in, grad_up_in
-
-    partial_one = against(
-        projected, jnp.concatenate([w_query, key_weight, value_weight], axis=1)
-    )
-    grad_normed_one = tensor_sum_half(partial_one, core)
-    scale_one = half_of(scale_one, core)
-    weighted = grad_normed_one * attn_gain
-    inner_mean = jnp.mean(weighted * inputs_half, axis=-1, keepdims=True)
-    back_one = scale_one * weighted - inputs_half * (scale_one * scale_one * scale_one) * inner_mean
-    gain_one_half = jnp.sum(grad_normed_one * inputs_half * scale_one, axis=0)
-    input_half = grad_hidden + back_one
-    grad_input = joined(input_half, swap(input_half, "tensor", 1), core)
-
-    activation_o, grad_gate_o, grad_up_o = feed_forward(normed_others, cotangent_others)
-
-    def rows_of(left, left_others, right, right_others):
-        def term(offsets):
-            ours = blocks(left, offsets)
-            theirs = blocks(left_others, offsets)
-            return [
-                over_rows(a, right) + over_rows(b, right_others) for a, b in zip(ours, theirs)
-            ]
-
-        return reduced(term, split_bits)
-
-    def columns_of(left, left_others, right, right_others):
-        def term(offsets):
-            ours = blocks(right, offsets)
-            theirs = blocks(right_others, offsets)
-            return [
-                over_rows(left, a) + over_rows(left_others, b) for a, b in zip(ours, theirs)
-            ]
-
-        return reduced(term, split_bits)
-
-    grad_w_down = columns_of(activation, activation_o, cotangent, cotangent_others)
-    grad_w_gate = rows_of(normed_two, normed_others, grad_gate_in, grad_gate_o)
-    grad_w_up = rows_of(normed_two, normed_others, grad_up_in, grad_up_o)
-
-    out_part = over_rows(head_outputs, near(grad_attn, z_low)) + over_rows(
-        heads_far, grad_attn_far
-    )
-    proj_part = over_rows(near(normed_one, z_low), projected) + over_rows(
-        normed_one_far, projected_far
-    )
-    x_low, z_high = place % 2, place // 4
-    width_out = width // groups
-
-    def reduced_far(parts):
-        column = lambda which: lax.dynamic_index_in_dim(parts, which, 1, False)
-        parts = column(x_low) + swap(column(1 - x_low), "dp", 1)
-        piece = lambda which: lax.dynamic_index_in_dim(parts, which, 0, False)
-        return piece(z_high) + swap(piece(1 - z_high), "dp", 4)
-
-    grad_w_out = reduced_far(
-        out_part.reshape(query_width, 2, 2, width_out).transpose(1, 2, 0, 3)
-    )
-    grad_w_proj = reduced_far(proj_part.reshape(2, 2, width_out, -1))
+    (
+        kept,
+        _,
+        came,
+        out_mine,
+        out_came,
+        proj_mine,
+        proj_came,
+        input_half,
+        input_twin,
+        gain_one_half,
+    ) = last(
+        normed_others, cotangent_others, normed_two, cotangent, activation, grad_gate_in,
+        grad_up_in, w_gate, w_up, w_down, projected, projected_far, w_query, key_weight,
+        value_weight, head_outputs, grad_attn, grad_attn_far, normed_one, normed_one_far,
+        heads_far, grad_hidden, tokens, attn_gain,
+    )
+    gain_one_half = gain_one_half[0]
+    grad_input = joined(input_half, input_twin, core)
+    grad_w_gate = kept[0] + came[0]
+    grad_w_up = kept[1] + came[1]
+    grad_w_down = (kept[2] + came[2]).T
+    grad_w_out = out_mine + out_came
+    grad_w_proj = proj_mine + proj_came
     grad_w_query = grad_w_proj[:, :query_width]
     grad_w_key = grad_w_proj[:, query_width : query_width + kv_width]
     grad_w_value = grad_w_proj[:, query_width + kv_width :]
@@ -980,6 +1431,110 @@
         grad_w_up,
         grad_w_down,
     )
+
+
+def product(left_matrix, right_matrix):
+    return jnp.dot(left_matrix, right_matrix, preferred_element_type=F32)
+
+
+def over_rows(left_matrix, right_matrix):
+    return lax.dot_general(
+        left_matrix, right_matrix, (((0,), (0,)), ((), ())), preferred_element_type=F32
+    )
+
+
+def against(gradient, weight):
+    return lax.dot_general(
+        gradient, weight, (((1,), (1,)), ((), ())), preferred_element_type=F32
+    )
+
+
+def narrowed(value):
+    return jnp.where(value == value, value, 0.0).astype(BF16)
+
+
+def tensor_sum_half(partial, core):
+    total = half_of(partial, core) + swap(half_of(partial, 1 - core), "tensor", 1)
+    bit = 2
+    while bit < lax.axis_size("tensor"):
+        total = total + swap(total, "tensor", bit)
+        bit *= 2
+    return total
+
+
+def tables(places):
+    half_dim = HEAD_SIZE // 2
+    frequency = 500000.0 ** (-(jnp.arange(half_dim).astype(F32) * 2.0 / HEAD_SIZE))
+    angles = places.astype(F32)[..., None] * frequency
+    cosine_lookup = jnp.cos(angles)
+    sine_lookup = jnp.sin(angles)
+    return (
+        jnp.concatenate([cosine_lookup, cosine_lookup], -1),
+        jnp.concatenate([sine_lookup, sine_lookup], -1),
+    )
+
+
+def apply_rotary(field, cosine_lookup, sine_lookup):
+    half_dim = HEAD_SIZE // 2
+    turned = jnp.concatenate([-field[..., half_dim:], field[..., :half_dim]], -1)
+    return field * cosine_lookup + turned * sine_lookup
+
+
+def unrotate(gradient, cosine_lookup, sine_lookup):
+    half_dim = HEAD_SIZE // 2
+    sined = gradient * sine_lookup
+    return gradient * cosine_lookup + jnp.concatenate(
+        [sined[..., half_dim:], -sined[..., :half_dim]], -1
+    )
+
+
+def allowed_pairs(segment):
+    spots = jnp.arange(segment.shape[0])
+    return (spots[:, None] >= spots[None, :]) & (segment[:, None] == segment[None, :])
+
+
+def scores(query_rotated, key_rotated, segment):
+    raw_scores = jnp.einsum(
+        "qhgd,khd->hgqk", query_rotated, key_rotated, preferred_element_type=F32
+    ) * HEAD_SIZE ** (-0.5)
+    return jnp.where(allowed_pairs(segment), raw_scores, MASKED)
+
+
+def attend_forward(query_rotated, key_rotated, value_seq, segment):
+    masked = scores(query_rotated, key_rotated, segment)
+    row_peak = jnp.max(masked, axis=-1, keepdims=True)
+    log_total = row_peak + jnp.log(jnp.sum(jnp.exp(masked - row_peak), axis=-1, keepdims=True))
+    attention_probs = jnp.exp(masked - log_total).astype(BF16)
+    combined_heads = jnp.einsum(
+        "ojus,sov->uojv", attention_probs, value_seq, preferred_element_type=F32
+    )
+    return (combined_heads, log_total)
+
+
+def attend_backward(query_rotated, key_rotated, value_seq, segment, log_total, grad_heads):
+    masked = scores(query_rotated, key_rotated, segment)
+    attention_probs = jnp.exp(masked - log_total)
+    grad_probs = jnp.einsum("qhgd,khd->hgqk", grad_heads, value_seq, preferred_element_type=F32)
+    row_sum = jnp.sum(attention_probs * grad_probs, axis=-1, keepdims=True)
+    grad_raw = jnp.where(
+        allowed_pairs(segment), attention_probs * (grad_probs - row_sum), 0.0
+    ).astype(BF16)
+    factor = HEAD_SIZE ** (-0.5)
+    grad_query_rot = (
+        jnp.einsum("ojus,sov->uojv", grad_raw, key_rotated, preferred_element_type=F32) * factor
+    )
+    grad_key_rot = (
+        jnp.einsum("hgqk,qhgd->khd", grad_raw, query_rotated, preferred_element_type=F32) * factor
+    )
+    grad_value_rot = jnp.einsum(
+        "hgqk,qhgd->khd", attention_probs.astype(BF16), grad_heads, preferred_element_type=F32
+    )
+    return (grad_query_rot, grad_key_rot, grad_value_rot)
+
+
+def per_sequence(step, *fields):
+    results = [step(*[field[s] for field in fields]) for s in range(fields[0].shape[0])]
+    return [jnp.stack(parts) for parts in zip(*results)]
 
 
 def general_body(

time: 623 us -> 475 us (0.76); the launches traced: 612 us -> 474 us
  Pallas kernels: 247 us -> 431 us
  matrix products: 139 us -> 0 us
  waiting for transfers between devices: 76.3 us -> 0.02 us
  local copies, waits for them, and re-layouts: 59.1 us -> 6.88 us
  other arithmetic: 60 us -> 28.3 us
  starting transfers between devices: 28.9 us -> 7.47 us
    pallas_call x1 -> x2, Pallas kernels: 247 us -> 431 us  [the longest x1 233 us: middle(): pl.pallas_call(middle_kernel, out_shape=(jax.ShapeDtypeStruct((row_count,...]
    dot_general x25 -> x0, matrix products: 139 us -> none  [the longest x16 58.6 us: over_rows(): lax.dot_general(left_matrix, right_matrix, (((0,), (0,)), ((), ())), pref...]
    ppermute x20 -> x8, waiting for transfers between devices: 76.3 us -> 0.02 us  [swap(): return lax.ppermute(value, axis, [(i, i ^ bit) for i in range(size)])]
    convert_element_type x10 -> x2, other arithmetic: 32.7 us -> 3.47 us  [the longest x1 2.79 us: body(): half_of(cotangent, core).astype(F32)]
    ppermute x20 -> x8, starting transfers between devices: 28.9 us -> 7.47 us  [swap(): return lax.ppermute(value, axis, [(i, i ^ bit) for i in range(size)])]
    unnamed x137 -> x17, local copies, waits for them, and re-layouts: 19.3 us -> 3.09 us
    dynamic_slice x4 -> x0, local copies, waits for them, and re-layouts: 11.3 us -> none  [the longest x2 7.23 us: near(): lax.dynamic_index_in_dim(parts, which, 2, False)]
    reshape x4 -> x1, local copies, waits for them, and re-layouts: 10.8 us -> 1.54 us  [middle(): segment.reshape(row_count, 1)]
  transfers between devices with their start and end apart: 20 -> 8, of which waited for: 5 -> 0; matrix products, arithmetic and copies ran while one was open for 38% -> 5% of each run, Pallas kernels for 40% -> 0%
where the time goes in v3:
time: 475 us; the launch traced here: 474 us
  Pallas kernels  431 us (91%)
  other arithmetic  28.3 us (6%)
  starting transfers between devices  7.47 us (2%)
  local copies, waits for them, and re-layouts  6.88 us (1%)
    pallas_call x1, Pallas kernels, middle(): pl.pallas_call(middle_kernel, out_shape=(jax.ShapeDtypeStruct((row_count,...  233 us
    pallas_call x1, Pallas kernels, last(): pl.pallas_call(last_kernel, out_shape=(triple, triple, triple, out_block,...  198 us
  transfers between devices with their start and end apart: 8, of which 0 were waited for; matrix products, arithmetic and copies ran while one was open for 5% of the time, Pallas kernels for 0%

profile of v3, /device:TPU:0, one launch (start us, length us, event | category | flops | bytes accessed | tf_op | source)
XLA Modules:
  0.0 474.1 jit_solution(7901040078489741822)
XLA Ops:
  0.7 1.5 copy.25.segment_column_ref
  2.3 0.7 convert_element_type.23
  3.0 2.8 dynamic-slice_convert_fusion.cot_half_ref
  5.8 1.8 fusion
  7.6 232.5 %feed_forward.1 = (bf16[512,2048]{1,0:T(8,128)(2,1)}, bf16[512,512]{1,0:T(8,128)(2,1)}, bf16[512,512]{1,0:T(8,128)(2,1)}, bf16[512,512]{1,0:T(8,128)(2,1)}, bf16...) custom-call(bf16[2048,512]{1,0:T(8,128)(2,1)} %w_query_ref.3, ...), custom_call_target="tpu_custom_call" | custom-call | tf_op jit(solution)/shard_map/feed_forward/pallas_call | solution.py:741
  240.1 198.0 %weight_gradients.1 = (f32[3,256,2048]{2,1,0:T(8,128)}, f32[3,256,2048]{2,1,0:T(8,128)}, f32[3,256,2048]{2,1,0:T(8,128)}, f32[512,256]{1,0:T(8,128)}, f32[512,25...) custom-call(f32[6,256,2048]{2,1,0:T(8,128)} %get-tuple-element.40.no, ...), custom_call_target="tpu_custom_call" | custom-call | tf_op jit(solution)/shard_map/weight_gradients/pallas_call | solution.py:1253
  438.2 0.7 pad_maximum_fusion.2
  439.0 8.5 %add_bitcast_fusion = (f32[2048,256]{0,1:T(8,128)S(1)}, f32[256,2048]{1,0:T(8,128)}, f32[256,2048]{1,0:T(8,128)}) fusion(f32[3,256,2048]{2,1,0:T(8,128)} %get-tuple-element.64, f32[3,256,2048]{2,1,0:T(8,128)} %get-tuple-element.63), kind=kLoop, calls=%fused_computation.2 | loop fusion | flops 1572864 | bytes 18874368 | tf_op jit(solution)/shard_map/transpose | solution.py:1410
  447.5 2.5 broadcast_select_fusion.1
  450.0 1.3 copy-done.1
  451.3 1.5 select_convert_fusion.1
  452.8 1.6 collective-permute-start.2
  454.9 4.7 pad_maximum_fusion
  459.7 1.5 collective-permute-start.4
  461.6 2.7 pad_maximum_fusion.1
  464.3 1.5 add.108
  465.8 0.6 collective-permute-start.1
  466.4 1.6 collective-permute-start.3
  468.1 1.1 collective-permute-start.7
  469.2 0.7 fusion.9
  469.9 0.9 slice.45
  470.8 1.8 copy.26
  472.6 0.9 add.109
  473.5 0.6 fusion.10
  (35 shorter events, 1.2 us)
Async XLA Ops:
  438.9 13.9 %collective-permute-start = (f32[2,2048]{1,0:T(2,128)S(1)}, f32[2,2048]{1,0:T(2,128)S(1)}, u32[]{:S(2)}, u32[]{:S(2)}) collective-permute-start(f32[2,2048]{1,0:T(2,128)S(1)} %pad_maximum_fusion.2), channel_id=1, source_target_pairs={{0,1},{1,0},{2,3},{3,2},{4,5},{5,4},{6,7},{7,6},{8,9},{9,8},{10,11... | collective-permute-start | bytes 49160 | tf_op jit(solution)/shard_map/ppermute | solution.py:19
  439.0 8.5 %copy-start.2 = (f32[256,2048]{1,0:T(8,128)S(1)}, f32[256,2048]{1,0:T(8,128)}, u32[]{:S(2)}) copy-start(f32[256,2048]{1,0:T(8,128)} %get-tuple-element.55) | copy-start | bytes 6291460
  439.0 8.5 %copy-start.3 = (f32[256,2048]{1,0:T(8,128)S(1)}, f32[256,2048]{1,0:T(8,128)}, u32[]{:S(2)}) copy-start(f32[256,2048]{1,0:T(8,128)} %get-tuple-element.56) | copy-start | bytes 6291460
  447.5 2.5 copy-start
  447.5 3.7 copy-start.1
  451.3 1.5 copy-start.6
  451.3 1.5 copy-start.7
  452.8 8.3 %collective-permute-start.2 = (f32[2,256]{1,0:T(2,128)S(1)}, f32[2,256]{1,0:T(2,128)S(1)}, u32[]{:S(2)}, u32[]{:S(2)}) collective-permute-start(f32[2,256]{1,0:T(2,128)S(1)} %get-tuple-element.99), channel_id=1, source_target_pairs={{0,4},{4,0},{8,12},{12,8},{16,20},{20,16},{24,28},{28,24},{1,5},{5... | collective-permute-start | bytes 6152 | tf_op jit(solution)/shard_map/ppermute | solution.py:19
  454.4 6.8 %collective-permute-start.5 = (f32[2,256]{1,0:T(2,128)S(1)}, f32[2,256]{1,0:T(2,128)S(1)}, u32[]{:S(2)}, u32[]{:S(2)}) collective-permute-start(f32[2,256]{1,0:T(2,128)S(1)} %get-tuple-element.97), channel_id=1, source_target_pairs={{0,4},{4,0},{8,12},{12,8},{16,20},{20,16},{24,28},{28,24},{1,5},{5... | collective-permute-start | bytes 6152 | tf_op jit(solution)/shard_map/ppermute | solution.py:19
  459.7 8.4 %collective-permute-start.4 = (f32[2,256]{1,0:T(2,128)S(1)}, f32[2,256]{1,0:T(2,128)S(1)}, u32[]{:S(2)}, u32[]{:S(2)}) collective-permute-start(f32[2,256]{1,0:T(2,128)S(1)} %get-tuple-element.98), channel_id=1, source_target_pairs={{0,4},{4,0},{8,12},{12,8},{16,20},{20,16},{24,28},{28,24},{1,5},{5... | collective-permute-start | bytes 6152 | tf_op jit(solution)/shard_map/ppermute | solution.py:19
  461.2 6.9 %collective-permute-start.6 = (f32[2,256]{1,0:T(2,128)S(1)}, f32[2,256]{1,0:T(2,128)S(1)}, u32[]{:S(2)}, u32[]{:S(2)}) collective-permute-start(f32[2,256]{1,0:T(2,128)S(1)} %get-tuple-element.101), channel_id=1, source_target_pairs={{0,8},{4,12},{8,0},{12,4},{16,24},{20,28},{24,16},{28,20},{1,9},{5... | collective-permute-start | bytes 6152 | tf_op jit(solution)/shard_map/ppermute | solution.py:19
  465.8 7.7 %collective-permute-start.1 = (f32[2,256]{1,0:T(2,128)S(1)}, f32[2,256]{1,0:T(2,128)S(1)}, u32[]{:S(2)}, u32[]{:S(2)}) collective-permute-start(f32[2,256]{1,0:T(2,128)S(1)} %get-tuple-element.96), channel_id=1, source_target_pairs={{0,4},{4,0},{8,12},{12,8},{16,20},{20,16},{24,28},{28,24},{1,5},{5... | collective-permute-start | bytes 6152 | tf_op jit(solution)/shard_map/ppermute | solution.py:19
  466.4 7.0 %collective-permute-start.3 = (f32[2,256]{1,0:T(2,128)S(1)}, f32[2,256]{1,0:T(2,128)S(1)}, u32[]{:S(2)}, u32[]{:S(2)}) collective-permute-start(f32[2,256]{1,0:T(2,128)S(1)} %get-tuple-element.100), channel_id=1, source_target_pairs={{0,8},{4,12},{8,0},{12,4},{16,24},{20,28},{24,16},{28,20},{1,9},{5... | collective-permute-start | bytes 6152 | tf_op jit(solution)/shard_map/ppermute | solution.py:19
  468.1 5.4 %collective-permute-start.7 = (f32[2,256]{1,0:T(2,128)S(1)}, f32[2,256]{1,0:T(2,128)S(1)}, u32[]{:S(2)}, u32[]{:S(2)}) collective-permute-start(f32[2,256]{1,0:T(2,128)S(1)} %fusion.6), channel_id=1, source_target_pairs={{0,16},{4,20},{8,24},{12,28},{16,0},{20,4},{24,8},{28,12},{1,17},{... | collective-permute-start | bytes 6152 | tf_op jit(solution)/shard_map/ppermute | solution.py:19
  470.8 1.8 copy-start.4
  470.8 1.8 copy-start.5

commit v4 on v3

--- a/solution.py
+++ b/solution.py
@@ -51,7 +51,6 @@
     w_out_ref,
     tokens_ref,
     cot_ref,
-    cot_half_ref,
     gain_one_ref,
     gain_ref,
     w_gate_ref,
@@ -72,9 +71,7 @@
     grad_attn_out,
     projected_out,
     grad_attn_far,
-    projected_far,
-    mixed_half_out,
-    mixed_twin_out,
+    branch_out,
     normed_out,
     activation_out,
     grad_gate_out,
@@ -97,6 +94,8 @@
     mine,
     core_in,
     y_in,
+    product,
+    log_total_ref,
     local_sem,
     core_send,
     core_recv,
@@ -108,33 +107,37 @@
     n_recv,
     twin_send,
     twin_recv,
-    end_send,
-    end_recv,
     hidden_send,
     hidden_recv,
     far_send,
     far_recv,
-    log_total_ref,
 ):
     dp, tensor = lax.axis_index("dp"), lax.axis_index("tensor")
-    core = tensor % 2
+    core, y_bit = tensor % 2, (tensor // 2) % 2
+    z_low = (dp // 2) % 2
     twin_id = (dp, flip(tensor, 1))
     y_id = (dp, flip(tensor, 2))
     x_id = (flip(dp, 1), tensor)
     z_id = (flip(dp, 4), tensor)
     far_id = (flip(dp, 2), tensor)
     half, width = hidden.shape
+    run = half // 2
+    row_count = 2 * half
     hidden_units = gate_w.shape[1]
-    chunk = half // CHUNKS
-    my_row = pl.multiple_of(core * half, half)
-    twin_row = pl.multiple_of((1 - core) * half, half)
-    row_count = 2 * half
     query_width = w_query_ref.shape[1]
     tiles = width // TILE
+    chunk = half // CHUNKS
     transposed = (((1,), (1,)), ((), ()))
-    z_low = (dp // 2) % 2
+    everything = slice(None)
     heads = gg.at[:, pl.ds(0, query_width)]
     tok = gu
+    cot_half = mine.at[1]
+
+    def own_row(block, which):
+        return pl.multiple_of(block * half + which * run, run)
+
+    def own_chunk(k, which):
+        return own_row(k // 2, which) + (k % 2) * chunk
 
     def remote(src, dst, send, recv, device):
         return pltpu.make_async_remote_copy(
@@ -158,13 +161,27 @@
         "down": pltpu.make_async_copy(w_down_ref, down_w, local_sem.at[6]),
         "gate": pltpu.make_async_copy(w_gate_ref, gate_w, local_sem.at[7]),
         "cot": pltpu.make_async_copy(cot_ref, cot, local_sem.at[8]),
+        "cot_0": pltpu.make_async_copy(
+            cot_ref.at[pl.ds(own_row(0, core), run)], act.at[pl.ds(0, run)], local_sem.at[10]
+        ),
+        "cot_1": pltpu.make_async_copy(
+            cot_ref.at[pl.ds(own_row(1, core), run)], act.at[pl.ds(run, run)], local_sem.at[11]
+        ),
     }
-    for name in ("tok", "query", "key", "value", "w_out", "up", "down"):
+    for name in ("cot_0", "cot_1", "tok", "query", "key", "value", "w_out", "up", "down"):
         loads[name].start()
 
     barrier = pltpu.get_barrier_semaphore()
     for device in (twin_id, y_id, x_id, z_id, far_id):
         pl.semaphore_signal(barrier, inc=1, device_id=device, device_id_type=MESH)
+    loads["cot_0"].wait()
+    loads["cot_1"].wait()
+
+    def widen(i):
+        window = pl.ds(pl.multiple_of(i * ROWS, ROWS), ROWS)
+        cot_half[window, :] = act[window, :].astype(F32)
+
+    loop(half // ROWS, widen)
     pl.semaphore_wait(barrier, 5)
 
     def rows(k):
@@ -187,19 +204,43 @@
             twin_send.at[which, slot], twin_recv.at[which, slot], twin_id,
         )
 
-    def send_z(source, slots, k, send, recv):
-        from_z(source, slots, k, send, recv).start()
-        from_z(source, slots, k + 1, send, recv).start()
-
-    def relay(source, slots, k, send, recv):
-        for i in (k, k + 1):
-            from_z(source, slots, i, send, recv).wait_recv()
-            from_zx(slots, i, send, recv).start()
-            from_z(source, slots, i, send, recv).wait_send()
-
-    send_z(cot_half_ref, cot_others, 0, cot_send, cot_recv)
+    half_chunk = pl.ds(pl.multiple_of((2 + y_bit) * chunk, chunk), chunk)
+
+    def last_z():
+        return remote(
+            normed_sent.at[half_chunk], normed_others.at[1, half_chunk],
+            n_send.at[1, 2], n_recv.at[1, 2], z_id,
+        )
+
+    def last_y():
+        return remote(
+            normed_others.at[1, half_chunk], normed_others.at[1, half_chunk],
+            n_send.at[1, 3], n_recv.at[1, 3], y_id,
+        )
+
+    quarter = pl.ds(pl.multiple_of(y_bit * run, run), run)
+
+    def quarter_z():
+        return remote(
+            cot_half.at[quarter], cot_others.at[1, quarter],
+            cot_send.at[1, 0], cot_recv.at[1, 0], z_id,
+        )
+
+    def quarter_zx():
+        return remote(
+            cot_others.at[1, quarter], cot_others.at[2, quarter],
+            cot_send.at[2, 0], cot_recv.at[2, 0], x_id,
+        )
+
+    def quarter_y():
+        return remote(
+            cot_others.at[1, quarter], cot_others.at[1, quarter],
+            cot_send.at[1, 1], cot_recv.at[1, 1], y_id,
+        )
+
+    quarter_z().start()
     for k in range(CHUNKS):
-        from_x(cot_half_ref, cot_others, k, cot_send, cot_recv).start()
+        from_x(cot_half, cot_others, k, cot_send, cot_recv).start()
 
     def far_columns(b):
         return pl.ds(pl.multiple_of(b * 1024 + (1 - z_low) * 512, 512), 512)
@@ -217,22 +258,23 @@
     normed_one_store = pltpu.make_async_copy(normed, normed_one_out, local_sem.at[9])
     normed_one_store.start()
 
-    def stage_far(i):
-        window = pl.ds(pl.multiple_of(i * ROWS, ROWS), ROWS)
-        here = pl.ds(pl.multiple_of(my_row + i * ROWS, ROWS), ROWS)
-        for b in range(2):
-            core_in[2, window, pl.ds(b * 512, 512)] = normed[here, far_columns(b)].astype(F32)
-
-    loop(half // ROWS, stage_far)
-    early = pl.ds(0, 1024)
+    for block in range(2):
+
+        def stage_far(i, block=block):
+            window = pl.ds(pl.multiple_of(block * run + i * ROWS, ROWS), ROWS)
+            here = pl.ds(pl.multiple_of(own_row(block, core) + i * ROWS, ROWS), ROWS)
+            for b in range(2):
+                core_in[2, window, pl.ds(b * 512, 512)] = normed[here, far_columns(b)].astype(F32)
+
+        loop(run // ROWS, stage_far)
     normed_one_copy = remote(
-        core_in.at[2, :, early], normed_one_far.at[0], far_send.at[0], far_recv.at[0], far_id
+        core_in.at[2, :, pl.ds(0, 1024)], normed_one_far.at[0],
+        far_send.at[0], far_recv.at[0], far_id,
     )
     normed_one_copy.start()
 
     lane = lax.broadcasted_iota(jnp.int32, (TILE, 128), 1)
     factor = HEAD_SIZE ** (-0.5)
-    everything = slice(None)
 
     def turn(value):
         return jnp.where(lane % 64 < 32, pltpu.roll(value, 96, 1), pltpu.roll(value, 32, 1))
@@ -243,12 +285,10 @@
     def unrotate_tile(value, window):
         return value * cosine_ref[window, :] + turn(value) * sine_ref[window, :]
 
-    for name in ("query", "key", "value"):
-        loads[name].wait()
-    for block in range(2):
+    def project_in(block):
         window = pl.ds(block * TILE, TILE)
 
-        def query_tile(j, window=window):
+        def query_tile(j):
             projection = jnp.dot(
                 normed[window, :],
                 gate_w[:, pl.ds(pl.multiple_of(j * TILE, TILE), TILE)],
@@ -276,15 +316,6 @@
             )
             for i, padded in enumerate(halves_of):
                 act[window, pl.ds(base + i * 128, 128)] = padded.astype(BF16)
-    normed_one_store.wait()
-    loads["gate"].start()
-    keeps = [
-        pltpu.make_async_copy(act.at[:, pl.ds(0, 512)], query_ref, local_sem.at[0]),
-        pltpu.make_async_copy(act.at[:, pl.ds(1024, 512)], keys_ref, local_sem.at[1]),
-        pltpu.make_async_copy(act.at[:, pl.ds(1536, 512)], values_ref, local_sem.at[2]),
-    ]
-    for keep in keeps:
-        keep.start()
 
     def allowed_of(block):
         keys_seen = (block + 1) * TILE
@@ -295,49 +326,32 @@
             segment_column_ref[pl.ds(0, keys_seen), :] == segment_row_ref[:, window]
         )
 
-    def forward_pair(p):
+    def attend(block, p):
         kv = p // 2
         column = pl.multiple_of(p * 128, 128)
-        for block in range(2):
-            window = pl.ds(block * TILE, TILE)
-            seen = pl.ds(0, (block + 1) * TILE)
-            queries = act[window, pl.ds(column, 128)]
-            allowed = allowed_of(block)
-            result = jnp.zeros((TILE, 128), F32)
-            for side in range(2):
-                padded = pl.multiple_of((kv * 2 + side) * 128, 128)
-                keys = act[seen, pl.ds(pl.multiple_of(1024 + padded, 128), 128)]
-                vals = act[seen, pl.ds(pl.multiple_of(1536 + padded, 128), 128)]
-                raw = jnp.where(
-                    allowed,
-                    lax.dot_general(keys, queries, transposed, preferred_element_type=F32)
-                    * factor,
-                    MASKED,
-                )
-                peak = jnp.max(raw, axis=0, keepdims=True)
-                lifted = jnp.exp(raw - peak)
-                summed = jnp.sum(lifted, axis=0, keepdims=True)
-                log_total_ref[pl.ds(2 * p + side, 1), window] = peak + jnp.log(summed)
-                result = result + lax.dot_general(
-                    (lifted * (1.0 / summed)).astype(BF16), vals, (((0,), (0,)), ((), ())),
-                    preferred_element_type=F32,
-                )
-            heads[window, pl.ds(column, 128)] = result.astype(BF16)
-
-    loop(4, forward_pair)
-    heads_store = pltpu.make_async_copy(heads, heads_out, local_sem.at[3])
-    heads_store.start()
-
-    loads["w_out"].wait()
-
-    def project(into, first_row):
-        def step(j):
-            columns = pl.ds(pl.multiple_of(j * TILE, TILE), TILE)
-            into[:, columns] = jnp.dot(
-                heads[pl.ds(first_row, half), :], cot[:, columns], preferred_element_type=F32
+        window = pl.ds(block * TILE, TILE)
+        seen = pl.ds(0, (block + 1) * TILE)
+        queries = act[window, pl.ds(column, 128)]
+        allowed = allowed_of(block)
+        result = jnp.zeros((TILE, 128), F32)
+        for side in range(2):
+            padded = pl.multiple_of((kv * 2 + side) * 128, 128)
+            keys = act[seen, pl.ds(pl.multiple_of(1024 + padded, 128), 128)]
+            vals = act[seen, pl.ds(pl.multiple_of(1536 + padded, 128), 128)]
+            raw = jnp.where(
+                allowed,
+                lax.dot_general(keys, queries, transposed, preferred_element_type=F32) * factor,
+                MASKED,
             )
-
-        loop(width // TILE, step)
+            peak = jnp.max(raw, axis=0, keepdims=True)
+            lifted = jnp.exp(raw - peak)
+            summed = jnp.sum(lifted, axis=0, keepdims=True)
+            log_total_ref[pl.ds(2 * p + side, 1), window] = peak + jnp.log(summed)
+            result = result + lax.dot_general(
+                (lifted * (1.0 / summed)).astype(BF16), vals, (((0,), (0,)), ((), ())),
+                preferred_element_type=F32,
+            )
+        heads[window, pl.ds(column, 128)] = result.astype(BF16)
 
     def core_copy(which, window, k):
         return remote(
@@ -347,155 +361,172 @@
 
     def y_copy(which, window, k):
         return remote(
-            mine.at[which % 2].at[window], y_in.at[which % 2].at[window],
+            mine.at[which].at[window], y_in.at[which].at[window],
             y_send.at[which, k], y_recv.at[which, k], y_id,
         )
 
+    def split_tile(which, block, columns, value):
+        product[...] = value
+        local = pl.ds(block * run, run)
+        away[local, columns] = product[pl.ds(pl.multiple_of((1 - core) * run, run), run), :]
+        mine[which, local, columns] = product[pl.ds(pl.multiple_of(core * run, run), run), :]
+
     row_windows = [(rows(k), everything) for k in range(CHUNKS)]
 
-    def column_window(j):
-        return (everything, pl.ds(pl.multiple_of(j * TILE, TILE), TILE))
-
-    project(away, twin_row)
-    for k in range(CHUNKS):
-        core_copy(0, row_windows[k], k).start()
-    project(mine.at[0], my_row)
+    def tile_of(j):
+        return pl.ds(pl.multiple_of(j * TILE, TILE), TILE)
+
+    for name in ("query", "key", "value", "w_out"):
+        loads[name].wait()
+    for block in range(2):
+        project_in(block)
+        loop(query_width // 128, functools.partial(attend, block))
+
+        def project(j, block=block):
+            split_tile(0, block, tile_of(j), jnp.dot(
+                heads[pl.ds(block * TILE, TILE), :], cot[:, tile_of(j)],
+                preferred_element_type=F32,
+            ))
+
+        loop(tiles, project)
+        for k in (2 * block, 2 * block + 1):
+            core_copy(0, row_windows[k], k).start()
+        for k in (2 * block, 2 * block + 1):
+            core_copy(0, row_windows[k], k).wait_recv()
+
+            def add(i, k=k):
+                window = pl.ds(pl.multiple_of(k * chunk + i * ROWS, ROWS), ROWS)
+                mine[0, window, :] = mine[0, window, :] + core_in[0, window, :]
+
+            loop(chunk // ROWS, add)
+            y_copy(0, row_windows[k], k).start()
+    normed_one_store.wait()
+    loads["gate"].start()
     loads["cot"].start()
-    for k in range(CHUNKS):
-        core_copy(0, row_windows[k], k).wait_recv()
-
-        def add(i, k=k):
-            window = pl.ds(pl.multiple_of(k * chunk + i * ROWS, ROWS), ROWS)
-            mine[0, window, :] = mine[0, window, :] + core_in[0, window, :]
-
-        loop(chunk // ROWS, add)
-        y_copy(0, row_windows[k], k).start()
+    keeps = [
+        pltpu.make_async_copy(act.at[:, pl.ds(0, 512)], query_ref, local_sem.at[0]),
+        pltpu.make_async_copy(act.at[:, pl.ds(1024, 512)], keys_ref, local_sem.at[1]),
+        pltpu.make_async_copy(act.at[:, pl.ds(1536, 512)], values_ref, local_sem.at[2]),
+        pltpu.make_async_copy(heads, heads_out, local_sem.at[3]),
+    ]
+    for keep in keeps:
+        keep.start()
 
     def stage_heads(i):
         window = pl.ds(pl.multiple_of(i * ROWS, ROWS), ROWS)
         for b in range(2):
             here = pl.ds(pl.multiple_of(b * half + i * ROWS, ROWS), ROWS)
-            mine[1, window, pl.ds(b * 512, 512)] = heads[here, :].astype(F32)
+            core_in[2, window, pl.ds(1024 + b * 512, 512)] = heads[here, :].astype(F32)
 
     loop(half // ROWS, stage_heads)
     heads_copy = remote(
-        mine.at[1, :, early], heads_far, far_send.at[1], far_recv.at[1], far_id
+        core_in.at[2, :, pl.ds(1024, 1024)], heads_far, far_send.at[1], far_recv.at[1], far_id
     )
     heads_copy.start()
+    for keep in keeps:
+        keep.wait()
+
+    for name in ("cot", "up", "down"):
+        loads[name].wait()
+
+    def activation_grad(j):
+        gg[:, tile_of(j)] = lax.dot_general(
+            cot[...], down_w[tile_of(j), :], transposed, preferred_element_type=F32
+        ).astype(BF16)
+
+    loop(hidden_units // TILE, activation_grad)
+    loads["gate"].wait()
     gain = gain_ref[...]
-    for k in range(CHUNKS):
-        y_copy(0, row_windows[k], k).wait_recv()
-
-        def normalize_rows(i, k=k):
-            offset = pl.multiple_of(k * chunk + i * ROWS, ROWS)
-            window = pl.ds(offset, ROWS)
-            own = tok[pl.ds(pl.multiple_of(my_row + offset, ROWS), ROWS), :].astype(F32)
-            values = own + (mine[0, window, :] + y_in[0, window, :])
-            scale = lax.rsqrt(jnp.mean(values * values, axis=-1, keepdims=True) + EPSILON)
-            rounded = (values * scale * gain).astype(BF16)
-            hidden[window, :] = values
-            normed[pl.ds(pl.multiple_of(my_row + offset, ROWS), ROWS), :] = rounded
-            normed_sent[window, :] = rounded.astype(F32)
-
-        loop(chunk // ROWS, normalize_rows)
-        remote(
+
+    def twin_copy(k):
+        return remote(
             normed_sent.at[rows(k)], normed_twin.at[rows(k)],
             n_send.at[3, k], n_recv.at[3, k], twin_id,
-        ).start()
-        if k == 2:
-            relay(cot_half_ref, cot_others, 0, cot_send, cot_recv)
-            send_z(cot_half_ref, cot_others, 2, cot_send, cot_recv)
-        from_x(normed_sent, normed_others, k, n_send, n_recv).start()
-    for k in range(CHUNKS):
-        remote(
-            normed_sent.at[rows(k)], normed_twin.at[rows(k)],
-            n_send.at[3, k], n_recv.at[3, k], twin_id,
-        ).wait_recv()
-
-        def take(i, k=k):
-            offset = pl.multiple_of(k * chunk + i * ROWS, ROWS)
-            normed[pl.ds(pl.multiple_of(twin_row + offset, ROWS), ROWS), :] = normed_twin[
-                pl.ds(offset, ROWS), :
-            ].astype(BF16)
-
-        loop(chunk // ROWS, take)
-
-    for name in ("cot", "gate", "up", "down"):
-        loads[name].wait()
-    for keep in keeps + [heads_store]:
-        keep.wait()
-
-    def units(j):
-        columns = pl.ds(pl.multiple_of(j * TILE, TILE), TILE)
-        gate = jnp.dot(normed[...], gate_w[:, columns], preferred_element_type=F32)
-        up = jnp.dot(normed[...], up_w[:, columns], preferred_element_type=F32)
-        back = lax.dot_general(
-            cot[...], down_w[columns, :], (((1,), (1,)), ((), ())), preferred_element_type=F32
         )
-        sigmoid = jax.nn.sigmoid(gate)
-        swish = gate * sigmoid
-        act[:, columns] = (swish * up).astype(BF16)
-        gg[:, columns] = (back * up * sigmoid * (1.0 + gate * (1.0 - sigmoid))).astype(BF16)
-        gu[:, columns] = (back * swish).astype(BF16)
-
-    loop(hidden_units // TILE, units)
-
-    for k in range(CHUNKS):
-        core_copy(0, row_windows[k], k).wait_send()
-    normed_one_copy.wait()
-    heads_copy.wait()
-    normed_one_twin = remote(
-        normed_one_far.at[0], normed_one_far.at[1], far_send.at[2], far_recv.at[2], twin_id
-    )
-    normed_one_twin.start()
-
-    def column_sums(which, tile_product, forwarded=True):
-        def produce(j):
-            value = tile_product(j)
-            columns = pl.ds(pl.multiple_of(j * TILE, TILE), TILE)
-            away[:, columns] = value[0]
-            mine[which % 2, :, columns] = value[1]
-            core_copy(which, column_window(j), j).start()
-
-        def forward(j):
-            core_copy(which, column_window(j), j).wait_recv()
-            columns = pl.ds(pl.multiple_of(j * TILE, TILE), TILE)
-            mine[which % 2, :, columns] = (
-                mine[which % 2, :, columns] + core_in[which, :, columns]
-            )
-            if forwarded:
-                y_copy(which, column_window(j), j).start()
-
-        produce(0)
-
-        def step(j):
+
+    def block_window(block, j):
+        return (pl.ds(block * run, run), tile_of(j))
+
+    for block in range(2):
+        chunks = (2 * block, 2 * block + 1)
+        for k in chunks:
+            y_copy(0, row_windows[k], k).wait_recv()
+
+            def normalize_rows(i, k=k):
+                window = pl.ds(pl.multiple_of(k * chunk + i * ROWS, ROWS), ROWS)
+                here = pl.ds(pl.multiple_of(own_chunk(k, core) + i * ROWS, ROWS), ROWS)
+                values = tok[here, :].astype(F32) + (mine[0, window, :] + y_in[0, window, :])
+                scale = lax.rsqrt(jnp.mean(values * values, axis=-1, keepdims=True) + EPSILON)
+                rounded = (values * scale * gain).astype(BF16)
+                hidden[window, :] = values
+                normed[here, :] = rounded
+                normed_sent[window, :] = rounded.astype(F32)
+
+            loop(chunk // ROWS, normalize_rows)
+            twin_copy(k).start()
+            if block == 0:
+                from_z(normed_sent, normed_others, k, n_send, n_recv).start()
+            elif k == 3:
+                last_z().start()
+            from_x(normed_sent, normed_others, k, n_send, n_recv).start()
+        for k in chunks:
+            twin_copy(k).wait_recv()
+
+            def take(i, k=k):
+                here = pl.ds(pl.multiple_of(own_chunk(k, 1 - core) + i * ROWS, ROWS), ROWS)
+                normed[here, :] = normed_twin[
+                    pl.ds(pl.multiple_of(k * chunk + i * ROWS, ROWS), ROWS), :
+                ].astype(BF16)
+
+            loop(chunk // ROWS, take)
+        window = pl.ds(block * TILE, TILE)
+
+        def units(j, window=window):
+            columns = tile_of(j)
+            gate = jnp.dot(normed[window, :], gate_w[:, columns], preferred_element_type=F32)
+            up = jnp.dot(normed[window, :], up_w[:, columns], preferred_element_type=F32)
+            back = gg[window, columns].astype(F32)
+            sigmoid = jax.nn.sigmoid(gate)
+            swish = gate * sigmoid
+            act[window, columns] = (swish * up).astype(BF16)
+            gg[window, columns] = (
+                back * up * sigmoid * (1.0 + gate * (1.0 - sigmoid))
+            ).astype(BF16)
+            gu[window, columns] = (back * swish).astype(BF16)
+
+        if block == 0:
+            loop(hidden_units // TILE, units)
+            quarter_z().wait()
+            quarter_zx().start()
+            for k in range(CHUNKS):
+                from_x(cot_half, cot_others, k, cot_send, cot_recv).wait_send()
+                core_copy(0, row_windows[k], k).wait_send()
+        else:
+            loop(hidden_units // TILE, units)
+            normed_one_copy.wait()
+            heads_copy.wait()
+
+        def produce(j, block=block, window=window):
+            split_tile(1, block, tile_of(j), lax.dot_general(
+                gg[window, :], gate_w[tile_of(j), :], transposed, preferred_element_type=F32
+            ) + lax.dot_general(
+                gu[window, :], up_w[tile_of(j), :], transposed, preferred_element_type=F32
+            ))
+            core_copy(1, block_window(block, j), block * tiles + j).start()
+
+        def forward(j, block=block):
+            where = block_window(block, j)
+            core_copy(1, where, block * tiles + j).wait_recv()
+            mine[(1,) + where] = mine[(1,) + where] + core_in[(1,) + where]
+            y_copy(1, where, block * tiles + j).start()
+
+        def step(j, produce=produce, forward=forward):
             produce(j + 1)
             forward(j)
 
+        produce(0)
         loop(tiles - 1, step)
         forward(tiles - 1)
-
-    def halves(dot_of):
-        return dot_of(pl.ds(twin_row, half)), dot_of(pl.ds(my_row, half))
-
-    def back_tile(j):
-        columns = pl.ds(pl.multiple_of(j * TILE, TILE), TILE)
-        return halves(
-            lambda part: lax.dot_general(
-                gg[part, :], gate_w[columns, :], transposed, preferred_element_type=F32
-            )
-            + lax.dot_general(
-                gu[part, :], up_w[columns, :], transposed, preferred_element_type=F32
-            )
-        )
-
-    def branch_tile(j):
-        columns = pl.ds(pl.multiple_of(j * TILE, TILE), TILE)
-        return halves(
-            lambda part: jnp.dot(act[part, :], down_w[:, columns], preferred_element_type=F32)
-        )
-
-    column_sums(1, back_tile)
     stores = [
         pltpu.make_async_copy(normed, normed_out, local_sem.at[7]),
         pltpu.make_async_copy(act, activation_out, local_sem.at[8]),
@@ -504,16 +535,44 @@
     ]
     for store in stores:
         store.start()
-    relay(cot_half_ref, cot_others, 2, cot_send, cot_recv)
-    send_z(normed_sent, normed_others, 0, n_send, n_recv)
-    loop(tiles, lambda j: core_copy(1, column_window(j), j).wait_send())
+    normed_one_twin = remote(
+        normed_one_far.at[0], normed_one_far.at[1], far_send.at[2], far_recv.at[2], twin_id
+    )
+    normed_one_twin.start()
+
+    for block in range(2):
+        loop(tiles, lambda j: core_copy(1, block_window(block, j), block * tiles + j).wait_send())
     for k in range(CHUNKS):
         y_copy(0, row_windows[k], k).wait_send()
-    column_sums(2, branch_tile, forwarded=False)
-    for k in range(CHUNKS):
-        from_x(cot_half_ref, cot_others, k, cot_send, cot_recv).wait_recv()
-    to_twin(cot_others, 0, 0).start()
-    to_twin(cot_others, 0, 1).start()
+
+    def branch_produce(j):
+        for block in range(2):
+            split_tile(0, block, tile_of(j), jnp.dot(
+                act[pl.ds(block * TILE, TILE), :], down_w[:, tile_of(j)],
+                preferred_element_type=F32,
+            ))
+        core_copy(2, (everything, tile_of(j)), j).start()
+
+    def branch_add(j):
+        core_copy(2, (everything, tile_of(j)), j).wait_recv()
+        mine[0, :, tile_of(j)] = mine[0, :, tile_of(j)] + core_in[2, :, tile_of(j)]
+
+    def branch_step(j):
+        branch_produce(j + 1)
+        branch_add(j)
+
+    branch_produce(0)
+    loop(tiles - 1, branch_step)
+    branch_add(tiles - 1)
+    first_y = (1 - y_bit).astype(F32)
+
+    def add_hidden(i):
+        window = pl.ds(pl.multiple_of(i * ROWS, ROWS), ROWS)
+        mine[0, window, :] = mine[0, window, :] + hidden[window, :] * first_y
+
+    loop(half // ROWS, add_hidden)
+    branch_store = pltpu.make_async_copy(mine.at[0], branch_out, local_sem.at[12])
+    branch_store.start()
 
     for store in stores:
         store.wait()
@@ -525,10 +584,18 @@
     ]
     for operand in operands:
         operand.start()
-
-    loop(tiles, lambda j: y_copy(1, column_window(j), j).wait_recv())
-    loop(tiles, lambda j: y_copy(2, column_window(j), j).start())
+    for k in (0, 1):
+        from_z(normed_sent, normed_others, k, n_send, n_recv).wait_recv()
+        from_zx(normed_others, k, n_send, n_recv).start()
+    for k in range(CHUNKS):
+        from_x(cot_half, cot_others, k, cot_send, cot_recv).wait_recv()
+    to_twin(cot_others, 0, 0).start()
+    for operand in operands:
+        operand.wait()
+
     gain_out[...] = jnp.zeros_like(gain_out)
+    sums = y_in.at[0]
+    sums[:, pl.ds(0, 1024)] = jnp.zeros((TILE, 1024), F32)
 
     def hidden_copy(k):
         return remote(
@@ -536,66 +603,13 @@
             hidden_send.at[k], hidden_recv.at[k], twin_id,
         )
 
-    for k in range(CHUNKS):
-
-        def norm_rows(i, k=k):
-            offset = pl.multiple_of(k * chunk + i * ROWS, ROWS)
-            window = pl.ds(offset, ROWS)
-            incoming = mine[1, window, :] + y_in[1, window, :]
-            values = hidden[window, :]
-            scale = lax.rsqrt(jnp.mean(values * values, axis=-1, keepdims=True) + EPSILON)
-            weighted = incoming * gain
-            inner = jnp.mean(weighted * values, axis=-1, keepdims=True)
-            back = scale * weighted - values * (scale * scale * scale) * inner
-            here = pl.ds(pl.multiple_of(my_row + offset, ROWS), ROWS)
-            total = cot[here, :].astype(F32) + back
-            core_in[0, window, :] = total
-            normed[here, :] = total.astype(BF16)
-            gain_out[...] = gain_out[...] + jnp.sum(
-                incoming * values * scale, axis=0, keepdims=True
-            )
-
-        loop(chunk // ROWS, norm_rows)
-        hidden_copy(k).start()
-    hidden_store = pltpu.make_async_copy(core_in.at[0], grad_hidden_out, local_sem.at[4])
-    hidden_store.start()
-    relay(normed_sent, normed_others, 0, n_send, n_recv)
-    send_z(normed_sent, normed_others, 2, n_send, n_recv)
-    for k in range(CHUNKS):
-        hidden_copy(k).wait_recv()
-
-        def take_hidden(i, k=k):
-            offset = pl.multiple_of(k * chunk + i * ROWS, ROWS)
-            normed[pl.ds(pl.multiple_of(twin_row + offset, ROWS), ROWS), :] = normed_twin[
-                pl.ds(offset, ROWS), :
-            ].astype(BF16)
-
-        loop(chunk // ROWS, take_hidden)
-    grad_attn_store = pltpu.make_async_copy(normed, grad_attn_out, local_sem.at[5])
-    grad_attn_store.start()
-
-    hidden_far = [
-        remote(
-            core_in.at[0, :, far_columns(b)], grad_attn_far.at[0, :, pl.ds(b * 512, 512)],
-            far_send.at[3 + b], far_recv.at[3 + b], far_id,
+    def hidden_far(block, b):
+        local = pl.ds(block * run, run)
+        return remote(
+            core_in.at[0, local, far_columns(b)],
+            grad_attn_far.at[0, local, pl.ds(b * 512, 512)],
+            far_send.at[3 + 2 * block + b], far_recv.at[3 + 2 * block + b], far_id,
         )
-        for b in range(2)
-    ]
-    for copy in hidden_far:
-        copy.start()
-
-    for operand in operands:
-        operand.wait()
-
-    def head_tile(j):
-        columns = pl.ds(pl.multiple_of(j * TILE, TILE), TILE)
-        act[:, pl.ds(pl.multiple_of(512 + j * TILE, TILE), TILE)] = lax.dot_general(
-            normed[...], gate_w[columns, :], transposed, preferred_element_type=F32
-        ).astype(BF16)
-
-    loop(512 // TILE, head_tile)
-    sums = y_in.at[1]
-    sums[:, pl.ds(0, 1024)] = jnp.zeros((TILE, 1024), F32)
 
     def gather_into(offset, kv, value):
         for part in range(value.shape[0] // TILE):
@@ -603,48 +617,94 @@
             sums[:, columns] = sums[:, columns] + value[part * TILE : (part + 1) * TILE]
 
     def put(block, column, value):
-        rounded = value.astype(BF16)
-        gu[pl.ds(block * TILE, TILE), pl.ds(column, 128)] = rounded
-        core_in[1, :, pl.ds(block * 768 + column, 128)] = rounded.astype(F32)
-
-    def pair(p):
+        gu[pl.ds(block * TILE, TILE), pl.ds(column, 128)] = value.astype(BF16)
+
+    def attend_back(block, p):
         kv = p // 2
         column = pl.multiple_of(p * 128, 128)
-        for block in range(2):
-            keys_seen = (block + 1) * TILE
+        keys_seen = (block + 1) * TILE
+        window = pl.ds(block * TILE, TILE)
+        seen = pl.ds(0, keys_seen)
+        queries = act[window, pl.ds(column, 128)]
+        upstream = act[window, pl.ds(pl.multiple_of(512 + column, 128), 128)]
+        allowed = allowed_of(block)
+        query_grad = jnp.zeros((TILE, 128), F32)
+        for side in range(2):
+            padded = pl.multiple_of((kv * 2 + side) * 128, 128)
+            keys = act[seen, pl.ds(pl.multiple_of(1024 + padded, 128), 128)]
+            vals = act[seen, pl.ds(pl.multiple_of(1536 + padded, 128), 128)]
+            raw = lax.dot_general(keys, queries, transposed, preferred_element_type=F32) * factor
+            log_total = log_total_ref[pl.ds(2 * p + side, 1), window]
+            probs = jnp.exp(jnp.where(allowed, raw - log_total, MASKED))
+            grad_probs = lax.dot_general(
+                vals, upstream, transposed, preferred_element_type=F32
+            )
+            row_sum = jnp.sum(probs * grad_probs, axis=0, keepdims=True)
+            grad_raw = (probs * (grad_probs - row_sum)).astype(BF16)
+            query_grad = query_grad + lax.dot_general(
+                grad_raw, keys, (((0,), (0,)), ((), ())), preferred_element_type=F32
+            )
+            own = (lax.broadcasted_iota(jnp.int32, (keys_seen, 128), 1) // 64) == side
+            gather_into(0, kv, jnp.where(
+                own, jnp.dot(grad_raw, queries, preferred_element_type=F32), 0.0
+            ))
+            gather_into(512, kv, jnp.where(
+                own, jnp.dot(probs.astype(BF16), upstream, preferred_element_type=F32), 0.0
+            ))
+        put(block, column, unrotate_tile(query_grad * factor, window))
+
+    for block in range(2):
+        loop(tiles, lambda j: y_copy(1, block_window(block, j), block * tiles + j).wait_recv())
+        if block == 1:
+            quarter_y().start()
+        for k in (2 * block, 2 * block + 1):
+
+            def norm_rows(i, k=k):
+                window = pl.ds(pl.multiple_of(k * chunk + i * ROWS, ROWS), ROWS)
+                here = pl.ds(pl.multiple_of(own_chunk(k, core) + i * ROWS, ROWS), ROWS)
+                incoming = mine[1, window, :] + y_in[1, window, :]
+                values = hidden[window, :]
+                scale = lax.rsqrt(jnp.mean(values * values, axis=-1, keepdims=True) + EPSILON)
+                weighted = incoming * gain
+                inner = jnp.mean(weighted * values, axis=-1, keepdims=True)
+                back = scale * weighted - values * (scale * scale * scale) * inner
+                total = cot[here, :].astype(F32) + back
+                core_in[0, window, :] = total
+                normed[here, :] = total.astype(BF16)
+                gain_out[...] = gain_out[...] + jnp.sum(
+                    incoming * values * scale, axis=0, keepdims=True
+                )
+
+            loop(chunk // ROWS, norm_rows)
+            hidden_copy(k).start()
+        for b in range(2):
+            hidden_far(block, b).start()
+        for k in (2 * block, 2 * block + 1):
+            hidden_copy(k).wait_recv()
+
+            def take_hidden(i, k=k):
+                here = pl.ds(pl.multiple_of(own_chunk(k, 1 - core) + i * ROWS, ROWS), ROWS)
+                normed[here, :] = normed_twin[
+                    pl.ds(pl.multiple_of(k * chunk + i * ROWS, ROWS), ROWS), :
+                ].astype(BF16)
+
+            loop(chunk // ROWS, take_hidden)
+
+        def head_tile(j, block=block):
             window = pl.ds(block * TILE, TILE)
-            seen = pl.ds(0, keys_seen)
-            queries = act[window, pl.ds(column, 128)]
-            upstream = act[window, pl.ds(pl.multiple_of(512 + column, 128), 128)]
-            allowed = allowed_of(block)
-            query_grad = jnp.zeros((TILE, 128), F32)
-            for side in range(2):
-                padded = pl.multiple_of((kv * 2 + side) * 128, 128)
-                keys = act[seen, pl.ds(pl.multiple_of(1024 + padded, 128), 128)]
-                vals = act[seen, pl.ds(pl.multiple_of(1536 + padded, 128), 128)]
-                raw = lax.dot_general(
-                    keys, queries, transposed, preferred_element_type=F32
-                ) * factor
-                log_total = log_total_ref[pl.ds(2 * p + side, 1), window]
-                probs = jnp.exp(jnp.where(allowed, raw - log_total, MASKED))
-                grad_probs = lax.dot_general(
-                    vals, upstream, transposed, preferred_element_type=F32
-                )
-                row_sum = jnp.sum(probs * grad_probs, axis=0, keepdims=True)
-                grad_raw = (probs * (grad_probs - row_sum)).astype(BF16)
-                query_grad = query_grad + lax.dot_general(
-                    grad_raw, keys, (((0,), (0,)), ((), ())), preferred_element_type=F32
-                )
-                own = (lax.broadcasted_iota(jnp.int32, (keys_seen, 128), 1) // 64) == side
-                gather_into(0, kv, jnp.where(
-                    own, jnp.dot(grad_raw, queries, preferred_element_type=F32), 0.0
-                ))
-                gather_into(512, kv, jnp.where(
-                    own, jnp.dot(probs.astype(BF16), upstream, preferred_element_type=F32), 0.0
-                ))
-            put(block, column, unrotate_tile(query_grad * factor, window))
-
-    loop(4, pair)
+            act[window, pl.ds(pl.multiple_of(512 + j * TILE, TILE), TILE)] = lax.dot_general(
+                normed[window, :], gate_w[tile_of(j), :], transposed, preferred_element_type=F32
+            ).astype(BF16)
+
+        loop(512 // TILE, head_tile)
+        loop(query_width // 128, functools.partial(attend_back, block))
+
+    grad_stores = [
+        pltpu.make_async_copy(core_in.at[0], grad_hidden_out, local_sem.at[4]),
+        pltpu.make_async_copy(normed, grad_attn_out, local_sem.at[5]),
+    ]
+    for store in grad_stores:
+        store.start()
 
     def both(offset, block):
         def folded(kv):
@@ -662,70 +722,44 @@
     )
     projected_store.start()
 
-    projected_copy = remote(
-        core_in.at[1, :, pl.ds(0, 1536)], projected_far, far_send.at[5], far_recv.at[5], far_id
-    )
-    projected_copy.start()
-    for copy in hidden_far:
-        copy.wait_recv()
+    last_z().wait()
+    last_y().start()
+    for block in range(2):
+        for b in range(2):
+            hidden_far(block, b).wait()
     hidden_far_twin = remote(
         grad_attn_far.at[0], grad_attn_far.at[1], far_send.at[7], far_recv.at[7], twin_id
     )
     hidden_far_twin.start()
-
     for k in range(CHUNKS):
         from_x(normed_sent, normed_others, k, n_send, n_recv).wait_recv()
     to_twin(normed_others, 1, 0).start()
-    for k in range(CHUNKS):
-        from_zx(cot_others, k, cot_send, cot_recv).wait_recv()
-    to_twin(cot_others, 0, 2).start()
-    relay(normed_sent, normed_others, 2, n_send, n_recv)
+    quarter_y().wait()
+    to_twin(cot_others, 0, 1).start()
+    last_y().wait()
     to_twin(normed_others, 1, 1).start()
 
-    loop(tiles, lambda j: y_copy(2, column_window(j), j).wait_recv())
-    loop(tiles, lambda j: y_copy(2, column_window(j), j).wait_send())
-
-    def mixed_rows(i):
-        window = pl.ds(pl.multiple_of(i * ROWS, ROWS), ROWS)
-        mine[0, window, :] = hidden[window, :] + (mine[0, window, :] + y_in[0, window, :])
-
-    loop(half // ROWS, mixed_rows)
-    mixed_copy = remote(
-        mine.at[0], mixed_twin_out, end_send.at[1], end_recv.at[1], twin_id
-    )
-    mixed_copy.start()
-    mixed_store = pltpu.make_async_copy(mine.at[0], mixed_half_out, local_sem.at[12])
-    mixed_store.start()
-    for k in range(CHUNKS):
-        from_zx(normed_others, k, n_send, n_recv).wait_recv()
-    to_twin(normed_others, 1, 2).start()
-
-    for store in (hidden_store, grad_attn_store, projected_store, mixed_store):
+    for store in grad_stores + [projected_store, branch_store]:
         store.wait()
-    mixed_copy.wait()
-    for copy in hidden_far:
-        copy.wait_send()
-    for copy in (hidden_far_twin, normed_one_twin, projected_copy):
+    for copy in (hidden_far_twin, normed_one_twin, quarter_zx()):
         copy.wait()
     for k in range(CHUNKS):
         hidden_copy(k).wait_send()
-        from_x(cot_half_ref, cot_others, k, cot_send, cot_recv).wait_send()
+        twin_copy(k).wait_send()
         from_x(normed_sent, normed_others, k, n_send, n_recv).wait_send()
-        from_zx(cot_others, k, cot_send, cot_recv).wait_send()
-        from_zx(normed_others, k, n_send, n_recv).wait_send()
-        remote(
-            normed_sent.at[rows(k)], normed_twin.at[rows(k)],
-            n_send.at[3, k], n_recv.at[3, k], twin_id,
-        ).wait_send()
-    loop(tiles, lambda j: y_copy(1, column_window(j), j).wait_send())
-    loop(tiles, lambda j: core_copy(2, column_window(j), j).wait_send())
-    for slot in range(3):
+    for k in (0, 1):
+        from_z(normed_sent, normed_others, k, n_send, n_recv).wait_send()
+        from_zx(normed_others, k, n_send, n_recv).wait()
+    for block in range(2):
+        loop(tiles, lambda j: y_copy(1, block_window(block, j), block * tiles + j).wait_send())
+    loop(tiles, lambda j: core_copy(2, (everything, tile_of(j)), j).wait_send())
+    for slot in range(2):
         to_twin(cot_others, 0, slot).wait()
         to_twin(normed_others, 1, slot).wait()
 
 
 def middle(
-    w_query, w_key, w_value, w_out, tokens, cotangent, cotangent_half, gain_one, gain,
+    w_query, w_key, w_value, w_out, tokens, cotangent, gain_one, gain,
     w_gate, w_up, w_down, segment, cosine, sine,
 ):
     row_count, width = tokens.shape
@@ -749,16 +783,15 @@
             jax.ShapeDtypeStruct((row_count, width), BF16),
             jax.ShapeDtypeStruct((row_count, 768), BF16),
             jax.ShapeDtypeStruct((2, half, width // 2), F32),
-            jax.ShapeDtypeStruct((half, 2 * 768), F32),
-            wide, wide,
+            wide,
             jax.ShapeDtypeStruct((row_count, width), BF16),
             units, units, units,
             jax.ShapeDtypeStruct((1, width), F32),
-            jax.ShapeDtypeStruct((6, half, width), F32),
-            jax.ShapeDtypeStruct((6, half, width), F32),
+            jax.ShapeDtypeStruct((5, half, width), F32),
+            jax.ShapeDtypeStruct((5, half, width), F32),
         ),
-        in_specs=[hbm] * 7 + [vmem] * 2 + [hbm] * 3 + [vmem] * 4,
-        out_specs=(hbm,) * 18 + (vmem,) + (hbm,) * 2,
+        in_specs=[hbm] * 6 + [vmem] * 2 + [hbm] * 3 + [vmem] * 4,
+        out_specs=(hbm,) * 16 + (vmem,) + (hbm,) * 2,
         scratch_shapes=[
             pltpu.VMEM(w_gate.shape, BF16),
             pltpu.VMEM(w_up.shape, BF16),
@@ -775,22 +808,22 @@
             pltpu.VMEM((2, half, width), F32),
             pltpu.VMEM((3, half, width), F32),
             pltpu.VMEM((2, half, width), F32),
+            pltpu.VMEM((half, TILE), F32),
+            pltpu.VMEM((8, row_count), F32),
             dma((13,)),
-            dma((3, tiles)), dma((3, tiles)), dma((3, tiles)), dma((3, tiles)),
+            dma((3, 2 * tiles)), dma((3, 2 * tiles)), dma((2, 2 * tiles)), dma((2, 2 * tiles)),
             dma((3, CHUNKS)), dma((3, CHUNKS)),
             dma((4, CHUNKS)), dma((4, CHUNKS)),
-            dma((2, 3)), dma((2, 3)),
-            dma((2,)), dma((2,)),
+            dma((2, 2)), dma((2, 2)),
             dma((CHUNKS,)), dma((CHUNKS,)),
             dma((8,)), dma((8,)),
-            pltpu.VMEM((8, row_count), F32),
         ],
         compiler_params=pltpu.CompilerParams(
             collective_id=0, has_side_effects=True, vmem_limit_bytes=64 * 1024 * 1024
         ),
         name="feed_forward",
     )(
-        w_query, w_key, w_value, w_out, tokens, cotangent, cotangent_half,
+        w_query, w_key, w_value, w_out, tokens, cotangent,
         gain_one.reshape(1, width), gain.reshape(1, width), w_gate, w_up, w_down,
         segment.reshape(row_count, 1), segment.reshape(1, row_count), cosine, sine,
     )
@@ -808,7 +841,8 @@
     w_up_ref,
     w_down_ref,
     projected_ref,
-    projected_far_ref,
+    branch_ref,
+    gain_two_ref,
     w_query_ref,
     w_key_ref,
     w_value_ref,
@@ -824,12 +858,18 @@
     kept_out,
     sent_out,
     came_out,
+    down_kept,
+    down_sent,
+    down_came,
     out_mine,
     out_came,
     proj_mine,
     proj_came,
-    input_half_out,
-    input_twin_out,
+    input_out,
+    mixed_out,
+    branch_came,
+    normed_late,
+    cot_late,
     gain_out,
     normed,
     cot,
@@ -853,9 +893,10 @@
     proj_part,
     out_x,
     proj_x,
-    own_columns,
     far_staged,
     far_heads,
+    gains,
+    gains_came,
     load_sem,
     piece_sem,
     weight_sem,
@@ -873,6 +914,11 @@
     z_recv,
     end_send,
     end_recv,
+    gain_send,
+    gain_recv,
+    late_send,
+    late_recv,
+    product,
 ):
     dp, tensor = lax.axis_index("dp"), lax.axis_index("tensor")
     core = tensor % 2
@@ -885,8 +931,12 @@
     half, width = tok.shape
     row_count = 2 * half
     tiles = width // TILE
-    my_row = pl.multiple_of(core * half, half)
-    twin_row = pl.multiple_of((1 - core) * half, half)
+    run = half // 2
+    y_bit = (tensor // 2) % 2
+
+    def own_row(block, which):
+        return pl.multiple_of(block * half + which * run, run)
+
     everything = slice(None)
     transposed = (((1,), (1,)), ((), ()))
     over = (((0,), (0,)), ((), ()))
@@ -905,15 +955,18 @@
     near = [
         pl.ds(pl.multiple_of(b * 1024 + z_low * 512, 512), 512) for b in range(2)
     ]
+    own_columns = [units.at[0, pl.ds(i * row_count, row_count)] for i in range(4)]
     loads = [
-        pltpu.make_async_copy(normed_ref.at[:, away_block], own_columns.at[0], load_sem.at[0]),
-        pltpu.make_async_copy(normed_ref.at[:, home_block], own_columns.at[1], load_sem.at[1]),
-        pltpu.make_async_copy(cot_ref.at[:, away_block], own_columns.at[2], load_sem.at[2]),
-        pltpu.make_async_copy(cot_ref.at[:, home_block], own_columns.at[3], load_sem.at[3]),
+        pltpu.make_async_copy(normed_ref.at[:, away_block], own_columns[0], load_sem.at[0]),
+        pltpu.make_async_copy(normed_ref.at[:, home_block], own_columns[1], load_sem.at[1]),
+        pltpu.make_async_copy(cot_ref.at[:, away_block], own_columns[2], load_sem.at[2]),
+        pltpu.make_async_copy(cot_ref.at[:, home_block], own_columns[3], load_sem.at[3]),
         pltpu.make_async_copy(w_query_ref, w_proj.at[:, pl.ds(0, 512)], load_sem.at[4]),
         pltpu.make_async_copy(w_key_ref, w_proj.at[:, pl.ds(512, 128)], load_sem.at[5]),
         pltpu.make_async_copy(w_value_ref, w_proj.at[:, pl.ds(640, 128)], load_sem.at[6]),
-        pltpu.make_async_copy(tokens_ref.at[pl.ds(my_row, half)], tok, load_sem.at[7]),
+        pltpu.make_async_copy(
+            tokens_ref.at[pl.ds(own_row(0, core), run)], tok.at[pl.ds(0, run)], load_sem.at[7]
+        ),
         pltpu.make_async_copy(heads_ref, heads.at[0], load_sem.at[8]),
         pltpu.make_async_copy(
             grad_attn_ref.at[:, near[0]], grad_attn.at[0, :, pl.ds(0, 512)], load_sem.at[9]
@@ -928,11 +981,35 @@
             normed_one_ref.at[:, near[1]], normed_one.at[0, :, pl.ds(512, 512)], load_sem.at[12]
         ),
         pltpu.make_async_copy(projected_ref, projected.at[0], load_sem.at[13]),
+        pltpu.make_async_copy(
+            tokens_ref.at[pl.ds(own_row(1, core), run)], tok.at[pl.ds(run, run)], load_sem.at[14]
+        ),
     ]
 
+    late_normed = pl.ds(run, run)
+    early_normed = pl.ds(0, run)
+    late_cot = pl.ds(pl.multiple_of((1 - y_bit) * run, run), run)
+    early_cot = pl.ds(pl.multiple_of(y_bit * run, run), run)
+
     def piece_load(i, slot):
-        source = normed_others_ref.at[i] if i < 6 else cot_others_ref.at[i - 6]
-        return pltpu.make_async_copy(source, staged.at[slot], piece_sem.at[slot])
+        which, part = i // 6, i % 6
+        source = (normed_others_ref, cot_others_ref)[which]
+        late = (normed_late, cot_late)[which]
+        into = staged.at[slot]
+        if part in (0, 1, 3, 4):
+            return [pltpu.make_async_copy(source.at[part], into, piece_sem.at[slot])]
+        if part == 5:
+            return [pltpu.make_async_copy(late.at[1], into, piece_sem.at[slot])]
+        early_rows = (early_normed, early_cot)[which]
+        late_rows = (late_normed, late_cot)[which]
+        return [
+            pltpu.make_async_copy(
+                source.at[2, early_rows], into.at[early_rows], piece_sem.at[slot]
+            ),
+            pltpu.make_async_copy(
+                late.at[0, late_rows], into.at[late_rows], piece_sem.at[2 + slot]
+            ),
+        ]
 
     def weight_loads(j, slot):
         return [
@@ -947,82 +1024,129 @@
             ),
         ]
 
-    piece_load(0, 0).start()
-    piece_load(1, 1).start()
+    order = [0, 1, 3, 4, 6, 7, 9, 10, 2, 5, 8, 11]
+    for i in range(2):
+        for load in piece_load(order[i], i):
+            load.start()
+    loads[13].start()
     for load in loads[:4]:
         load.start()
     for load in weight_loads(0, 0):
         load.start()
 
     barrier = pltpu.get_barrier_semaphore()
-    for device in (twin_id, y_id, x_id, z_id, far_id):
+    peers = []
+    for m in range(1, 8):
+        peer = dp
+        for bit in (1, 2, 4):
+            peer = flip(peer, bit) if m & bit else peer
+        peers.append(peer)
+    for device in [twin_id, y_id] + [(peer, tensor) for peer in peers]:
         pl.semaphore_signal(barrier, inc=1, device_id=device, device_id_type=MESH)
-    pl.semaphore_wait(barrier, 5)
-
-    for i in range(12):
-        piece_load(i, i % 2).wait()
+    pl.semaphore_wait(barrier, 9)
+    late_copies = [
+        remote(normed_others_ref.at[1, late_normed], normed_late.at[0, late_normed],
+               late_send.at[0], late_recv.at[0], x_id),
+        remote(cot_others_ref.at[2, early_cot], cot_late.at[0, early_cot],
+               late_send.at[1], late_recv.at[1], y_id),
+        remote(normed_others_ref.at[2, early_normed], normed_late.at[1, early_normed],
+               late_send.at[2], late_recv.at[2], twin_id),
+        remote(cot_others_ref.at[2, early_cot], cot_late.at[1, early_cot],
+               late_send.at[3], late_recv.at[3], twin_id),
+    ]
+    for copy in late_copies:
+        copy.start()
+
+    loads[13].wait()
+
+    def widen(r):
+        window = pl.ds(pl.multiple_of(r * ROWS, ROWS), ROWS)
+        for s in range(2):
+            there = pl.ds(pl.multiple_of(s * half + r * ROWS, ROWS), ROWS)
+            proj_part[0, s, window, :] = projected[0, there, :].astype(F32)
+
+    loop(half // ROWS, widen)
+    projected_copy = remote(proj_part.at[0], far_staged, end_send.at[2], end_recv.at[2], far_id)
+    projected_copy.start()
+    branch_copy = remote(branch_ref, branch_came, end_send.at[1], end_recv.at[1], y_id)
+
+    late_twins = [
+        remote(normed_late.at[0, late_normed], normed_late.at[1, late_normed],
+               late_send.at[4], late_recv.at[4], twin_id),
+        remote(cot_late.at[0, late_cot], cot_late.at[1, late_cot],
+               late_send.at[5], late_recv.at[5], twin_id),
+    ]
+    def take_piece(place):
+        i, slot = order[place], place % 2
+        for load in piece_load(i, slot):
+            load.wait()
         rows_to, turned_to = (normed, normed_t) if i < 6 else (cot, cot_t)
-        base = (i % 6) * half
-
-        def convert(r, i=i, rows_to=rows_to, base=base):
+        base = {0: 0, 1: 1, 3: 2, 4: 3, 2: 4, 5: 5}[i % 6] * half
+
+        def convert(r, slot=slot, rows_to=rows_to, base=base):
             window = pl.ds(pl.multiple_of(r * ROWS, ROWS), ROWS)
             rows_to[pl.ds(pl.multiple_of(base + r * ROWS, ROWS), ROWS), :] = staged[
-                i % 2, window, :
+                slot, window, :
             ].astype(BF16)
 
         loop(half // ROWS, convert)
         for part, block in enumerate((away_block, home_block)):
             turned_to[pl.ds(part * TILE, TILE), pl.ds(row_count + base, half)] = (
-                staged[i % 2, :, block].T.astype(BF16)
+                staged[slot, :, block].T.astype(BF16)
             )
-        if i + 2 < 12:
-            piece_load(i + 2, i % 2).start()
+        if place == 5:
+            for copy, later in zip(late_copies[:2], late_twins):
+                copy.wait()
+                later.start()
+            branch_copy.start()
+        if place == 6:
+            for copy in late_copies[2:]:
+                copy.wait()
+        if place == 7:
+            for copy in late_twins:
+                copy.wait()
+        if place + 2 < 12:
+            for load in piece_load(order[place + 2], slot):
+                load.start()
+    for place in range(8):
+        take_piece(place)
     for part in range(4):
         loads[part].wait()
         turned_to = (normed_t, cot_t)[part // 2]
         turned_to[pl.ds((part % 2) * TILE, TILE), pl.ds(0, row_count)] = (
-            own_columns[part].astype(F32).T.astype(BF16)
+            own_columns[part][...].astype(F32).T.astype(BF16)
         )
-
-    for load in loads[4:]:
-        load.start()
-    far_loads = (
-        [
-            pltpu.make_async_copy(
-                grad_attn_far_ref.at[s], staged.at[0, :, pl.ds(s * 1024, 1024)], piece_sem.at[s]
-            )
-            for s in range(2)
-        ]
-        + [
-            pltpu.make_async_copy(
-                normed_one_far_ref.at[s], staged.at[1, :, pl.ds(s * 1024, 1024)],
-                piece_sem.at[2 + s],
-            )
-            for s in range(2)
-        ]
-        + [
-            pltpu.make_async_copy(projected_far_ref, far_staged, piece_sem.at[4]),
-            pltpu.make_async_copy(heads_far_ref, far_heads, piece_sem.at[5]),
-        ]
-    )
-    for load in far_loads:
-        load.start()
 
     def row_copy(j):
         window = (everything, everything, tile_of(j))
-        return remote(
-            sent_out.at[window], came_out.at[window], row_send.at[j], row_recv.at[j], far_id
-        )
+        return [
+            remote(
+                sent_out.at[window], came_out.at[window],
+                row_send.at[0, j], row_recv.at[0, j], far_id,
+            ),
+            remote(
+                down_sent.at[tile_of(j)], down_came.at[tile_of(j)],
+                row_send.at[1, j], row_recv.at[1, j], far_id,
+            ),
+        ]
 
     def stores(j, slot):
         return [
             pltpu.make_async_copy(
-                total.at[slot, :, pl.ds(0, TILE)], sent_out.at[:, :, tile_of(j)],
+                total.at[slot, pl.ds(0, 2), pl.ds(0, TILE)], sent_out.at[:, :, tile_of(j)],
                 store_sem.at[slot, 0],
             ),
             pltpu.make_async_copy(
-                total.at[slot, :, pl.ds(TILE, TILE)], kept_out.at[:, :, tile_of(j)],
+                total.at[slot, pl.ds(0, 2), pl.ds(TILE, TILE)], kept_out.at[:, :, tile_of(j)],
                 store_sem.at[slot, 1],
+            ),
+            pltpu.make_async_copy(
+                total.at[slot, 2, pl.ds(0, TILE)], down_sent.at[tile_of(j)],
+                store_sem.at[slot, 2],
+            ),
+            pltpu.make_async_copy(
+                total.at[slot, 2, pl.ds(TILE, TILE)], down_kept.at[tile_of(j)],
+                store_sem.at[slot, 3],
             ),
         ]
 
@@ -1034,15 +1158,20 @@
             for i, source in enumerate((gg_ref, gu_ref, act_ref))
         ]
 
-    def feed_forward_tile(j):
+    def feed_forward_tile(j, first=False):
         slot = j % 2
         for load in weight_loads(j, slot):
             load.wait()
 
-        @pl.when(j + 1 < tiles)
-        def _():
-            for load in weight_loads(j + 1, 1 - slot):
+        if first:
+            for load in weight_loads(1, 1):
                 load.start()
+        else:
+
+            @pl.when(j + 1 < tiles)
+            def _():
+                for load in weight_loads(j + 1, 1 - slot):
+                    load.start()
 
         for load in unit_loads(j):
             load.start()
@@ -1061,21 +1190,27 @@
             units[0, to, :] = (back * up * sigmoid * (1.0 + gate * (1.0 - sigmoid))).astype(BF16)
             units[1, to, :] = (back * swish).astype(BF16)
 
-        loop(normed.shape[0] // 512, block)
+        if first:
+            loop(2, block)
+            for place in range(8, 12):
+                take_piece(place)
+            block(2)
+        else:
+            loop(normed.shape[0] // 512, block)
         for load in unit_loads(j):
             load.wait()
 
-        @pl.when(j >= 1)
-        def _():
-            for store in stores(j - 1, 1 - slot):
-                store.wait()
-            row_copy(j - 1).start()
-
         total[slot, 0] = jnp.dot(normed_t[...], units[0], preferred_element_type=F32)
         total[slot, 1] = jnp.dot(normed_t[...], units[1], preferred_element_type=F32)
-        total[slot, 2] = jnp.dot(cot_t[...], units[2], preferred_element_type=F32)
+        turned = jnp.dot(cot_t[...], units[2], preferred_element_type=F32)
+        for part in range(2):
+            total[slot, 2, pl.ds(part * TILE, TILE)] = turned[part * TILE : (part + 1) * TILE].T
         for store in stores(j, slot):
             store.start()
+        for store in stores(j, slot):
+            store.wait()
+        for copy in row_copy(j):
+            copy.start()
 
     def x_copies(slot):
         return [
@@ -1086,18 +1221,22 @@
         ]
 
     def attention_parts():
-        for load in far_loads + loads[8:]:
+        for load in far_loads + loads[8:13]:
             load.wait()
+        projected_copy.wait()
 
         def convert(r):
             window = pl.ds(pl.multiple_of(r * ROWS, ROWS), ROWS)
+            block, rest = r // (run // ROWS), r % (run // ROWS)
             for s in range(2):
-                start = my_row if s == 0 else twin_row
-                here = pl.ds(pl.multiple_of(start + r * ROWS, ROWS), ROWS)
+                which = core if s == 0 else 1 - core
+                here = pl.ds(
+                    pl.multiple_of(block * half + which * run + rest * ROWS, ROWS), ROWS
+                )
                 grad_attn[1, here, :] = staged[0, window, pl.ds(s * 1024, 1024)].astype(BF16)
                 normed_one[1, here, :] = staged[1, window, pl.ds(s * 1024, 1024)].astype(BF16)
                 there = pl.ds(pl.multiple_of(s * half + r * ROWS, ROWS), ROWS)
-                projected[1, there, :] = far_staged[window, pl.ds(s * 768, 768)].astype(BF16)
+                projected[1, there, :] = far_staged[s, window, :].astype(BF16)
                 heads[1, there, :] = far_heads[window, pl.ds(s * 512, 512)].astype(BF16)
 
         loop(half // ROWS, convert)
@@ -1133,16 +1272,18 @@
         )
 
     def attention_sums():
-        for load in loads[4:8]:
+        for load in loads[4:8] + loads[14:]:
             load.wait()
 
         def produce(j):
-            weight = w_proj[tile_of(j), :]
-            for slot, start in ((0, twin_row), (1, my_row)):
-                staged[slot, :, tile_of(j)] = lax.dot_general(
-                    projected[0, pl.ds(start, half), :], weight, transposed,
-                    preferred_element_type=F32,
-                )
+            product[...] = lax.dot_general(
+                projected[0], w_proj[tile_of(j), :], transposed, preferred_element_type=F32
+            )
+            for block in range(2):
+                for slot, which in ((0, 1 - core), (1, core)):
+                    staged[slot, pl.ds(block * run, run), tile_of(j)] = product[
+                        pl.ds(own_row(block, which), run), :
+                    ]
             core_copy(j).start()
 
         def forward(j):
@@ -1160,20 +1301,42 @@
         forward(tiles - 1)
         loop(tiles, lambda j: core_copy(j).wait_send())
 
+    feed_forward_tile(0, first=True)
+    for load in loads[4:13] + loads[14:]:
+        load.start()
+    far_loads = (
+        [
+            pltpu.make_async_copy(
+                grad_attn_far_ref.at[s], staged.at[0, :, pl.ds(s * 1024, 1024)], piece_sem.at[s]
+            )
+            for s in range(2)
+        ]
+        + [
+            pltpu.make_async_copy(
+                normed_one_far_ref.at[s], staged.at[1, :, pl.ds(s * 1024, 1024)],
+                piece_sem.at[2 + s],
+            )
+            for s in range(2)
+        ]
+        + [
+            pltpu.make_async_copy(heads_far_ref, far_heads, piece_sem.at[5]),
+        ]
+    )
+    for load in far_loads:
+        load.start()
+
+
     def step(j):
-        feed_forward_tile(j)
-
-        @pl.when(j == 1)
+        feed_forward_tile(j + 1)
+
+        @pl.when(j == 0)
         def _():
             attention_parts()
             attention_sums()
 
-    loop(tiles, step)
+    loop(tiles - 1, step)
     hidden_load = pltpu.make_async_copy(grad_hidden_ref, core_in, load_sem.at[0])
     hidden_load.start()
-    for store in stores(tiles - 1, (tiles - 1) % 2):
-        store.wait()
-    row_copy(tiles - 1).start()
 
     def z_copies():
         return [
@@ -1197,7 +1360,8 @@
         store.start()
 
     gain = gain_ref[...]
-    gain_out[...] = jnp.zeros_like(gain_out)
+    gains[pl.ds(0, 1), :] = jnp.zeros_like(gain)
+    gains[pl.ds(1, 1), :] = gain_two_ref[...]
     hidden_load.wait()
     loop(tiles, lambda j: y_copy(j).wait_recv())
 
@@ -1210,33 +1374,101 @@
         inner = jnp.mean(weighted * values, axis=-1, keepdims=True)
         back = scale * weighted - values * (scale * scale * scale) * inner
         staged[0, window, :] = core_in[window, :] + back
-        gain_out[...] = gain_out[...] + jnp.sum(
+        gains[pl.ds(0, 1), :] = gains[pl.ds(0, 1), :] + jnp.sum(
             incoming * values * scale, axis=0, keepdims=True
         )
 
     loop(half // ROWS, norm_rows)
-    input_copy = remote(
-        staged.at[0], input_twin_out, end_send.at[0], end_recv.at[0], twin_id
-    )
-    input_copy.start()
-    input_store = pltpu.make_async_copy(staged.at[0], input_half_out, load_sem.at[3])
-    input_store.start()
-
-    for store in part_stores + [input_store]:
-        store.wait()
-    input_copy.wait()
+
+    def to_rows(slot, out, sems, first):
+        copies, kept = [], []
+        for block in range(2):
+            local, here = pl.ds(block * run, run), pl.ds(own_row(block, core), run)
+            copies.append(remote(
+                staged.at[slot, local], out.at[here],
+                end_send.at[sems + block], end_recv.at[sems + block], twin_id,
+            ))
+            kept.append(pltpu.make_async_copy(
+                staged.at[slot, local], out.at[here], load_sem.at[first + block]
+            ))
+        for copy in copies + kept:
+            copy.start()
+        return copies, kept
+
+    input_copies, input_stores = to_rows(0, input_out, 3, 3)
+
+    gain_twin = remote(gains, gains_came, gain_send.at[7], gain_recv.at[7], twin_id)
+    gain_twin.start()
+
+    loop(tiles, lambda j: y_copy(j).wait_send())
+    branch_copy.wait()
+    branch_loads = [
+        pltpu.make_async_copy(branch_ref, staged.at[1], load_sem.at[5]),
+        pltpu.make_async_copy(branch_came, y_in, load_sem.at[6]),
+    ]
+    for load in branch_loads:
+        load.start()
+    gain_twin.wait()
+    gains[...] = gains[...] + gains_came[...]
+
+    def gain_copy(m):
+        return remote(
+            gains.at[:, tile_of(peers[m])], gain_out.at[m], gain_send.at[m], gain_recv.at[m],
+            (peers[m], tensor),
+        )
+
+    for m in range(7):
+        gain_copy(m).start()
+    gain_out[7] = gains[:, tile_of(dp)]
+    for load in branch_loads:
+        load.wait()
+
+    def mixed_rows(i):
+        window = pl.ds(pl.multiple_of(i * ROWS, ROWS), ROWS)
+        staged[1, window, :] = staged[1, window, :] + y_in[window, :]
+
+    loop(half // ROWS, mixed_rows)
+    mixed_copy = remote(staged.at[1], core_in, end_send.at[5], end_recv.at[5], twin_id)
+    mixed_copy.start()
+
+    def put_mixed(source, which, first):
+        def narrow(i):
+            window = pl.ds(pl.multiple_of(i * ROWS, ROWS), ROWS)
+            tok[window, :] = source[window, :].astype(BF16)
+
+        loop(half // ROWS, narrow)
+        copies = [
+            pltpu.make_async_copy(
+                tok.at[pl.ds(block * run, run)], mixed_out.at[pl.ds(own_row(block, which), run)],
+                load_sem.at[first + block],
+            )
+            for block in range(2)
+        ]
+        for copy in copies:
+            copy.start()
+        for copy in copies:
+            copy.wait()
+
+    put_mixed(staged.at[1], core, 7)
+    mixed_copy.wait()
+    put_mixed(core_in, 1 - core, 9)
+
+    for copy in part_stores + input_stores + input_copies:
+        copy.wait()
+    for m in range(7):
+        gain_copy(m).wait()
     for slot in range(2):
         for copy in x_copies(slot):
             copy.wait_send()
-    loop(tiles, lambda j: y_copy(j).wait_send())
     for copy in z_copies():
         copy.wait()
-    loop(tiles, lambda j: row_copy(j).wait())
+    for part in range(2):
+        loop(tiles, lambda j: row_copy(j)[part].wait())
 
 
 def last(
     normed_others, cot_others, normed, cot, act, gg, gu, w_gate, w_up, w_down,
-    projected, projected_far, w_query, w_key, w_value, heads, grad_attn, grad_attn_far,
+    projected, branch, gain_two, w_query, w_key, w_value, heads, grad_attn, grad_attn_far,
     normed_one, normed_one_far, heads_far, grad_hidden, tokens, gain,
 ):
     row_count, width = tokens.shape
@@ -1246,18 +1478,24 @@
     hbm = pl.BlockSpec(memory_space=pl.ANY)
     vmem = pl.BlockSpec(memory_space=pltpu.VMEM)
     wide = jax.ShapeDtypeStruct((half, width), F32)
-    triple = jax.ShapeDtypeStruct((3, TILE, hidden_units), F32)
+    rows_pair = jax.ShapeDtypeStruct((2, TILE, hidden_units), F32)
+    columns = jax.ShapeDtypeStruct((hidden_units, TILE), F32)
     out_block = jax.ShapeDtypeStruct((512, TILE), F32)
     proj_block = jax.ShapeDtypeStruct((TILE, 768), F32)
     dma = pltpu.SemaphoreType.DMA
     return pl.pallas_call(
         last_kernel,
         out_shape=(
-            triple, triple, triple, out_block, out_block, proj_block, proj_block, wide, wide,
-            jax.ShapeDtypeStruct((1, width), F32),
+            rows_pair, rows_pair, rows_pair, columns, columns, columns, out_block, out_block, proj_block, proj_block,
+            jax.ShapeDtypeStruct((row_count, width), F32),
+            jax.ShapeDtypeStruct((row_count, width), BF16),
+            wide,
+            jax.ShapeDtypeStruct((2, half, width), F32),
+            jax.ShapeDtypeStruct((2, half, width), F32),
+            jax.ShapeDtypeStruct((8, 2, TILE), F32),
         ),
-        in_specs=[hbm] * 23 + [vmem],
-        out_specs=(hbm,) * 9 + (vmem,),
+        in_specs=[hbm] * 12 + [vmem] + [hbm] * 11 + [vmem],
+        out_specs=(hbm,) * 15 + (vmem,),
         scratch_shapes=[
             pltpu.VMEM((6 * half, width), BF16),
             pltpu.VMEM((6 * half, width), BF16),
@@ -1281,13 +1519,15 @@
             pltpu.VMEM((2, 2, TILE, 768), F32),
             pltpu.VMEM((2, 512, TILE), F32),
             pltpu.VMEM((2, TILE, 768), F32),
-            pltpu.VMEM((4, row_count, TILE), BF16),
-            pltpu.VMEM((half, 2 * 768), F32),
+            pltpu.VMEM((2, half, 768), F32),
             pltpu.VMEM((half, 1024), F32),
-            dma((14,)), dma((6,)), dma((2, 3)), dma((3,)), dma((2, 2)),
-            dma((tiles,)), dma((tiles,)),
+            pltpu.VMEM((2, width), F32),
+            pltpu.VMEM((2, width), F32),
+            dma((15,)), dma((6,)), dma((2, 3)), dma((3,)), dma((2, 4)),
+            dma((2, tiles)), dma((2, tiles)),
             dma((tiles,)), dma((tiles,)), dma((tiles,)), dma((tiles,)),
-            dma((2, 2)), dma((2, 2)), dma((2,)), dma((2,)), dma((1,)), dma((1,)),
+            dma((2, 2)), dma((2, 2)), dma((2,)), dma((2,)), dma((7,)), dma((7,)), dma((8,)), dma((8,)),
+            dma((6,)), dma((6,)), pltpu.VMEM((row_count, TILE), F32),
         ],
         compiler_params=pltpu.CompilerParams(
             collective_id=1, has_side_effects=True, vmem_limit_bytes=64 * 1024 * 1024
@@ -1295,7 +1535,803 @@
         name="weight_gradients",
     )(
         normed_others, cot_others, normed, cot, act, gg, gu, w_gate, w_up, w_down,
-        projected, projected_far, w_query, w_key, w_value, heads, grad_attn, grad_attn_far,
+        projected, branch, gain_two, w_query, w_key, w_value, heads, grad_attn, grad_attn_far,
+        normed_one, normed_one_far, heads_far, grad_hidden, tokens, gain.reshape(1, width),
+    )
+
+
+def body(
+    tokens,
+    segments,
+    positions,
+    attn_gain,
+    w_query,
+    key_weight,
+    value_weight,
+    w_out,
+    mlp_gain,
+    w_gate,
+    w_up,
+    w_down,
+    cotangent,
+):
+    groups = lax.axis_size("dp")
+    place = lax.axis_index("dp")
+    core = lax.axis_index("tensor") % 2
+    row_count, width = tokens.shape
+    half = row_count // 2
+    hidden_units = w_gate.shape[1]
+    tiles = width // TILE
+    hbm = pl.BlockSpec(memory_space=pl.ANY)
+    vmem = pl.BlockSpec(memory_space=pltpu.VMEM)
+    wide = jax.ShapeDtypeStruct((half, width), F32)
+    units = jax.ShapeDtypeStruct((row_count, hidden_units), BF16)
+    square = jax.ShapeDtypeStruct((row_count, 512), BF16)
+    dma = pltpu.SemaphoreType.DMA
+    return pl.pallas_call(
+        middle_kernel,
+        out_shape=(
+            jax.ShapeDtypeStruct((row_count, width), BF16),
+            square, square, square, square,
+            jax.ShapeDtypeStruct((2, half, width // 2), F32),
+            jax.ShapeDtypeStruct((half, width // 2), F32),
+            wide,
+            jax.ShapeDtypeStruct((row_count, width), BF16),
+            jax.ShapeDtypeStruct((row_count, 768), BF16),
+            jax.ShapeDtypeStruct((2, half, width // 2), F32),
+            wide,
+            jax.ShapeDtypeStruct((row_count, width), BF16),
+            units, units, units,
+            jax.ShapeDtypeStruct((1, width), F32),
+            jax.ShapeDtypeStruct((5, half, width), F32),
+            jax.ShapeDtypeStruct((5, half, width), F32),
+        ),
+        in_specs=[hbm] * 6 + [vmem] * 2 + [hbm] * 3 + [vmem] * 4,
+        out_specs=(hbm,) * 16 + (vmem,) + (hbm,) * 2,
+        scratch_shapes=[
+            pltpu.VMEM(w_gate.shape, BF16),
+            pltpu.VMEM(w_up.shape, BF16),
+            pltpu.VMEM(w_down.shape, BF16),
+            pltpu.VMEM((row_count, width), BF16),
+            pltpu.VMEM((half, width), F32),
+            pltpu.VMEM((row_count, width), BF16),
+            pltpu.VMEM((half, width), F32),
+            pltpu.VMEM((half, width), F32),
+            pltpu.VMEM((row_count, hidden_units), BF16),
+            pltpu.VMEM((row_count, hidden_units), BF16),
+            pltpu.VMEM((row_count, hidden_units), BF16),
+            pltpu.VMEM((half, width), F32),
+            pltpu.VMEM((2, half, width), F32),
+            pltpu.VMEM((3, half, width), F32),
+            pltpu.VMEM((2, half, width), F32),
+            pltpu.VMEM((half, TILE), F32),
+            pltpu.VMEM((8, row_count), F32),
+            dma((13,)),
+            dma((3, 2 * tiles)), dma((3, 2 * tiles)), dma((2, 2 * tiles)), dma((2, 2 * tiles)),
+            dma((3, CHUNKS)), dma((3, CHUNKS)),
+            dma((4, CHUNKS)), dma((4, CHUNKS)),
+            dma((2, 2)), dma((2, 2)),
+            dma((CHUNKS,)), dma((CHUNKS,)),
+            dma((8,)), dma((8,)),
+        ],
+        compiler_params=pltpu.CompilerParams(
+            collective_id=0, has_side_effects=True, vmem_limit_bytes=64 * 1024 * 1024
+        ),
+        name="feed_forward",
+    )(
+        w_query, w_key, w_value, w_out, tokens, cotangent,
+        gain_one.reshape(1, width), gain.reshape(1, width), w_gate, w_up, w_down,
+        segment.reshape(row_count, 1), segment.reshape(1, row_count), cosine, sine,
+    )
+
+
+def last_kernel(
+    normed_others_ref,
+    cot_others_ref,
+    normed_ref,
+    cot_ref,
+    act_ref,
+    gg_ref,
+    gu_ref,
+    w_gate_ref,
+    w_up_ref,
+    w_down_ref,
+    projected_ref,
+    branch_ref,
+    gain_two_ref,
+    w_query_ref,
+    w_key_ref,
+    w_value_ref,
+    heads_ref,
+    grad_attn_ref,
+    grad_attn_far_ref,
+    normed_one_ref,
+    normed_one_far_ref,
+    heads_far_ref,
+    grad_hidden_ref,
+    tokens_ref,
+    gain_ref,
+    kept_out,
+    sent_out,
+    came_out,
+    down_kept,
+    down_sent,
+    down_came,
+    out_mine,
+    out_came,
+    proj_mine,
+    proj_came,
+    input_out,
+    mixed_out,
+    branch_came,
+    normed_late,
+    cot_late,
+    gain_out,
+    normed,
+    cot,
+    normed_t,
+    cot_t,
+    units,
+    gate_w,
+    up_w,
+    down_w,
+    total,
+    staged,
+    core_in,
+    y_in,
+    w_proj,
+    tok,
+    heads,
+    grad_attn,
+    normed_one,
+    projected,
+    out_part,
+    proj_part,
+    out_x,
+    proj_x,
+    far_staged,
+    far_heads,
+    gains,
+    gains_came,
+    load_sem,
+    piece_sem,
+    weight_sem,
+    unit_sem,
+    store_sem,
+    row_send,
+    row_recv,
+    core_send,
+    core_recv,
+    y_send,
+    y_recv,
+    x_send,
+    x_recv,
+    z_send,
+    z_recv,
+    end_send,
+    end_recv,
+    gain_send,
+    gain_recv,
+    late_send,
+    late_recv,
+    product,
+):
+    dp, tensor = lax.axis_index("dp"), lax.axis_index("tensor")
+    core = tensor % 2
+    x_low, z_low, z_high = dp % 2, (dp // 2) % 2, dp // 4
+    twin_id = (dp, flip(tensor, 1))
+    y_id = (dp, flip(tensor, 2))
+    x_id = (flip(dp, 1), tensor)
+    z_id = (flip(dp, 4), tensor)
+    far_id = (flip(dp, 2), tensor)
+    half, width = tok.shape
+    row_count = 2 * half
+    tiles = width // TILE
+    run = half // 2
+    y_bit = (tensor // 2) % 2
+
+    def own_row(block, which):
+        return pl.multiple_of(block * half + which * run, run)
+
+    everything = slice(None)
+    transposed = (((1,), (1,)), ((), ()))
+    over = (((0,), (0,)), ((), ()))
+
+    def remote(src, dst, send, recv, device):
+        return pltpu.make_async_remote_copy(
+            src_ref=src, dst_ref=dst, send_sem=send, recv_sem=recv,
+            device_id=device, device_id_type=MESH,
+        )
+
+    def tile_of(j):
+        return pl.ds(pl.multiple_of(j * TILE, TILE), TILE)
+
+    away_block = tile_of(flip(dp, 2))
+    home_block = tile_of(dp)
+    near = [
+        pl.ds(pl.multiple_of(b * 1024 + z_low * 512, 512), 512) for b in range(2)
+    ]
+    own_columns = [units.at[0, pl.ds(i * row_count, row_count)] for i in range(4)]
+    loads = [
+        pltpu.make_async_copy(normed_ref.at[:, away_block], own_columns[0], load_sem.at[0]),
+        pltpu.make_async_copy(normed_ref.at[:, home_block], own_columns[1], load_sem.at[1]),
+        pltpu.make_async_copy(cot_ref.at[:, away_block], own_columns[2], load_sem.at[2]),
+        pltpu.make_async_copy(cot_ref.at[:, home_block], own_columns[3], load_sem.at[3]),
+        pltpu.make_async_copy(w_query_ref, w_proj.at[:, pl.ds(0, 512)], load_sem.at[4]),
+        pltpu.make_async_copy(w_key_ref, w_proj.at[:, pl.ds(512, 128)], load_sem.at[5]),
+        pltpu.make_async_copy(w_value_ref, w_proj.at[:, pl.ds(640, 128)], load_sem.at[6]),
+        pltpu.make_async_copy(
+            tokens_ref.at[pl.ds(own_row(0, core), run)], tok.at[pl.ds(0, run)], load_sem.at[7]
+        ),
+        pltpu.make_async_copy(heads_ref, heads.at[0], load_sem.at[8]),
+        pltpu.make_async_copy(
+            grad_attn_ref.at[:, near[0]], grad_attn.at[0, :, pl.ds(0, 512)], load_sem.at[9]
+        ),
+        pltpu.make_async_copy(
+            grad_attn_ref.at[:, near[1]], grad_attn.at[0, :, pl.ds(512, 512)], load_sem.at[10]
+        ),
+        pltpu.make_async_copy(
+            normed_one_ref.at[:, near[0]], normed_one.at[0, :, pl.ds(0, 512)], load_sem.at[11]
+        ),
+        pltpu.make_async_copy(
+            normed_one_ref.at[:, near[1]], normed_one.at[0, :, pl.ds(512, 512)], load_sem.at[12]
+        ),
+        pltpu.make_async_copy(projected_ref, projected.at[0], load_sem.at[13]),
+        pltpu.make_async_copy(
+            tokens_ref.at[pl.ds(own_row(1, core), run)], tok.at[pl.ds(run, run)], load_sem.at[14]
+        ),
+    ]
+
+    late_normed = pl.ds(run, run)
+    early_normed = pl.ds(0, run)
+    late_cot = pl.ds(pl.multiple_of((1 - y_bit) * run, run), run)
+    early_cot = pl.ds(pl.multiple_of(y_bit * run, run), run)
+
+    def piece_load(i, slot):
+        which, part = i // 6, i % 6
+        source = (normed_others_ref, cot_others_ref)[which]
+        late = (normed_late, cot_late)[which]
+        into = staged.at[slot]
+        if part in (0, 1, 3, 4):
+            return [pltpu.make_async_copy(source.at[part], into, piece_sem.at[slot])]
+        if part == 5:
+            return [pltpu.make_async_copy(late.at[1], into, piece_sem.at[slot])]
+        early_rows = (early_normed, early_cot)[which]
+        late_rows = (late_normed, late_cot)[which]
+        return [
+            pltpu.make_async_copy(
+                source.at[2, early_rows], into.at[early_rows], piece_sem.at[slot]
+            ),
+            pltpu.make_async_copy(
+                late.at[0, late_rows], into.at[late_rows], piece_sem.at[2 + slot]
+            ),
+        ]
+
+    def weight_loads(j, slot):
+        return [
+            pltpu.make_async_copy(
+                w_gate_ref.at[:, tile_of(j)], gate_w.at[slot], weight_sem.at[slot, 0]
+            ),
+            pltpu.make_async_copy(
+                w_up_ref.at[:, tile_of(j)], up_w.at[slot], weight_sem.at[slot, 1]
+            ),
+            pltpu.make_async_copy(
+                w_down_ref.at[tile_of(j), :], down_w.at[slot], weight_sem.at[slot, 2]
+            ),
+        ]
+
+    order = [0, 1, 3, 4, 6, 7, 9, 10, 2, 5, 8, 11]
+    for i in range(2):
+        for load in piece_load(order[i], i):
+            load.start()
+    loads[13].start()
+    for load in loads[:4]:
+        load.start()
+    for load in weight_loads(0, 0):
+        load.start()
+
+    barrier = pltpu.get_barrier_semaphore()
+    peers = []
+    for m in range(1, 8):
+        peer = dp
+        for bit in (1, 2, 4):
+            peer = flip(peer, bit) if m & bit else peer
+        peers.append(peer)
+    for device in [twin_id, y_id] + [(peer, tensor) for peer in peers]:
+        pl.semaphore_signal(barrier, inc=1, device_id=device, device_id_type=MESH)
+    pl.semaphore_wait(barrier, 9)
+    late_copies = [
+        remote(normed_others_ref.at[1, late_normed], normed_late.at[0, late_normed],
+               late_send.at[0], late_recv.at[0], x_id),
+        remote(cot_others_ref.at[2, early_cot], cot_late.at[0, early_cot],
+               late_send.at[1], late_recv.at[1], y_id),
+        remote(normed_others_ref.at[2, early_normed], normed_late.at[1, early_normed],
+               late_send.at[2], late_recv.at[2], twin_id),
+        remote(cot_others_ref.at[2, early_cot], cot_late.at[1, early_cot],
+               late_send.at[3], late_recv.at[3], twin_id),
+    ]
+    for copy in late_copies:
+        copy.start()
+
+    loads[13].wait()
+
+    def widen(r):
+        window = pl.ds(pl.multiple_of(r * ROWS, ROWS), ROWS)
+        for s in range(2):
+            there = pl.ds(pl.multiple_of(s * half + r * ROWS, ROWS), ROWS)
+            proj_part[0, s, window, :] = projected[0, there, :].astype(F32)
+
+    loop(half // ROWS, widen)
+    projected_copy = remote(proj_part.at[0], far_staged, end_send.at[2], end_recv.at[2], far_id)
+    projected_copy.start()
+    branch_copy = remote(branch_ref, branch_came, end_send.at[1], end_recv.at[1], y_id)
+
+    late_twins = [
+        remote(normed_late.at[0, late_normed], normed_late.at[1, late_normed],
+               late_send.at[4], late_recv.at[4], twin_id),
+        remote(cot_late.at[0, late_cot], cot_late.at[1, late_cot],
+               late_send.at[5], late_recv.at[5], twin_id),
+    ]
+    def take_piece(place):
+        i, slot = order[place], place % 2
+        for load in piece_load(i, slot):
+            load.wait()
+        rows_to, turned_to = (normed, normed_t) if i < 6 else (cot, cot_t)
+        base = {0: 0, 1: 1, 3: 2, 4: 3, 2: 4, 5: 5}[i % 6] * half
+
+        def convert(r, slot=slot, rows_to=rows_to, base=base):
+            window = pl.ds(pl.multiple_of(r * ROWS, ROWS), ROWS)
+            rows_to[pl.ds(pl.multiple_of(base + r * ROWS, ROWS), ROWS), :] = staged[
+                slot, window, :
+            ].astype(BF16)
+
+        loop(half // ROWS, convert)
+        for part, block in enumerate((away_block, home_block)):
+            turned_to[pl.ds(part * TILE, TILE), pl.ds(row_count + base, half)] = (
+                staged[slot, :, block].T.astype(BF16)
+            )
+        if place == 5:
+            for copy, later in zip(late_copies[:2], late_twins):
+                copy.wait()
+                later.start()
+            branch_copy.start()
+        if place == 6:
+            for copy in late_copies[2:]:
+                copy.wait()
+        if place == 7:
+            for copy in late_twins:
+                copy.wait()
+        if place + 2 < 12:
+            for load in piece_load(order[place + 2], slot):
+                load.start()
+    for place in range(8):
+        take_piece(place)
+    for part in range(4):
+        loads[part].wait()
+        turned_to = (normed_t, cot_t)[part // 2]
+        turned_to[pl.ds((part % 2) * TILE, TILE), pl.ds(0, row_count)] = (
+            own_columns[part][...].astype(F32).T.astype(BF16)
+        )
+
+    def row_copy(j):
+        window = (everything, everything, tile_of(j))
+        return [
+            remote(
+                sent_out.at[window], came_out.at[window],
+                row_send.at[0, j], row_recv.at[0, j], far_id,
+            ),
+            remote(
+                down_sent.at[tile_of(j)], down_came.at[tile_of(j)],
+                row_send.at[1, j], row_recv.at[1, j], far_id,
+            ),
+        ]
+
+    def stores(j, slot):
+        return [
+            pltpu.make_async_copy(
+                total.at[slot, pl.ds(0, 2), pl.ds(0, TILE)], sent_out.at[:, :, tile_of(j)],
+                store_sem.at[slot, 0],
+            ),
+            pltpu.make_async_copy(
+                total.at[slot, pl.ds(0, 2), pl.ds(TILE, TILE)], kept_out.at[:, :, tile_of(j)],
+                store_sem.at[slot, 1],
+            ),
+            pltpu.make_async_copy(
+                total.at[slot, 2, pl.ds(0, TILE)], down_sent.at[tile_of(j)],
+                store_sem.at[slot, 2],
+            ),
+            pltpu.make_async_copy(
+                total.at[slot, 2, pl.ds(TILE, TILE)], down_kept.at[tile_of(j)],
+                store_sem.at[slot, 3],
+            ),
+        ]
+
+    def unit_loads(j):
+        return [
+            pltpu.make_async_copy(
+                source.at[:, tile_of(j)], units.at[i, pl.ds(0, row_count)], unit_sem.at[i]
+            )
+            for i, source in enumerate((gg_ref, gu_ref, act_ref))
+        ]
+
+    def feed_forward_tile(j, first=False):
+        slot = j % 2
+        for load in weight_loads(j, slot):
+            load.wait()
+
+        if first:
+            for load in weight_loads(1, 1):
+                load.start()
+        else:
+
+            @pl.when(j + 1 < tiles)
+            def _():
+                for load in weight_loads(j + 1, 1 - slot):
+                    load.start()
+
+        for load in unit_loads(j):
+            load.start()
+
+        def block(m):
+            rows = pl.ds(pl.multiple_of(m * 512, 512), 512)
+            to = pl.ds(pl.multiple_of(row_count + m * 512, 512), 512)
+            gate = jnp.dot(normed[rows, :], gate_w[slot], preferred_element_type=F32)
+            up = jnp.dot(normed[rows, :], up_w[slot], preferred_element_type=F32)
+            back = lax.dot_general(
+                cot[rows, :], down_w[slot], transposed, preferred_element_type=F32
+            )
+            sigmoid = jax.nn.sigmoid(gate)
+            swish = gate * sigmoid
+            units[2, to, :] = (swish * up).astype(BF16)
+            units[0, to, :] = (back * up * sigmoid * (1.0 + gate * (1.0 - sigmoid))).astype(BF16)
+            units[1, to, :] = (back * swish).astype(BF16)
+
+        if first:
+            loop(2, block)
+            for place in range(8, 12):
+                take_piece(place)
+            block(2)
+        else:
+            loop(normed.shape[0] // 512, block)
+        for load in unit_loads(j):
+            load.wait()
+
+        total[slot, 0] = jnp.dot(normed_t[...], units[0], preferred_element_type=F32)
+        total[slot, 1] = jnp.dot(normed_t[...], units[1], preferred_element_type=F32)
+        turned = jnp.dot(cot_t[...], units[2], preferred_element_type=F32)
+        for part in range(2):
+            total[slot, 2, pl.ds(part * TILE, TILE)] = turned[part * TILE : (part + 1) * TILE].T
+        for store in stores(j, slot):
+            store.start()
+        for store in stores(j, slot):
+            store.wait()
+        for copy in row_copy(j):
+            copy.start()
+
+    def x_copies(slot):
+        return [
+            remote(out_part.at[0, slot], out_x.at[slot], x_send.at[0, slot],
+                   x_recv.at[0, slot], x_id),
+            remote(proj_part.at[0, slot], proj_x.at[slot], x_send.at[1, slot],
+                   x_recv.at[1, slot], x_id),
+        ]
+
+    def attention_parts():
+        for load in far_loads + loads[8:13]:
+            load.wait()
+        projected_copy.wait()
+
+        def convert(r):
+            window = pl.ds(pl.multiple_of(r * ROWS, ROWS), ROWS)
+            block, rest = r // (run // ROWS), r % (run // ROWS)
+            for s in range(2):
+                which = core if s == 0 else 1 - core
+                here = pl.ds(
+                    pl.multiple_of(block * half + which * run + rest * ROWS, ROWS), ROWS
+                )
+                grad_attn[1, here, :] = staged[0, window, pl.ds(s * 1024, 1024)].astype(BF16)
+                normed_one[1, here, :] = staged[1, window, pl.ds(s * 1024, 1024)].astype(BF16)
+                there = pl.ds(pl.multiple_of(s * half + r * ROWS, ROWS), ROWS)
+                projected[1, there, :] = far_staged[s, window, :].astype(BF16)
+                heads[1, there, :] = far_heads[window, pl.ds(s * 512, 512)].astype(BF16)
+
+        loop(half // ROWS, convert)
+        for side in range(2):
+            x_at = 1 - x_low if side == 0 else x_low
+            for slot in range(2):
+                z_at = 1 - z_high if slot == 0 else z_high
+                columns = pl.ds(pl.multiple_of(z_at * 512 + x_at * 256, 256), 256)
+                out_part[side, slot] = lax.dot_general(
+                    heads[0], grad_attn[0, :, columns], over, preferred_element_type=F32
+                ) + lax.dot_general(
+                    heads[1], grad_attn[1, :, columns], over, preferred_element_type=F32
+                )
+                proj_part[side, slot] = lax.dot_general(
+                    normed_one[0, :, columns], projected[0], over, preferred_element_type=F32
+                ) + lax.dot_general(
+                    normed_one[1, :, columns], projected[1], over, preferred_element_type=F32
+                )
+                if side == 0:
+                    for copy in x_copies(slot):
+                        copy.start()
+
+    def core_copy(j):
+        window = (everything, tile_of(j))
+        return remote(
+            staged.at[0].at[window], core_in.at[window], core_send.at[j], core_recv.at[j], twin_id
+        )
+
+    def y_copy(j):
+        window = (everything, tile_of(j))
+        return remote(
+            staged.at[1].at[window], y_in.at[window], y_send.at[j], y_recv.at[j], y_id
+        )
+
+    def attention_sums():
+        for load in loads[4:8] + loads[14:]:
+            load.wait()
+
+        def produce(j):
+            product[...] = lax.dot_general(
+                projected[0], w_proj[tile_of(j), :], transposed, preferred_element_type=F32
+            )
+            for block in range(2):
+                for slot, which in ((0, 1 - core), (1, core)):
+                    staged[slot, pl.ds(block * run, run), tile_of(j)] = product[
+                        pl.ds(own_row(block, which), run), :
+                    ]
+            core_copy(j).start()
+
+        def forward(j):
+            core_copy(j).wait_recv()
+            staged[1, :, tile_of(j)] = staged[1, :, tile_of(j)] + core_in[:, tile_of(j)]
+            y_copy(j).start()
+
+        produce(0)
+
+        def step(j):
+            produce(j + 1)
+            forward(j)
+
+        loop(tiles - 1, step)
+        forward(tiles - 1)
+        loop(tiles, lambda j: core_copy(j).wait_send())
+
+    feed_forward_tile(0, first=True)
+    for load in loads[4:13] + loads[14:]:
+        load.start()
+    far_loads = (
+        [
+            pltpu.make_async_copy(
+                grad_attn_far_ref.at[s], staged.at[0, :, pl.ds(s * 1024, 1024)], piece_sem.at[s]
+            )
+            for s in range(2)
+        ]
+        + [
+            pltpu.make_async_copy(
+                normed_one_far_ref.at[s], staged.at[1, :, pl.ds(s * 1024, 1024)],
+                piece_sem.at[2 + s],
+            )
+            for s in range(2)
+        ]
+        + [
+            pltpu.make_async_copy(heads_far_ref, far_heads, piece_sem.at[5]),
+        ]
+    )
+    for load in far_loads:
+        load.start()
+
+
+    def step(j):
+        feed_forward_tile(j + 1)
+
+        @pl.when(j == 0)
+        def _():
+            attention_parts()
+            attention_sums()
+
+    loop(tiles - 1, step)
+    hidden_load = pltpu.make_async_copy(grad_hidden_ref, core_in, load_sem.at[0])
+    hidden_load.start()
+
+    def z_copies():
+        return [
+            remote(out_part.at[1, 0], out_came, z_send.at[0], z_recv.at[0], z_id),
+            remote(proj_part.at[1, 0], proj_came, z_send.at[1], z_recv.at[1], z_id),
+        ]
+
+    for slot in range(2):
+        for copy in x_copies(slot):
+            copy.wait_recv()
+        out_part[1, slot] = out_part[1, slot] + out_x[slot]
+        proj_part[1, slot] = proj_part[1, slot] + proj_x[slot]
+        if slot == 0:
+            for copy in z_copies():
+                copy.start()
+    part_stores = [
+        pltpu.make_async_copy(out_part.at[1, 1], out_mine, load_sem.at[1]),
+        pltpu.make_async_copy(proj_part.at[1, 1], proj_mine, load_sem.at[2]),
+    ]
+    for store in part_stores:
+        store.start()
+
+    gain = gain_ref[...]
+    gains[pl.ds(0, 1), :] = jnp.zeros_like(gain)
+    gains[pl.ds(1, 1), :] = gain_two_ref[...]
+    hidden_load.wait()
+    loop(tiles, lambda j: y_copy(j).wait_recv())
+
+    def norm_rows(i):
+        window = pl.ds(pl.multiple_of(i * ROWS, ROWS), ROWS)
+        incoming = staged[1, window, :] + y_in[window, :]
+        values = tok[window, :].astype(F32)
+        scale = lax.rsqrt(jnp.mean(values * values, axis=-1, keepdims=True) + EPSILON)
+        weighted = incoming * gain
+        inner = jnp.mean(weighted * values, axis=-1, keepdims=True)
+        back = scale * weighted - values * (scale * scale * scale) * inner
+        staged[0, window, :] = core_in[window, :] + back
+        gains[pl.ds(0, 1), :] = gains[pl.ds(0, 1), :] + jnp.sum(
+            incoming * values * scale, axis=0, keepdims=True
+        )
+
+    loop(half // ROWS, norm_rows)
+
+    def to_rows(slot, out, sems, first):
+        copies, kept = [], []
+        for block in range(2):
+            local, here = pl.ds(block * run, run), pl.ds(own_row(block, core), run)
+            copies.append(remote(
+                staged.at[slot, local], out.at[here],
+                end_send.at[sems + block], end_recv.at[sems + block], twin_id,
+            ))
+            kept.append(pltpu.make_async_copy(
+                staged.at[slot, local], out.at[here], load_sem.at[first + block]
+            ))
+        for copy in copies + kept:
+            copy.start()
+        return copies, kept
+
+    input_copies, input_stores = to_rows(0, input_out, 3, 3)
+
+    gain_twin = remote(gains, gains_came, gain_send.at[7], gain_recv.at[7], twin_id)
+    gain_twin.start()
+
+    loop(tiles, lambda j: y_copy(j).wait_send())
+    branch_copy.wait()
+    branch_loads = [
+        pltpu.make_async_copy(branch_ref, staged.at[1], load_sem.at[5]),
+        pltpu.make_async_copy(branch_came, y_in, load_sem.at[6]),
+    ]
+    for load in branch_loads:
+        load.start()
+    gain_twin.wait()
+    gains[...] = gains[...] + gains_came[...]
+
+    def gain_copy(m):
+        return remote(
+            gains.at[:, tile_of(peers[m])], gain_out.at[m], gain_send.at[m], gain_recv.at[m],
+            (peers[m], tensor),
+        )
+
+    for m in range(7):
+        gain_copy(m).start()
+    gain_out[7] = gains[:, tile_of(dp)]
+    for load in branch_loads:
+        load.wait()
+
+    def mixed_rows(i):
+        window = pl.ds(pl.multiple_of(i * ROWS, ROWS), ROWS)
+        staged[1, window, :] = staged[1, window, :] + y_in[window, :]
+
+    loop(half // ROWS, mixed_rows)
+    mixed_copy = remote(staged.at[1], core_in, end_send.at[5], end_recv.at[5], twin_id)
+    mixed_copy.start()
+
+    def put_mixed(source, which, first):
+        def narrow(i):
+            window = pl.ds(pl.multiple_of(i * ROWS, ROWS), ROWS)
+            tok[window, :] = source[window, :].astype(BF16)
+
+        loop(half // ROWS, narrow)
+        copies = [
+            pltpu.make_async_copy(
+                tok.at[pl.ds(block * run, run)], mixed_out.at[pl.ds(own_row(block, which), run)],
+                load_sem.at[first + block],
+            )
+            for block in range(2)
+        ]
+        for copy in copies:
+            copy.start()
+        for copy in copies:
+            copy.wait()
+
+    put_mixed(staged.at[1], core, 7)
+    mixed_copy.wait()
+    put_mixed(core_in, 1 - core, 9)
+
+    for copy in part_stores + input_stores + input_copies:
+        copy.wait()
+    for m in range(7):
+        gain_copy(m).wait()
+    for slot in range(2):
+        for copy in x_copies(slot):
+            copy.wait_send()
+    for copy in z_copies():
+        copy.wait()
+    for part in range(2):
+        loop(tiles, lambda j: row_copy(j)[part].wait())
+
+
+def last(
+    normed_others, cot_others, normed, cot, act, gg, gu, w_gate, w_up, w_down,
+    projected, branch, gain_two, w_query, w_key, w_value, heads, grad_attn, grad_attn_far,
+    normed_one, normed_one_far, heads_far, grad_hidden, tokens, gain,
+):
+    row_count, width = tokens.shape
+    half = row_count // 2
+    tiles = width // TILE
+    hidden_units = w_gate.shape[1]
+    hbm = pl.BlockSpec(memory_space=pl.ANY)
+    vmem = pl.BlockSpec(memory_space=pltpu.VMEM)
+    wide = jax.ShapeDtypeStruct((half, width), F32)
+    rows_pair = jax.ShapeDtypeStruct((2, TILE, hidden_units), F32)
+    columns = jax.ShapeDtypeStruct((hidden_units, TILE), F32)
+    out_block = jax.ShapeDtypeStruct((512, TILE), F32)
+    proj_block = jax.ShapeDtypeStruct((TILE, 768), F32)
+    dma = pltpu.SemaphoreType.DMA
+    return pl.pallas_call(
+        last_kernel,
+        out_shape=(
+            rows_pair, rows_pair, rows_pair, columns, columns, columns, out_block, out_block, proj_block, proj_block,
+            jax.ShapeDtypeStruct((row_count, width), F32),
+            jax.ShapeDtypeStruct((row_count, width), BF16),
+            wide,
+            jax.ShapeDtypeStruct((2, half, width), F32),
+            jax.ShapeDtypeStruct((2, half, width), F32),
+            jax.ShapeDtypeStruct((8, 2, TILE), F32),
+        ),
+        in_specs=[hbm] * 12 + [vmem] + [hbm] * 11 + [vmem],
+        out_specs=(hbm,) * 15 + (vmem,),
+        scratch_shapes=[
+            pltpu.VMEM((6 * half, width), BF16),
+            pltpu.VMEM((6 * half, width), BF16),
+            pltpu.VMEM((2 * TILE, row_count + 6 * half), BF16),
+            pltpu.VMEM((2 * TILE, row_count + 6 * half), BF16),
+            pltpu.VMEM((3, row_count + 6 * half, TILE), BF16),
+            pltpu.VMEM((2, width, TILE), BF16),
+            pltpu.VMEM((2, width, TILE), BF16),
+            pltpu.VMEM((2, TILE, width), BF16),
+            pltpu.VMEM((2, 3, 2 * TILE, TILE), F32),
+            pltpu.VMEM((2, half, width), F32),
+            pltpu.VMEM((half, width), F32),
+            pltpu.VMEM((half, width), F32),
+            pltpu.VMEM((width, 768), BF16),
+            pltpu.VMEM((half, width), BF16),
+            pltpu.VMEM((2, row_count, 512), BF16),
+            pltpu.VMEM((2, row_count, 1024), BF16),
+            pltpu.VMEM((2, row_count, 1024), BF16),
+            pltpu.VMEM((2, row_count, 768), BF16),
+            pltpu.VMEM((2, 2, 512, TILE), F32),
+            pltpu.VMEM((2, 2, TILE, 768), F32),
+            pltpu.VMEM((2, 512, TILE), F32),
+            pltpu.VMEM((2, TILE, 768), F32),
+            pltpu.VMEM((2, half, 768), F32),
+            pltpu.VMEM((half, 1024), F32),
+            pltpu.VMEM((2, width), F32),
+            pltpu.VMEM((2, width), F32),
+            dma((15,)), dma((6,)), dma((2, 3)), dma((3,)), dma((2, 4)),
+            dma((2, tiles)), dma((2, tiles)),
+            dma((tiles,)), dma((tiles,)), dma((tiles,)), dma((tiles,)),
+            dma((2, 2)), dma((2, 2)), dma((2,)), dma((2,)), dma((7,)), dma((7,)), dma((8,)), dma((8,)),
+            dma((6,)), dma((6,)), pltpu.VMEM((row_count, TILE), F32),
+        ],
+        compiler_params=pltpu.CompilerParams(
+            collective_id=1, has_side_effects=True, vmem_limit_bytes=64 * 1024 * 1024
+        ),
+        name="weight_gradients",
+    )(
+        normed_others, cot_others, normed, cot, act, gg, gu, w_gate, w_up, w_down,
+        projected, branch, gain_two, w_query, w_key, w_value, heads, grad_attn, grad_attn_far,
         normed_one, normed_one_far, heads_far, grad_hidden, tokens, gain.reshape(1, width),
     )
 
@@ -1369,9 +2405,7 @@
         grad_attn,
         projected,
         grad_attn_far,
-        projected_far,
-        mixed_half,
-        mixed_twin,
+        branch,
         normed_two,
         activation,
         grad_gate_in,
@@ -1381,42 +2415,41 @@
         normed_others,
     ) = middle(
         w_query, key_weight, value_weight, w_out, tokens, cotangent,
-        half_of(cotangent, core).astype(F32), attn_gain, mlp_gain, w_gate, w_up, w_down,
-        segments, cosine_tile, sine_tile,
-    )
-    gain_two_half = gain_two_half[0]
-    mixed = joined(mixed_half, mixed_twin, core).astype(BF16)
+        attn_gain, mlp_gain, w_gate, w_up, w_down, segments, cosine_tile, sine_tile,
+    )
     (
         kept,
         _,
         came,
+        down_kept,
+        _,
+        down_came,
         out_mine,
         out_came,
         proj_mine,
         proj_came,
-        input_half,
-        input_twin,
-        gain_one_half,
+        grad_input,
+        mixed,
+        _,
+        _,
+        _,
+        gains,
     ) = last(
         normed_others, cotangent_others, normed_two, cotangent, activation, grad_gate_in,
-        grad_up_in, w_gate, w_up, w_down, projected, projected_far, w_query, key_weight,
+        grad_up_in, w_gate, w_up, w_down, projected, branch, gain_two_half, w_query, key_weight,
         value_weight, head_outputs, grad_attn, grad_attn_far, normed_one, normed_one_far,
         heads_far, grad_hidden, tokens, attn_gain,
     )
-    gain_one_half = gain_one_half[0]
-    grad_input = joined(input_half, input_twin, core)
     grad_w_gate = kept[0] + came[0]
     grad_w_up = kept[1] + came[1]
-    grad_w_down = (kept[2] + came[2]).T
+    grad_w_down = down_kept + down_came
     grad_w_out = out_mine + out_came
     grad_w_proj = proj_mine + proj_came
     grad_w_query = grad_w_proj[:, :query_width]
     grad_w_key = grad_w_proj[:, query_width : query_width + kv_width]
     grad_w_value = grad_w_proj[:, query_width + kv_width :]
 
-    gains = jnp.stack([gain_one_half, gain_two_half])
-    gains = gains + swap(gains, "tensor", 1)
-    gains = reduced(lambda offsets: blocks(gains, offsets), all_bits)
+    gains = jnp.sum(gains, axis=0)
     grad_attn_gain, grad_mlp_gain = gains[0], gains[1]
     return (
         mixed,

time: 475 us -> 412 us (0.87)
  Pallas kernels: 431 us -> 389 us
  other arithmetic: 28.3 us -> 13 us
  starting transfers between devices: 7.47 us -> 0 us
    pallas_call x1, Pallas kernels: 233 us -> 174 us  [middle(): pl.pallas_call(middle_kernel, out_shape=(jax.ShapeDtypeStruct((row_count,...]
    pallas_call x1, Pallas kernels: 198 us -> 215 us  [last(): pl.pallas_call(last_kernel, out_shape=(rows_pair, rows_pair, rows_pair, c...]
    transpose x1 -> x0, other arithmetic: 8.52 us -> none  [body(): grad_w_down = (kept[2] + came[2]).T]
    concatenate x2 -> x0, other arithmetic: 7.47 us -> none  [joined(): return jnp.concatenate([first, second], axis=0)]
    ppermute x8 -> x0, starting transfers between devices: 7.47 us -> none  [swap(): return lax.ppermute(value, axis, [(i, i ^ bit) for i in range(size)])]
    add x4 -> x2, other arithmetic: 0.05 us -> 6.12 us  [the longest x1 3.34 us: body(): grad_w_down = down_kept + down_came]
  transfers between devices with their start and end apart: 8 -> 0, of which waited for: 0 -> 0; matrix products, arithmetic and copies ran while one was open for 5% -> 0% of each run, Pallas kernels for 0% -> 0%
where the time goes in v4:
time: 412 us; the launch traced here: 411 us
  Pallas kernels  389 us (94%)
  other arithmetic  13 us (3%)
  local copies, waits for them, and re-layouts  8.75 us (2%)
    pallas_call x1, Pallas kernels, last(): pl.pallas_call(last_kernel, out_shape=(rows_pair, rows_pair, rows_pair, c...  215 us
    pallas_call x1, Pallas kernels, middle(): pl.pallas_call(middle_kernel, out_shape=(jax.ShapeDtypeStruct((row_count,...  174 us

profile of v4, /device:TPU:0, one launch (start us, length us, event | category | flops | bytes accessed | tf_op | source)
XLA Modules:
  0.0 411.2 jit_solution(5889582288219358577)
XLA Ops:
  0.7 0.1 mul.27
  0.8 0.7 convert_element_type.18
  1.4 1.5 copy.24.segment_column_ref
  3.0 1.8 fusion
  4.8 174.2 %feed_forward.1 = (bf16[512,2048]{1,0:T(8,128)(2,1)}, bf16[512,512]{1,0:T(8,128)(2,1)}, bf16[512,512]{1,0:T(8,128)(2,1)}, bf16[512,512]{1,0:T(8,128)(2,1)}, bf16...) custom-call(bf16[2048,512]{1,0:T(8,128)(2,1)} %w_query_ref.3, ...), custom_call_target="tpu_custom_call" | custom-call | tf_op jit(solution)/shard_map/feed_forward/pallas_call | solution.py:775
  179.0 214.6 %weight_gradients.1 = (f32[2,256,2048]{2,1,0:T(8,128)}, f32[2,256,2048]{2,1,0:T(8,128)}, f32[2,256,2048]{2,1,0:T(8,128)}, f32[2048,256]{1,0:T(8,128)}, f32[2048,...) custom-call(f32[5,256,2048]{2,1,0:T(8,128)} %get-tuple-element.38.no, ...), custom_call_target="tpu_custom_call" | custom-call | tf_op jit(solution)/shard_map/weight_gradients/pallas_call | solution.py:2282
  393.6 0.0 copy-start.5
  393.6 0.8 reduce_sum.9
  394.4 0.6 fusion.2
  394.9 0.0 copy-start.3
  394.9 2.2 add.33
  397.2 0.0 copy-done.5
  397.2 1.4 add.32
  398.5 0.7 fusion.1
  399.2 0.9 slice.37
  400.1 0.0 copy-done.3
  400.1 3.3 add.38
  403.5 0.0 copy-done.1
  403.5 0.0 copy-done
  403.5 2.8 add_bitcast_fusion
  406.2 0.0 copy-done.4
  406.2 1.3 copy.27
  407.6 1.6 copy-done.2
  409.2 2.0 copy.28
  (7 shorter events, 0.0 us)
Async XLA Ops:
  393.6 3.6 copy-start.5
  394.9 5.2 %copy-start.3 = (f32[2048,256]{1,0:T(8,128)S(1)}, f32[2048,256]{1,0:T(8,128)}, u32[]{:S(2)}) copy-start(f32[2048,256]{1,0:T(8,128)} %get-tuple-element.63) | copy-start | bytes 6291460
  397.2 6.3 %copy-start.1 = (f32[2,256,2048]{2,1,0:T(8,128)S(1)}, f32[2,256,2048]{2,1,0:T(8,128)}, u32[]{:S(2)}) copy-start(f32[2,256,2048]{2,1,0:T(8,128)} %get-tuple-element.62) | copy-start | bytes 12582916
  400.1 3.3 copy-start
  403.5 2.8 copy-start.4
  406.2 2.9 copy-start.2

commit v5 on v4

--- a/solution.py
+++ b/solution.py
@@ -12,22 +12,6 @@
 MASKED = -1e30
 F32 = jnp.float32
 BF16 = jnp.bfloat16
-
-
-def swap(value, axis, bit):
-    size = lax.axis_size(axis)
-    return lax.ppermute(value, axis, [(i, i ^ bit) for i in range(size)])
-
-
-def half_of(value, which, dim=0):
-    size = value.shape[dim] // 2
-    return lax.dynamic_slice_in_dim(value, which * size, size, dim)
-
-
-def joined(mine, other, which):
-    first = jnp.where(which == 0, mine, other)
-    second = jnp.where(which == 0, other, mine)
-    return jnp.concatenate([first, second], axis=0)
 
 
 MESH = pl.DeviceIdType.MESH
@@ -56,8 +40,7 @@
     w_gate_ref,
     w_up_ref,
     w_down_ref,
-    segment_column_ref,
-    segment_row_ref,
+    segment_ref,
     cosine_ref,
     sine_ref,
     normed_one_out,
@@ -83,7 +66,7 @@
     up_w,
     down_w,
     cot,
-    hidden,
+    cot_half,
     normed,
     normed_sent,
     normed_twin,
@@ -96,6 +79,7 @@
     y_in,
     product,
     log_total_ref,
+    segment_column,
     local_sem,
     core_send,
     core_recv,
@@ -111,6 +95,7 @@
     hidden_recv,
     far_send,
     far_recv,
+    free_sem,
 ):
     dp, tensor = lax.axis_index("dp"), lax.axis_index("tensor")
     core, y_bit = tensor % 2, (tensor // 2) % 2
@@ -120,7 +105,7 @@
     x_id = (flip(dp, 1), tensor)
     z_id = (flip(dp, 4), tensor)
     far_id = (flip(dp, 2), tensor)
-    half, width = hidden.shape
+    half, width = cot_half.shape
     run = half // 2
     row_count = 2 * half
     hidden_units = gate_w.shape[1]
@@ -131,7 +116,7 @@
     everything = slice(None)
     heads = gg.at[:, pl.ds(0, query_width)]
     tok = gu
-    cot_half = mine.at[1]
+    hidden = core_in.at[0]
 
     def own_row(block, which):
         return pl.multiple_of(block * half + which * run, run)
@@ -246,32 +231,34 @@
         return pl.ds(pl.multiple_of(b * 1024 + (1 - z_low) * 512, 512), 512)
 
     gain_one = gain_one_ref[...]
+    segments = segment_ref[...].astype(F32)
+    segment_column[...] = jnp.broadcast_to(segments, (8, row_count)).T
     loads["tok"].wait()
 
-    def first_norm(i):
-        window = pl.ds(pl.multiple_of(i * ROWS, ROWS), ROWS)
-        values = tok[window, :].astype(F32)
-        scale = lax.rsqrt(jnp.mean(values * values, axis=-1, keepdims=True) + EPSILON)
-        normed[window, :] = (values * scale * gain_one).astype(BF16)
-
-    loop(row_count // ROWS, first_norm)
+    def first_norm(block):
+        def step(i):
+            window = pl.ds(pl.multiple_of(block * half + i * ROWS, ROWS), ROWS)
+            values = tok[window, :].astype(F32)
+            scale = lax.rsqrt(jnp.mean(values * values, axis=-1, keepdims=True) + EPSILON)
+            normed[window, :] = (values * scale * gain_one).astype(BF16)
+
+        loop(half // ROWS, step)
+
     normed_one_store = pltpu.make_async_copy(normed, normed_one_out, local_sem.at[9])
-    normed_one_store.start()
-
-    for block in range(2):
-
-        def stage_far(i, block=block):
+
+    def stage_far(block):
+        def step(i):
             window = pl.ds(pl.multiple_of(block * run + i * ROWS, ROWS), ROWS)
             here = pl.ds(pl.multiple_of(own_row(block, core) + i * ROWS, ROWS), ROWS)
             for b in range(2):
                 core_in[2, window, pl.ds(b * 512, 512)] = normed[here, far_columns(b)].astype(F32)
 
-        loop(run // ROWS, stage_far)
+        loop(run // ROWS, step)
+
     normed_one_copy = remote(
         core_in.at[2, :, pl.ds(0, 1024)], normed_one_far.at[0],
         far_send.at[0], far_recv.at[0], far_id,
     )
-    normed_one_copy.start()
 
     lane = lax.broadcasted_iota(jnp.int32, (TILE, 128), 1)
     factor = HEAD_SIZE ** (-0.5)
@@ -323,7 +310,7 @@
         key_place = lax.broadcasted_iota(jnp.int32, (keys_seen, TILE), 0)
         query_place = lax.broadcasted_iota(jnp.int32, (keys_seen, TILE), 1) + block * TILE
         return (key_place <= query_place) & (
-            segment_column_ref[pl.ds(0, keys_seen), :] == segment_row_ref[:, window]
+            segment_column[pl.ds(0, keys_seen), pl.ds(0, 1)] == segments[:, block * TILE : (block + 1) * TILE]
         )
 
     def attend(block, p):
@@ -355,7 +342,7 @@
 
     def core_copy(which, window, k):
         return remote(
-            away.at[window], core_in.at[which].at[window],
+            away.at[window], core_in.at[min(which, 1)].at[window],
             core_send.at[which, k], core_recv.at[which, k], twin_id,
         )
 
@@ -376,6 +363,12 @@
     def tile_of(j):
         return pl.ds(pl.multiple_of(j * TILE, TILE), TILE)
 
+    first_norm(0)
+    first_norm(1)
+    normed_one_store.start()
+    stage_far(0)
+    stage_far(1)
+    normed_one_copy.start()
     for name in ("query", "key", "value", "w_out"):
         loads[name].wait()
     for block in range(2):
@@ -496,15 +489,10 @@
 
         if block == 0:
             loop(hidden_units // TILE, units)
-            quarter_z().wait()
-            quarter_zx().start()
             for k in range(CHUNKS):
-                from_x(cot_half, cot_others, k, cot_send, cot_recv).wait_send()
                 core_copy(0, row_windows[k], k).wait_send()
         else:
             loop(hidden_units // TILE, units)
-            normed_one_copy.wait()
-            heads_copy.wait()
 
         def produce(j, block=block, window=window):
             split_tile(1, block, tile_of(j), lax.dot_general(
@@ -535,10 +523,9 @@
     ]
     for store in stores:
         store.start()
-    normed_one_twin = remote(
-        normed_one_far.at[0], normed_one_far.at[1], far_send.at[2], far_recv.at[2], twin_id
-    )
-    normed_one_twin.start()
+    pl.semaphore_signal(free_sem, inc=1, device_id=twin_id, device_id_type=MESH)
+    quarter_z().wait()
+    quarter_zx().start()
 
     for block in range(2):
         loop(tiles, lambda j: core_copy(1, block_window(block, j), block * tiles + j).wait_send())
@@ -555,12 +542,13 @@
 
     def branch_add(j):
         core_copy(2, (everything, tile_of(j)), j).wait_recv()
-        mine[0, :, tile_of(j)] = mine[0, :, tile_of(j)] + core_in[2, :, tile_of(j)]
+        mine[0, :, tile_of(j)] = mine[0, :, tile_of(j)] + core_in[1, :, tile_of(j)]
 
     def branch_step(j):
         branch_produce(j + 1)
         branch_add(j)
 
+    pl.semaphore_wait(free_sem, 1)
     branch_produce(0)
     loop(tiles - 1, branch_step)
     branch_add(tiles - 1)
@@ -584,12 +572,6 @@
     ]
     for operand in operands:
         operand.start()
-    for k in (0, 1):
-        from_z(normed_sent, normed_others, k, n_send, n_recv).wait_recv()
-        from_zx(normed_others, k, n_send, n_recv).start()
-    for k in range(CHUNKS):
-        from_x(cot_half, cot_others, k, cot_send, cot_recv).wait_recv()
-    to_twin(cot_others, 0, 0).start()
     for operand in operands:
         operand.wait()
 
@@ -698,6 +680,13 @@
 
         loop(512 // TILE, head_tile)
         loop(query_width // 128, functools.partial(attend_back, block))
+        if block == 0:
+            for k in (0, 1):
+                from_z(normed_sent, normed_others, k, n_send, n_recv).wait_recv()
+                from_zx(normed_others, k, n_send, n_recv).start()
+            for k in range(CHUNKS):
+                from_x(cot_half, cot_others, k, cot_send, cot_recv).wait()
+            to_twin(cot_others, 0, 0).start()
 
     grad_stores = [
         pltpu.make_async_copy(core_in.at[0], grad_hidden_out, local_sem.at[4]),
@@ -724,6 +713,12 @@
 
     last_z().wait()
     last_y().start()
+    normed_one_copy.wait()
+    normed_one_twin = remote(
+        normed_one_far.at[0], normed_one_far.at[1], far_send.at[2], far_recv.at[2], twin_id
+    )
+    normed_one_twin.start()
+    heads_copy.wait()
     for block in range(2):
         for b in range(2):
             hidden_far(block, b).wait()
@@ -790,7 +785,7 @@
             jax.ShapeDtypeStruct((5, half, width), F32),
             jax.ShapeDtypeStruct((5, half, width), F32),
         ),
-        in_specs=[hbm] * 6 + [vmem] * 2 + [hbm] * 3 + [vmem] * 4,
+        in_specs=[hbm] * 6 + [vmem] * 2 + [hbm] * 3 + [vmem] * 3,
         out_specs=(hbm,) * 16 + (vmem,) + (hbm,) * 2,
         scratch_shapes=[
             pltpu.VMEM(w_gate.shape, BF16),
@@ -810,6 +805,7 @@
             pltpu.VMEM((2, half, width), F32),
             pltpu.VMEM((half, TILE), F32),
             pltpu.VMEM((8, row_count), F32),
+            pltpu.VMEM((row_count, 8), F32),
             dma((13,)),
             dma((3, 2 * tiles)), dma((3, 2 * tiles)), dma((2, 2 * tiles)), dma((2, 2 * tiles)),
             dma((3, CHUNKS)), dma((3, CHUNKS)),
@@ -817,6 +813,7 @@
             dma((2, 2)), dma((2, 2)),
             dma((CHUNKS,)), dma((CHUNKS,)),
             dma((8,)), dma((8,)),
+            pltpu.SemaphoreType.REGULAR,
         ],
         compiler_params=pltpu.CompilerParams(
             collective_id=0, has_side_effects=True, vmem_limit_bytes=64 * 1024 * 1024
@@ -825,7 +822,7 @@
     )(
         w_query, w_key, w_value, w_out, tokens, cotangent,
         gain_one.reshape(1, width), gain.reshape(1, width), w_gate, w_up, w_down,
-        segment.reshape(row_count, 1), segment.reshape(1, row_count), cosine, sine,
+        segment.reshape(1, row_count), cosine, sine,
     )
 
 
@@ -1540,6 +1537,57 @@
     )
 
 
+def finish_kernel(
+    kept, came, down_kept, down_came, out_mine, out_came, proj_mine, proj_came, input_in,
+    mixed_in, gains, w_gate, w_up, w_down, w_out, w_query, w_key, w_value, grad_input, mixed,
+    gain_sums,
+):
+    w_gate[...] = kept[0] + came[0]
+    w_up[...] = kept[1] + came[1]
+    w_down[...] = down_kept[...] + down_came[...]
+    w_out[...] = out_mine[...] + out_came[...]
+    queries, keys = w_query.shape[1], w_key.shape[1]
+    w_query[...] = proj_mine[:, :queries] + proj_came[:, :queries]
+    w_key[...] = proj_mine[:, queries : queries + keys] + proj_came[:, queries : queries + keys]
+    w_value[...] = proj_mine[:, queries + keys :] + proj_came[:, queries + keys :]
+    grad_input[...] = input_in[...]
+    mixed[...] = mixed_in[...]
+    gain_sums[...] = jnp.sum(gains[...], axis=0)
+
+
+def finish(*parts):
+    steps = 8
+    kept, down, out, proj, whole, gains = (parts[i] for i in (0, 2, 4, 6, 8, 10))
+    rows, units = kept.shape[1:]
+
+    def block(array, lead=()):
+        size = array[len(lead) :]
+        shape = lead + (size[0] // steps,) + size[1:]
+        return pl.BlockSpec(shape, lambda i: (0,) * len(lead) + (i,) + (0,) * (len(size) - 1))
+
+    fixed = lambda shape: pl.BlockSpec(shape, lambda i: (0,) * len(shape))
+    outs = [
+        (rows, units), (rows, units), down.shape, out.shape,
+        (proj.shape[0], 512), (proj.shape[0], 128), (proj.shape[0], 128), whole.shape,
+    ]
+    return pl.pallas_call(
+        finish_kernel,
+        grid=(steps,),
+        out_shape=[jax.ShapeDtypeStruct(shape, F32) for shape in outs]
+        + [
+            jax.ShapeDtypeStruct(whole.shape, BF16),
+            jax.ShapeDtypeStruct(gains.shape[1:], F32),
+        ],
+        in_specs=[block(kept.shape, (2,))] * 2
+        + [block(part.shape) for part in parts[2:10]]
+        + [fixed(gains.shape)],
+        out_specs=[block(shape) for shape in outs]
+        + [block(whole.shape), fixed(gains.shape[1:])],
+        compiler_params=pltpu.CompilerParams(vmem_limit_bytes=64 * 1024 * 1024),
+        name="last_sums",
+    )(*parts)
+
+
 def body(
     tokens,
     segments,
@@ -1555,9 +1603,6 @@
     w_down,
     cotangent,
 ):
-    groups = lax.axis_size("dp")
-    place = lax.axis_index("dp")
-    core = lax.axis_index("tensor") % 2
     row_count, width = tokens.shape
     half = row_count // 2
     hidden_units = w_gate.shape[1]
@@ -1586,7 +1631,7 @@
             jax.ShapeDtypeStruct((5, half, width), F32),
             jax.ShapeDtypeStruct((5, half, width), F32),
         ),
-        in_specs=[hbm] * 6 + [vmem] * 2 + [hbm] * 3 + [vmem] * 4,
+        in_specs=[hbm] * 6 + [vmem] * 2 + [hbm] * 3 + [vmem] * 3,
         out_specs=(hbm,) * 16 + (vmem,) + (hbm,) * 2,
         scratch_shapes=[
             pltpu.VMEM(w_gate.shape, BF16),
@@ -1606,6 +1651,7 @@
             pltpu.VMEM((2, half, width), F32),
             pltpu.VMEM((half, TILE), F32),
             pltpu.VMEM((8, row_count), F32),
+            pltpu.VMEM((row_count, 8), F32),
             dma((13,)),
             dma((3, 2 * tiles)), dma((3, 2 * tiles)), dma((2, 2 * tiles)), dma((2, 2 * tiles)),
             dma((3, CHUNKS)), dma((3, CHUNKS)),
@@ -1613,6 +1659,7 @@
             dma((2, 2)), dma((2, 2)),
             dma((CHUNKS,)), dma((CHUNKS,)),
             dma((8,)), dma((8,)),
+            pltpu.SemaphoreType.REGULAR,
         ],
         compiler_params=pltpu.CompilerParams(
             collective_id=0, has_side_effects=True, vmem_limit_bytes=64 * 1024 * 1024
@@ -1621,7 +1668,7 @@
     )(
         w_query, w_key, w_value, w_out, tokens, cotangent,
         gain_one.reshape(1, width), gain.reshape(1, width), w_gate, w_up, w_down,
-        segment.reshape(row_count, 1), segment.reshape(1, row_count), cosine, sine,
+        segment.reshape(1, row_count), cosine, sine,
     )
 
 
@@ -2336,6 +2383,57 @@
     )
 
 
+def finish_kernel(
+    kept, came, down_kept, down_came, out_mine, out_came, proj_mine, proj_came, input_in,
+    mixed_in, gains, w_gate, w_up, w_down, w_out, w_query, w_key, w_value, grad_input, mixed,
+    gain_sums,
+):
+    w_gate[...] = kept[0] + came[0]
+    w_up[...] = kept[1] + came[1]
+    w_down[...] = down_kept[...] + down_came[...]
+    w_out[...] = out_mine[...] + out_came[...]
+    queries, keys = w_query.shape[1], w_key.shape[1]
+    w_query[...] = proj_mine[:, :queries] + proj_came[:, :queries]
+    w_key[...] = proj_mine[:, queries : queries + keys] + proj_came[:, queries : queries + keys]
+    w_value[...] = proj_mine[:, queries + keys :] + proj_came[:, queries + keys :]
+    grad_input[...] = input_in[...]
+    mixed[...] = mixed_in[...]
+    gain_sums[...] = jnp.sum(gains[...], axis=0)
+
+
+def finish(*parts):
+    steps = 8
+    kept, down, out, proj, whole, gains = (parts[i] for i in (0, 2, 4, 6, 8, 10))
+    rows, units = kept.shape[1:]
+
+    def block(array, lead=()):
+        size = array[len(lead) :]
+        shape = lead + (size[0] // steps,) + size[1:]
+        return pl.BlockSpec(shape, lambda i: (0,) * len(lead) + (i,) + (0,) * (len(size) - 1))
+
+    fixed = lambda shape: pl.BlockSpec(shape, lambda i: (0,) * len(shape))
+    outs = [
+        (rows, units), (rows, units), down.shape, out.shape,
+        (proj.shape[0], 512), (proj.shape[0], 128), (proj.shape[0], 128), whole.shape,
+    ]
+    return pl.pallas_call(
+        finish_kernel,
+        grid=(steps,),
+        out_shape=[jax.ShapeDtypeStruct(shape, F32) for shape in outs]
+        + [
+            jax.ShapeDtypeStruct(whole.shape, BF16),
+            jax.ShapeDtypeStruct(gains.shape[1:], F32),
+        ],
+        in_specs=[block(kept.shape, (2,))] * 2
+        + [block(part.shape) for part in parts[2:10]]
+        + [fixed(gains.shape)],
+        out_specs=[block(shape) for shape in outs]
+        + [block(whole.shape), fixed(gains.shape[1:])],
+        compiler_params=pltpu.CompilerParams(vmem_limit_bytes=64 * 1024 * 1024),
+        name="last_sums",
+    )(*parts)
+
+
 def body(
     tokens,
     segments,
@@ -2440,16 +2538,21 @@
         value_weight, head_outputs, grad_attn, grad_attn_far, normed_one, normed_one_far,
         heads_far, grad_hidden, tokens, attn_gain,
     )
-    grad_w_gate = kept[0] + came[0]
-    grad_w_up = kept[1] + came[1]
-    grad_w_down = down_kept + down_came
-    grad_w_out = out_mine + out_came
-    grad_w_proj = proj_mine + proj_came
-    grad_w_query = grad_w_proj[:, :query_width]
-    grad_w_key = grad_w_proj[:, query_width : query_width + kv_width]
-    grad_w_value = grad_w_proj[:, query_width + kv_width :]
-
-    gains = jnp.sum(gains, axis=0)
+    (
+        grad_w_gate,
+        grad_w_up,
+        grad_w_down,
+        grad_w_out,
+        grad_w_query,
+        grad_w_key,
+        grad_w_value,
+        grad_input,
+        mixed,
+        gains,
+    ) = finish(
+        kept, came, down_kept, down_came, out_mine, out_came, proj_mine, proj_came, grad_input,
+        mixed, gains,
+    )
     grad_attn_gain, grad_mlp_gain = gains[0], gains[1]
     return (
         mixed,
@@ -2484,6 +2587,22 @@
 
 def narrowed(value):
     return jnp.where(value == value, value, 0.0).astype(BF16)
+
+
+def swap(value, axis, bit):
+    size = lax.axis_size(axis)
+    return lax.ppermute(value, axis, [(i, i ^ bit) for i in range(size)])
+
+
+def half_of(value, which, dim=0):
+    size = value.shape[dim] // 2
+    return lax.dynamic_slice_in_dim(value, which * size, size, dim)
+
+
+def joined(mine, other, which):
+    first = jnp.where(which == 0, mine, other)
+    second = jnp.where(which == 0, other, mine)
+    return jnp.concatenate([first, second], axis=0)
 
 
 def tensor_sum_half(partial, core):

time: 412 us -> 385 us (0.934)
  other arithmetic: 13 us -> 2.5 us
  Pallas kernels: 389 us -> 380 us
  local copies, waits for them, and re-layouts: 8.75 us -> 1.39 us
    pallas_call x1, Pallas kernels: 174 us -> 152 us  [middle(): pl.pallas_call(middle_kernel, out_shape=(jax.ShapeDtypeStruct((row_count,...]
    pallas_call x0 -> x1, Pallas kernels: none -> 13.5 us  [finish(): pl.pallas_call(finish_kernel, grid=(steps,), out_shape=[jax.ShapeDtypeStr...]
    add x4 -> x0, other arithmetic: 9.69 us -> none  [the longest x1 3.34 us: body(): grad_w_down = down_kept + down_came]
    unnamed x14 -> x0, local copies, waits for them, and re-layouts: 4.98 us -> none
where the time goes in v5:
time: 385 us
  Pallas kernels  380 us (99%)
    pallas_call x1, Pallas kernels, last(): pl.pallas_call(last_kernel, out_shape=(rows_pair, rows_pair, rows_pair, c...  215 us
    pallas_call x1, Pallas kernels, middle(): pl.pallas_call(middle_kernel, out_shape=(jax.ShapeDtypeStruct((row_count,...  152 us
    pallas_call x1, Pallas kernels, finish(): pl.pallas_call(finish_kernel, grid=(steps,), out_shape=[jax.ShapeDtypeStr...  13.5 us

profile of v5, /device:TPU:0, one launch (start us, length us, event | category | flops | bytes accessed | tf_op | source)
XLA Modules:
  0.0 384.7 jit_solution(15320206987935230294)
XLA Ops:
  0.7 0.1 mul.27
  0.8 0.7 convert_element_type.18
  1.4 1.8 fusion
  3.2 152.1 %feed_forward.1 = (bf16[512,2048]{1,0:T(8,128)(2,1)}, bf16[512,512]{1,0:T(8,128)(2,1)}, bf16[512,512]{1,0:T(8,128)(2,1)}, bf16[512,512]{1,0:T(8,128)(2,1)}, bf16...) custom-call(bf16[2048,512]{1,0:T(8,128)(2,1)} %w_query_ref.3, ...), custom_call_target="tpu_custom_call" | custom-call | tf_op jit(solution)/shard_map/feed_forward/pallas_call | solution.py:770
  155.4 214.6 %weight_gradients.1 = (f32[2,256,2048]{2,1,0:T(8,128)}, f32[2,256,2048]{2,1,0:T(8,128)}, f32[2,256,2048]{2,1,0:T(8,128)}, f32[2048,256]{1,0:T(8,128)}, f32[2048,...) custom-call(f32[5,256,2048]{2,1,0:T(8,128)} %get-tuple-element.48.no, ...), custom_call_target="tpu_custom_call" | custom-call | tf_op jit(solution)/shard_map/weight_gradients/pallas_call | solution.py:2329
  370.0 13.5 %last_sums.1 = (f32[256,2048]{1,0:T(8,128)}, f32[256,2048]{1,0:T(8,128)}, f32[2048,256]{1,0:T(8,128)}, f32[512,256]{1,0:T(8,128)}, f32[256,512]{1,0:T(8,128)}, /...) custom-call(f32[2,256,2048]{2,1,0:T(8,128)} %get-tuple-element.64.ke, ...), custom_call_target="tpu_custom_call" | custom-call | tf_op jit(solution)/shard_map/last_sums/pallas_call | solution.py:2419
  383.4 1.3 fusion.1
  (3 shorter events, 0.0 us)

commit v6 on v5

--- a/solution.py
+++ b/solution.py
@@ -41,8 +41,8 @@
     w_up_ref,
     w_down_ref,
     segment_ref,
-    cosine_ref,
-    sine_ref,
+    position_ref,
+    frequency_ref,
     normed_one_out,
     heads_out,
     query_ref,
@@ -80,6 +80,8 @@
     product,
     log_total_ref,
     segment_column,
+    cosine_ref,
+    sine_ref,
     local_sem,
     core_send,
     core_recv,
@@ -260,6 +262,13 @@
         far_send.at[0], far_recv.at[0], far_id,
     )
 
+    places = jnp.broadcast_to(position_ref[...].astype(F32), (8, row_count)).T
+    angles = places[:, 0:1] * frequency_ref[...]
+    cosine_ref[...] = jnp.cos(angles)
+    signs = lax.broadcasted_iota(jnp.int32, (row_count, 128), 1) % 64 < 32
+    sines = jnp.sin(angles)
+    sine_ref[...] = jnp.where(signs, sines, -sines)
+
     lane = lax.broadcasted_iota(jnp.int32, (TILE, 128), 1)
     factor = HEAD_SIZE ** (-0.5)
 
@@ -755,7 +764,7 @@
 
 def middle(
     w_query, w_key, w_value, w_out, tokens, cotangent, gain_one, gain,
-    w_gate, w_up, w_down, segment, cosine, sine,
+    w_gate, w_up, w_down, segment, position, frequency,
 ):
     row_count, width = tokens.shape
     half = row_count // 2
@@ -806,6 +815,8 @@
             pltpu.VMEM((half, TILE), F32),
             pltpu.VMEM((8, row_count), F32),
             pltpu.VMEM((row_count, 8), F32),
+            pltpu.VMEM((row_count, 128), F32),
+            pltpu.VMEM((row_count, 128), F32),
             dma((13,)),
             dma((3, 2 * tiles)), dma((3, 2 * tiles)), dma((2, 2 * tiles)), dma((2, 2 * tiles)),
             dma((3, CHUNKS)), dma((3, CHUNKS)),
@@ -822,8 +833,11 @@
     )(
         w_query, w_key, w_value, w_out, tokens, cotangent,
         gain_one.reshape(1, width), gain.reshape(1, width), w_gate, w_up, w_down,
-        segment.reshape(1, row_count), cosine, sine,
-    )
+        segment.reshape(1, row_count), position.reshape(1, row_count), frequency.reshape(1, 128),
+    )
+
+
+LAST = 2
 
 
 def last_kernel(
@@ -858,6 +872,7 @@
     down_kept,
     down_sent,
     down_came,
+    down_last,
     out_mine,
     out_came,
     proj_mine,
@@ -1138,14 +1153,15 @@
                 store_sem.at[slot, 1],
             ),
             pltpu.make_async_copy(
-                total.at[slot, 2, pl.ds(0, TILE)], down_sent.at[tile_of(j)],
-                store_sem.at[slot, 2],
-            ),
-            pltpu.make_async_copy(
                 total.at[slot, 2, pl.ds(TILE, TILE)], down_kept.at[tile_of(j)],
                 store_sem.at[slot, 3],
             ),
         ]
+
+    def down_store(slot, into):
+        return pltpu.make_async_copy(
+            total.at[slot, 2, pl.ds(0, TILE)], into, store_sem.at[slot, 2]
+        )
 
     def unit_loads(j):
         return [
@@ -1204,10 +1220,24 @@
             total[slot, 2, pl.ds(part * TILE, TILE)] = turned[part * TILE : (part + 1) * TILE].T
         for store in stores(j, slot):
             store.start()
+        here = j < tiles - LAST
+
+        @pl.when(here)
+        def _():
+            store = down_store(slot, down_sent.at[tile_of(j)])
+            store.start()
+            store.wait()
+            row_copy(j)[1].start()
+
+        @pl.when(jnp.logical_not(here))
+        def _():
+            store = down_store(slot, down_last.at[tile_of(j - (tiles - LAST))])
+            store.start()
+            store.wait()
+
         for store in stores(j, slot):
             store.wait()
-        for copy in row_copy(j):
-            copy.start()
+        row_copy(j)[0].start()
 
     def x_copies(slot):
         return [
@@ -1459,8 +1489,8 @@
             copy.wait_send()
     for copy in z_copies():
         copy.wait()
-    for part in range(2):
-        loop(tiles, lambda j: row_copy(j)[part].wait())
+    loop(tiles, lambda j: row_copy(j)[0].wait())
+    loop(tiles - LAST, lambda j: row_copy(j)[1].wait())
 
 
 def last(
@@ -1483,7 +1513,8 @@
     return pl.pallas_call(
         last_kernel,
         out_shape=(
-            rows_pair, rows_pair, rows_pair, columns, columns, columns, out_block, out_block, proj_block, proj_block,
+            rows_pair, rows_pair, rows_pair, columns, columns, columns,
+            jax.ShapeDtypeStruct((LAST * TILE, TILE), F32), out_block, out_block, proj_block, proj_block,
             jax.ShapeDtypeStruct((row_count, width), F32),
             jax.ShapeDtypeStruct((row_count, width), BF16),
             wide,
@@ -1492,7 +1523,7 @@
             jax.ShapeDtypeStruct((8, 2, TILE), F32),
         ),
         in_specs=[hbm] * 12 + [vmem] + [hbm] * 11 + [vmem],
-        out_specs=(hbm,) * 15 + (vmem,),
+        out_specs=(hbm,) * 16 + (vmem,),
         scratch_shapes=[
             pltpu.VMEM((6 * half, width), BF16),
             pltpu.VMEM((6 * half, width), BF16),
@@ -1540,7 +1571,7 @@
 def finish_kernel(
     kept, came, down_kept, down_came, out_mine, out_came, proj_mine, proj_came, input_in,
     mixed_in, gains, w_gate, w_up, w_down, w_out, w_query, w_key, w_value, grad_input, mixed,
-    gain_sums,
+    gain_one, gain_two,
 ):
     w_gate[...] = kept[0] + came[0]
     w_up[...] = kept[1] + came[1]
@@ -1552,7 +1583,9 @@
     w_value[...] = proj_mine[:, queries + keys :] + proj_came[:, queries + keys :]
     grad_input[...] = input_in[...]
     mixed[...] = mixed_in[...]
-    gain_sums[...] = jnp.sum(gains[...], axis=0)
+    total = jnp.sum(gains[...], axis=0)
+    gain_one[...] = total[0:1]
+    gain_two[...] = total[1:2]
 
 
 def finish(*parts):
@@ -1576,14 +1609,18 @@
         out_shape=[jax.ShapeDtypeStruct(shape, F32) for shape in outs]
         + [
             jax.ShapeDtypeStruct(whole.shape, BF16),
-            jax.ShapeDtypeStruct(gains.shape[1:], F32),
+            jax.ShapeDtypeStruct((1, gains.shape[2]), F32),
+            jax.ShapeDtypeStruct((1, gains.shape[2]), F32),
         ],
         in_specs=[block(kept.shape, (2,))] * 2
         + [block(part.shape) for part in parts[2:10]]
         + [fixed(gains.shape)],
         out_specs=[block(shape) for shape in outs]
-        + [block(whole.shape), fixed(gains.shape[1:])],
+        + [block(whole.shape)] + [fixed((1, gains.shape[2]))] * 2,
         compiler_params=pltpu.CompilerParams(vmem_limit_bytes=64 * 1024 * 1024),
+        cost_estimate=pl.CostEstimate(
+            flops=2_000_000, bytes_accessed=34_000_000, transcendentals=0
+        ),
         name="last_sums",
     )(*parts)
 
@@ -1652,6 +1689,8 @@
             pltpu.VMEM((half, TILE), F32),
             pltpu.VMEM((8, row_count), F32),
             pltpu.VMEM((row_count, 8), F32),
+            pltpu.VMEM((row_count, 128), F32),
+            pltpu.VMEM((row_count, 128), F32),
             dma((13,)),
             dma((3, 2 * tiles)), dma((3, 2 * tiles)), dma((2, 2 * tiles)), dma((2, 2 * tiles)),
             dma((3, CHUNKS)), dma((3, CHUNKS)),
@@ -1668,8 +1707,11 @@
     )(
         w_query, w_key, w_value, w_out, tokens, cotangent,
         gain_one.reshape(1, width), gain.reshape(1, width), w_gate, w_up, w_down,
-        segment.reshape(1, row_count), cosine, sine,
-    )
+        segment.reshape(1, row_count), position.reshape(1, row_count), frequency.reshape(1, 128),
+    )
+
+
+LAST = 2
 
 
 def last_kernel(
@@ -1704,6 +1746,7 @@
     down_kept,
     down_sent,
     down_came,
+    down_last,
     out_mine,
     out_came,
     proj_mine,
@@ -1984,14 +2027,15 @@
                 store_sem.at[slot, 1],
             ),
             pltpu.make_async_copy(
-                total.at[slot, 2, pl.ds(0, TILE)], down_sent.at[tile_of(j)],
-                store_sem.at[slot, 2],
-            ),
-            pltpu.make_async_copy(
                 total.at[slot, 2, pl.ds(TILE, TILE)], down_kept.at[tile_of(j)],
                 store_sem.at[slot, 3],
             ),
         ]
+
+    def down_store(slot, into):
+        return pltpu.make_async_copy(
+            total.at[slot, 2, pl.ds(0, TILE)], into, store_sem.at[slot, 2]
+        )
 
     def unit_loads(j):
         return [
@@ -2050,10 +2094,24 @@
             total[slot, 2, pl.ds(part * TILE, TILE)] = turned[part * TILE : (part + 1) * TILE].T
         for store in stores(j, slot):
             store.start()
+        here = j < tiles - LAST
+
+        @pl.when(here)
+        def _():
+            store = down_store(slot, down_sent.at[tile_of(j)])
+            store.start()
+            store.wait()
+            row_copy(j)[1].start()
+
+        @pl.when(jnp.logical_not(here))
+        def _():
+            store = down_store(slot, down_last.at[tile_of(j - (tiles - LAST))])
+            store.start()
+            store.wait()
+
         for store in stores(j, slot):
             store.wait()
-        for copy in row_copy(j):
-            copy.start()
+        row_copy(j)[0].start()
 
     def x_copies(slot):
         return [
@@ -2305,8 +2363,8 @@
             copy.wait_send()
     for copy in z_copies():
         copy.wait()
-    for part in range(2):
-        loop(tiles, lambda j: row_copy(j)[part].wait())
+    loop(tiles, lambda j: row_copy(j)[0].wait())
+    loop(tiles - LAST, lambda j: row_copy(j)[1].wait())
 
 
 def last(
@@ -2329,7 +2387,8 @@
     return pl.pallas_call(
         last_kernel,
         out_shape=(
-            rows_pair, rows_pair, rows_pair, columns, columns, columns, out_block, out_block, proj_block, proj_block,
+            rows_pair, rows_pair, rows_pair, columns, columns, columns,
+            jax.ShapeDtypeStruct((LAST * TILE, TILE), F32), out_block, out_block, proj_block, proj_block,
             jax.ShapeDtypeStruct((row_count, width), F32),
             jax.ShapeDtypeStruct((row_count, width), BF16),
             wide,
@@ -2338,7 +2397,7 @@
             jax.ShapeDtypeStruct((8, 2, TILE), F32),
         ),
         in_specs=[hbm] * 12 + [vmem] + [hbm] * 11 + [vmem],
-        out_specs=(hbm,) * 15 + (vmem,),
+        out_specs=(hbm,) * 16 + (vmem,),
         scratch_shapes=[
             pltpu.VMEM((6 * half, width), BF16),
             pltpu.VMEM((6 * half, width), BF16),
@@ -2386,7 +2445,7 @@
 def finish_kernel(
     kept, came, down_kept, down_came, out_mine, out_came, proj_mine, proj_came, input_in,
     mixed_in, gains, w_gate, w_up, w_down, w_out, w_query, w_key, w_value, grad_input, mixed,
-    gain_sums,
+    gain_one, gain_two,
 ):
     w_gate[...] = kept[0] + came[0]
     w_up[...] = kept[1] + came[1]
@@ -2398,7 +2457,9 @@
     w_value[...] = proj_mine[:, queries + keys :] + proj_came[:, queries + keys :]
     grad_input[...] = input_in[...]
     mixed[...] = mixed_in[...]
-    gain_sums[...] = jnp.sum(gains[...], axis=0)
+    total = jnp.sum(gains[...], axis=0)
+    gain_one[...] = total[0:1]
+    gain_two[...] = total[1:2]
 
 
 def finish(*parts):
@@ -2422,14 +2483,18 @@
         out_shape=[jax.ShapeDtypeStruct(shape, F32) for shape in outs]
         + [
             jax.ShapeDtypeStruct(whole.shape, BF16),
-            jax.ShapeDtypeStruct(gains.shape[1:], F32),
+            jax.ShapeDtypeStruct((1, gains.shape[2]), F32),
+            jax.ShapeDtypeStruct((1, gains.shape[2]), F32),
         ],
         in_specs=[block(kept.shape, (2,))] * 2
         + [block(part.shape) for part in parts[2:10]]
         + [fixed(gains.shape)],
         out_specs=[block(shape) for shape in outs]
-        + [block(whole.shape), fixed(gains.shape[1:])],
+        + [block(whole.shape)] + [fixed((1, gains.shape[2]))] * 2,
         compiler_params=pltpu.CompilerParams(vmem_limit_bytes=64 * 1024 * 1024),
+        cost_estimate=pl.CostEstimate(
+            flops=2_000_000, bytes_accessed=34_000_000, transcendentals=0
+        ),
         name="last_sums",
     )(*parts)
 
@@ -2488,9 +2553,7 @@
     query_width, kv_width = w_query.shape[1], key_weight.shape[1]
     half_dim = HEAD_SIZE // 2
     frequency = 500000.0 ** (-(jnp.arange(half_dim).astype(F32) * 2.0 / HEAD_SIZE))
-    angles = positions.reshape(row_count, 1).astype(F32) * jnp.tile(frequency, 4)
-    cosine_tile = jnp.cos(angles)
-    sine_tile = jnp.sin(angles) * jnp.where(jnp.arange(128) % HEAD_SIZE < half_dim, 1.0, -1.0)
+    frequency = jnp.tile(frequency, 4)
     (
         normed_one,
         head_outputs,
@@ -2513,7 +2576,7 @@
         normed_others,
     ) = middle(
         w_query, key_weight, value_weight, w_out, tokens, cotangent,
-        attn_gain, mlp_gain, w_gate, w_up, w_down, segments, cosine_tile, sine_tile,
+        attn_gain, mlp_gain, w_gate, w_up, w_down, segments, positions, frequency,
     )
     (
         kept,
@@ -2522,6 +2585,7 @@
         down_kept,
         _,
         down_came,
+        down_last,
         out_mine,
         out_came,
         proj_mine,
@@ -2538,6 +2602,8 @@
         value_weight, head_outputs, grad_attn, grad_attn_far, normed_one, normed_one_far,
         heads_far, grad_hidden, tokens, attn_gain,
     )
+    pairs = [(i, i ^ 2) for i in range(lax.axis_size("dp"))]
+    last_came = lax.ppermute(down_last, "dp", pairs)
     (
         grad_w_gate,
         grad_w_up,
@@ -2548,12 +2614,15 @@
         grad_w_value,
         grad_input,
         mixed,
-        gains,
+        grad_attn_gain,
+        grad_mlp_gain,
     ) = finish(
         kept, came, down_kept, down_came, out_mine, out_came, proj_mine, proj_came, grad_input,
         mixed, gains,
     )
-    grad_attn_gain, grad_mlp_gain = gains[0], gains[1]
+    done = grad_w_down.shape[0] - LAST * TILE
+    grad_w_down = lax.dynamic_update_slice(grad_w_down, down_kept[done:] + last_came, (done, 0))
+    grad_attn_gain, grad_mlp_gain = grad_attn_gain[0], grad_mlp_gain[0]
     return (
         mixed,
         grad_input,

time: 385 us -> 374 us (0.971)
  Pallas kernels: 380 us -> 370 us
    pallas_call x1, Pallas kernels: 215 us -> 203 us  [last(): pl.pallas_call(last_kernel, out_shape=(rows_pair, rows_pair, rows_pair, c...]
  transfers between devices with their start and end apart: 0 -> 1, of which waited for: 0 -> 0; matrix products, arithmetic and copies ran while one was open for 0% -> 0% of each run, Pallas kernels for 0% -> 4%
where the time goes in v6:
time: 374 us
  Pallas kernels  370 us (99%)
    pallas_call x1, Pallas kernels, last(): pl.pallas_call(last_kernel, out_shape=(rows_pair, rows_pair, rows_pair, c...  203 us
    pallas_call x1, Pallas kernels, middle(): pl.pallas_call(middle_kernel, out_shape=(jax.ShapeDtypeStruct((row_count,...  153 us
    pallas_call x1, Pallas kernels, finish(): pl.pallas_call(finish_kernel, grid=(steps,), out_shape=[jax.ShapeDtypeStr...  13.4 us
  transfers between devices with their start and end apart: 1, of which 0 were waited for; matrix products, arithmetic and copies ran while one was open for 0% of the time, Pallas kernels for 4%

profile of v6, /device:TPU:0, one launch (start us, length us, event | category | flops | bytes accessed | tf_op | source)
XLA Modules:
  0.0 374.1 jit_solution(12046040801455588019)
XLA Ops:
  0.7 0.6 reshape_tile.3.frequency_ref
  1.3 152.9 %feed_forward.1 = (bf16[512,2048]{1,0:T(8,128)(2,1)}, bf16[512,512]{1,0:T(8,128)(2,1)}, bf16[512,512]{1,0:T(8,128)(2,1)}, bf16[512,512]{1,0:T(8,128)(2,1)}, bf16...) custom-call(bf16[2048,512]{1,0:T(8,128)(2,1)} %w_query_ref.3, ...), custom_call_target="tpu_custom_call" | custom-call | tf_op jit(solution)/shard_map/feed_forward/pallas_call | solution.py:779
  154.1 203.4 %weight_gradients.1 = (f32[2,256,2048]{2,1,0:T(8,128)}, f32[2,256,2048]{2,1,0:T(8,128)}, f32[2,256,2048]{2,1,0:T(8,128)}, f32[2048,256]{1,0:T(8,128)}, f32[2048,...) custom-call(f32[5,256,2048]{2,1,0:T(8,128)} %get-tuple-element.50.no, ...), custom_call_target="tpu_custom_call" | custom-call | tf_op jit(solution)/shard_map/weight_gradients/pallas_call | solution.py:2387
  357.5 1.1 collective-permute-start
  358.6 13.4 %last_sums.1 = (f32[256,2048]{1,0:T(8,128)}, f32[256,2048]{1,0:T(8,128)}, f32[2048,256]{1,0:T(8,128)}, f32[512,256]{1,0:T(8,128)}, f32[256,512]{1,0:T(8,128)}, /...) custom-call(f32[2,256,2048]{2,1,0:T(8,128)} %get-tuple-element.66.ke, ...), custom_call_target="tpu_custom_call" | custom-call | flops 2000000 | bytes 34000000 | tf_op jit(solution)/shard_map/last_sums/pallas_call | solution.py:2480
  372.1 0.0 collective-permute-done
  372.1 2.1 add_dynamic-update-slice_fusion
  (2 shorter events, 0.0 us)
Async XLA Ops:
  357.5 14.6 %collective-permute-start = (f32[512,256]{1,0:T(8,128)}, f32[512,256]{1,0:T(8,128)}, u32[]{:S(2)}, u32[]{:S(2)}) collective-permute-start(f32[512,256]{1,0:T(8,128)} %get-tuple-element.88), channel_id=1, source_target_pairs={{0,8},{4,12},{8,0},{12,4},{16,24},{20,28},{24,16},{28,20},{1,9},{5... | collective-permute-start | bytes 1572872 | tf_op jit(solution)/shard_map/ppermute | solution.py:2606

commit v7 on v6

--- a/solution.py
+++ b/solution.py
@@ -205,6 +205,14 @@
             n_send.at[1, 3], n_recv.at[1, 3], y_id,
         )
 
+    def half_to_twin(slots, which, part, window):
+        return remote(
+            slots.at[1, window], slots.at[4, window],
+            twin_send.at[which, 1 + part], twin_recv.at[which, 1 + part], twin_id,
+        )
+
+    first_run, last_run = pl.ds(0, run), pl.ds(run, run)
+    other_quarter = pl.ds(pl.multiple_of((1 - y_bit) * run, run), run)
     quarter = pl.ds(pl.multiple_of(y_bit * run, run), run)
 
     def quarter_z():
@@ -535,6 +543,7 @@
     pl.semaphore_signal(free_sem, inc=1, device_id=twin_id, device_id_type=MESH)
     quarter_z().wait()
     quarter_zx().start()
+    half_to_twin(cot_others, 0, 0, quarter).start()
 
     for block in range(2):
         loop(tiles, lambda j: core_copy(1, block_window(block, j), block * tiles + j).wait_send())
@@ -693,6 +702,7 @@
             for k in (0, 1):
                 from_z(normed_sent, normed_others, k, n_send, n_recv).wait_recv()
                 from_zx(normed_others, k, n_send, n_recv).start()
+            half_to_twin(normed_others, 1, 0, first_run).start()
             for k in range(CHUNKS):
                 from_x(cot_half, cot_others, k, cot_send, cot_recv).wait()
             to_twin(cot_others, 0, 0).start()
@@ -739,9 +749,9 @@
         from_x(normed_sent, normed_others, k, n_send, n_recv).wait_recv()
     to_twin(normed_others, 1, 0).start()
     quarter_y().wait()
-    to_twin(cot_others, 0, 1).start()
+    half_to_twin(cot_others, 0, 1, other_quarter).start()
     last_y().wait()
-    to_twin(normed_others, 1, 1).start()
+    half_to_twin(normed_others, 1, 1, last_run).start()
 
     for store in grad_stores + [projected_store, branch_store]:
         store.wait()
@@ -757,9 +767,12 @@
     for block in range(2):
         loop(tiles, lambda j: y_copy(1, block_window(block, j), block * tiles + j).wait_send())
     loop(tiles, lambda j: core_copy(2, (everything, tile_of(j)), j).wait_send())
-    for slot in range(2):
-        to_twin(cot_others, 0, slot).wait()
-        to_twin(normed_others, 1, slot).wait()
+    to_twin(cot_others, 0, 0).wait()
+    to_twin(normed_others, 1, 0).wait()
+    half_to_twin(cot_others, 0, 0, quarter).wait()
+    half_to_twin(cot_others, 0, 1, other_quarter).wait()
+    half_to_twin(normed_others, 1, 0, first_run).wait()
+    half_to_twin(normed_others, 1, 1, last_run).wait()
 
 
 def middle(
@@ -821,7 +834,7 @@
             dma((3, 2 * tiles)), dma((3, 2 * tiles)), dma((2, 2 * tiles)), dma((2, 2 * tiles)),
             dma((3, CHUNKS)), dma((3, CHUNKS)),
             dma((4, CHUNKS)), dma((4, CHUNKS)),
-            dma((2, 2)), dma((2, 2)),
+            dma((2, 3)), dma((2, 3)),
             dma((CHUNKS,)), dma((CHUNKS,)),
             dma((8,)), dma((8,)),
             pltpu.SemaphoreType.REGULAR,
@@ -1036,7 +1049,7 @@
             ),
         ]
 
-    order = [0, 1, 3, 4, 6, 7, 9, 10, 2, 5, 8, 11]
+    order = [0, 1, 3, 4, 6, 7, 9, 10, 2, 8, 5, 11]
     for i in range(2):
         for load in piece_load(order[i], i):
             load.start()
@@ -1106,18 +1119,10 @@
             turned_to[pl.ds(part * TILE, TILE), pl.ds(row_count + base, half)] = (
                 staged[slot, :, block].T.astype(BF16)
             )
-        if place == 5:
-            for copy, later in zip(late_copies[:2], late_twins):
+        if place == 8:
+            for copy in late_copies[2:] + late_twins:
                 copy.wait()
-                later.start()
-            branch_copy.start()
-        if place == 6:
-            for copy in late_copies[2:]:
-                copy.wait()
-        if place == 7:
-            for copy in late_twins:
-                copy.wait()
-        if place + 2 < 12:
+        if place + 2 < 8 or 8 <= place < 10:
             for load in piece_load(order[place + 2], slot):
                 load.start()
     for place in range(8):
@@ -1205,6 +1210,13 @@
 
         if first:
             loop(2, block)
+            for copy, later in zip(late_copies[:2], late_twins):
+                copy.wait()
+                later.start()
+            branch_copy.start()
+            for place in (8, 9):
+                for load in piece_load(order[place], place % 2):
+                    load.start()
             for place in range(8, 12):
                 take_piece(place)
             block(2)
@@ -1695,7 +1707,7 @@
             dma((3, 2 * tiles)), dma((3, 2 * tiles)), dma((2, 2 * tiles)), dma((2, 2 * tiles)),
             dma((3, CHUNKS)), dma((3, CHUNKS)),
             dma((4, CHUNKS)), dma((4, CHUNKS)),
-            dma((2, 2)), dma((2, 2)),
+            dma((2, 3)), dma((2, 3)),
             dma((CHUNKS,)), dma((CHUNKS,)),
             dma((8,)), dma((8,)),
             pltpu.SemaphoreType.REGULAR,
@@ -1910,7 +1922,7 @@
             ),
         ]
 
-    order = [0, 1, 3, 4, 6, 7, 9, 10, 2, 5, 8, 11]
+    order = [0, 1, 3, 4, 6, 7, 9, 10, 2, 8, 5, 11]
     for i in range(2):
         for load in piece_load(order[i], i):
             load.start()
@@ -1980,18 +1992,10 @@
             turned_to[pl.ds(part * TILE, TILE), pl.ds(row_count + base, half)] = (
                 staged[slot, :, block].T.astype(BF16)
             )
-        if place == 5:
-            for copy, later in zip(late_copies[:2], late_twins):
+        if place == 8:
+            for copy in late_copies[2:] + late_twins:
                 copy.wait()
-                later.start()
-            branch_copy.start()
-        if place == 6:
-            for copy in late_copies[2:]:
-                copy.wait()
-        if place == 7:
-            for copy in late_twins:
-                copy.wait()
-        if place + 2 < 12:
+        if place + 2 < 8 or 8 <= place < 10:
             for load in piece_load(order[place + 2], slot):
                 load.start()
     for place in range(8):
@@ -2079,6 +2083,13 @@
 
         if first:
             loop(2, block)
+            for copy, later in zip(late_copies[:2], late_twins):
+                copy.wait()
+                later.start()
+            branch_copy.start()
+            for place in (8, 9):
+                for load in piece_load(order[place], place % 2):
+                    load.start()
             for place in range(8, 12):
                 take_piece(place)
             block(2)

time: 374 us -> 369 us (0.987)
  Pallas kernels: 370 us -> 364 us
    pallas_call x1, Pallas kernels: 203 us -> 199 us  [last(): pl.pallas_call(last_kernel, out_shape=(rows_pair, rows_pair, rows_pair, c...]
where the time goes in v7:
time: 369 us; the launch traced here: 368 us
  Pallas kernels  364 us (99%)
    pallas_call x1, Pallas kernels, last(): pl.pallas_call(last_kernel, out_shape=(rows_pair, rows_pair, rows_pair, c...  199 us
    pallas_call x1, Pallas kernels, middle(): pl.pallas_call(middle_kernel, out_shape=(jax.ShapeDtypeStruct((row_count,...  151 us
    pallas_call x1, Pallas kernels, finish(): pl.pallas_call(finish_kernel, grid=(steps,), out_shape=[jax.ShapeDtypeStr...  13.4 us
  transfers between devices with their start and end apart: 1, of which 0 were waited for; matrix products, arithmetic and copies ran while one was open for 0% of the time, Pallas kernels for 4%

profile of v7, /device:TPU:0, one launch (start us, length us, event | category | flops | bytes accessed | tf_op | source)
XLA Modules:
  0.0 368.2 jit_solution(4431043509938323181)
XLA Ops:
  0.7 0.6 reshape_tile.3.frequency_ref
  1.3 151.4 %feed_forward.1 = (bf16[512,2048]{1,0:T(8,128)(2,1)}, bf16[512,512]{1,0:T(8,128)(2,1)}, bf16[512,512]{1,0:T(8,128)(2,1)}, bf16[512,512]{1,0:T(8,128)(2,1)}, bf16...) custom-call(bf16[2048,512]{1,0:T(8,128)(2,1)} %w_query_ref.3, ...), custom_call_target="tpu_custom_call" | custom-call | tf_op jit(solution)/shard_map/feed_forward/pallas_call | solution.py:792
  152.7 198.9 %weight_gradients.1 = (f32[2,256,2048]{2,1,0:T(8,128)}, f32[2,256,2048]{2,1,0:T(8,128)}, f32[2,256,2048]{2,1,0:T(8,128)}, f32[2048,256]{1,0:T(8,128)}, f32[2048,...) custom-call(f32[5,256,2048]{2,1,0:T(8,128)} %get-tuple-element.50.no, ...), custom_call_target="tpu_custom_call" | custom-call | tf_op jit(solution)/shard_map/weight_gradients/pallas_call | solution.py:2398
  351.6 1.1 collective-permute-start
  352.7 13.4 %last_sums.1 = (f32[256,2048]{1,0:T(8,128)}, f32[256,2048]{1,0:T(8,128)}, f32[2048,256]{1,0:T(8,128)}, f32[512,256]{1,0:T(8,128)}, f32[256,512]{1,0:T(8,128)}, /...) custom-call(f32[2,256,2048]{2,1,0:T(8,128)} %get-tuple-element.66.ke, ...), custom_call_target="tpu_custom_call" | custom-call | flops 2000000 | bytes 34000000 | tf_op jit(solution)/shard_map/last_sums/pallas_call | solution.py:2491
  366.1 0.0 collective-permute-done
  366.1 2.1 add_dynamic-update-slice_fusion
  (2 shorter events, 0.0 us)
Async XLA Ops:
  351.6 14.6 %collective-permute-start = (f32[512,256]{1,0:T(8,128)}, f32[512,256]{1,0:T(8,128)}, u32[]{:S(2)}, u32[]{:S(2)}) collective-permute-start(f32[512,256]{1,0:T(8,128)} %get-tuple-element.88), channel_id=1, source_target_pairs={{0,8},{4,12},{8,0},{12,4},{16,24},{20,28},{24,16},{28,20},{1,9},{5... | collective-permute-start | bytes 1572872 | tf_op jit(solution)/shard_map/ppermute | solution.py:2617

commit v8 on v7

--- a/solution.py
+++ b/solution.py
@@ -271,11 +271,14 @@
     )
 
     places = jnp.broadcast_to(position_ref[...].astype(F32), (8, row_count)).T
-    angles = places[:, 0:1] * frequency_ref[...]
-    cosine_ref[...] = jnp.cos(angles)
-    signs = lax.broadcasted_iota(jnp.int32, (row_count, 128), 1) % 64 < 32
-    sines = jnp.sin(angles)
-    sine_ref[...] = jnp.where(signs, sines, -sines)
+
+    def make_tables(block):
+        window = pl.ds(block * half, half)
+        angles = places[block * half : (block + 1) * half, 0:1] * frequency_ref[...]
+        cosine_ref[window, :] = jnp.cos(angles)
+        sines = jnp.sin(angles)
+        signs = lax.broadcasted_iota(jnp.int32, (half, 128), 1) % 64 < 32
+        sine_ref[window, :] = jnp.where(signs, sines, -sines)
 
     lane = lax.broadcasted_iota(jnp.int32, (TILE, 128), 1)
     factor = HEAD_SIZE ** (-0.5)
@@ -389,6 +392,7 @@
     for name in ("query", "key", "value", "w_out"):
         loads[name].wait()
     for block in range(2):
+        make_tables(block)
         project_in(block)
         loop(query_width // 128, functools.partial(attend, block))
 
@@ -1601,7 +1605,7 @@
 
 
 def finish(*parts):
-    steps = 8
+    steps = 4
     kept, down, out, proj, whole, gains = (parts[i] for i in (0, 2, 4, 6, 8, 10))
     rows, units = kept.shape[1:]
 
@@ -2474,7 +2478,7 @@
 
 
 def finish(*parts):
-    steps = 8
+    steps = 4
     kept, down, out, proj, whole, gains = (parts[i] for i in (0, 2, 4, 6, 8, 10))
     rows, units = kept.shape[1:]
 

time: 369 us -> 367 us (level)
  transfers between devices with their start and end apart: 1 -> 1, of which waited for: 0 -> 1; matrix products, arithmetic and copies ran while one was open for 0% -> 0% of each run, Pallas kernels for 4% -> 3%
where the time goes in v8:
time: 367 us
  Pallas kernels  362 us (99%)
    pallas_call x1, Pallas kernels, last(): pl.pallas_call(last_kernel, out_shape=(rows_pair, rows_pair, rows_pair, c...  199 us
    pallas_call x1, Pallas kernels, middle(): pl.pallas_call(middle_kernel, out_shape=(jax.ShapeDtypeStruct((row_count,...  151 us
    pallas_call x1, Pallas kernels, finish(): pl.pallas_call(finish_kernel, grid=(steps,), out_shape=[jax.ShapeDtypeStr...  12.2 us
  transfers between devices with their start and end apart: 1, of which 1 were waited for; matrix products, arithmetic and copies ran while one was open for 0% of the time, Pallas kernels for 3%

profile of v8, /device:TPU:0, one launch (start us, length us, event | category | flops | bytes accessed | tf_op | source)
XLA Modules:
  0.0 366.9 jit_solution(3340689921265826247)
XLA Ops:
  0.7 0.6 reshape_tile.3.frequency_ref
  1.3 151.0 %feed_forward.1 = (bf16[512,2048]{1,0:T(8,128)(2,1)}, bf16[512,512]{1,0:T(8,128)(2,1)}, bf16[512,512]{1,0:T(8,128)(2,1)}, bf16[512,512]{1,0:T(8,128)(2,1)}, bf16...) custom-call(bf16[2048,512]{1,0:T(8,128)(2,1)} %w_query_ref.3, ...), custom_call_target="tpu_custom_call" | custom-call | tf_op jit(solution)/shard_map/feed_forward/pallas_call | solution.py:796
  152.3 198.9 %weight_gradients.1 = (f32[2,256,2048]{2,1,0:T(8,128)}, f32[2,256,2048]{2,1,0:T(8,128)}, f32[2,256,2048]{2,1,0:T(8,128)}, f32[2048,256]{1,0:T(8,128)}, f32[2048,...) custom-call(f32[5,256,2048]{2,1,0:T(8,128)} %get-tuple-element.50.no, ...), custom_call_target="tpu_custom_call" | custom-call | tf_op jit(solution)/shard_map/weight_gradients/pallas_call | solution.py:2402
  351.1 1.1 collective-permute-start
  352.3 12.2 %last_sums.1 = (f32[256,2048]{1,0:T(8,128)}, f32[256,2048]{1,0:T(8,128)}, f32[2048,256]{1,0:T(8,128)}, f32[512,256]{1,0:T(8,128)}, f32[256,512]{1,0:T(8,128)}, /...) custom-call(f32[2,256,2048]{2,1,0:T(8,128)} %get-tuple-element.66.ke, ...), custom_call_target="tpu_custom_call" | custom-call | flops 2000000 | bytes 34000000 | tf_op jit(solution)/shard_map/last_sums/pallas_call | solution.py:2495
  364.5 0.4 collective-permute-done
  364.9 2.1 add_dynamic-update-slice_fusion
  (2 shorter events, 0.0 us)
Async XLA Ops:
  351.1 13.7 %collective-permute-start = (f32[512,256]{1,0:T(8,128)}, f32[512,256]{1,0:T(8,128)}, u32[]{:S(2)}, u32[]{:S(2)}) collective-permute-start(f32[512,256]{1,0:T(8,128)} %get-tuple-element.88), channel_id=1, source_target_pairs={{0,8},{4,12},{8,0},{12,4},{16,24},{20,28},{24,16},{28,20},{1,9},{5... | collective-permute-start | bytes 1572872 | tf_op jit(solution)/shard_map/ppermute | solution.py:2621

commit v9 on v8

--- a/solution.py
+++ b/solution.py
@@ -2,6 +2,7 @@
 
 import jax
 import jax.numpy as jnp
+import numpy as np
 from jax import lax
 from jax.experimental import pallas as pl
 from jax.experimental.pallas import tpu as pltpu
@@ -53,6 +54,7 @@
     grad_hidden_out,
     grad_attn_out,
     projected_out,
+    projected_wide,
     grad_attn_far,
     branch_out,
     normed_out,
@@ -621,7 +623,9 @@
             sums[:, columns] = sums[:, columns] + value[part * TILE : (part + 1) * TILE]
 
     def put(block, column, value):
-        gu[pl.ds(block * TILE, TILE), pl.ds(column, 128)] = value.astype(BF16)
+        rounded = value.astype(BF16)
+        gu[pl.ds(block * TILE, TILE), pl.ds(column, 128)] = rounded
+        core_in[1, :, pl.ds(block * 768 + column, 128)] = rounded.astype(F32)
 
     def attend_back(block, p):
         kv = p // 2
@@ -732,7 +736,14 @@
     projected_store = pltpu.make_async_copy(
         gu.at[:, pl.ds(0, 768)], projected_out, local_sem.at[6]
     )
-    projected_store.start()
+    wide_stores = [
+        pltpu.make_async_copy(
+            core_in.at[1, :, pl.ds(b * 768, 768)], projected_wide.at[b], local_sem.at[b]
+        )
+        for b in range(2)
+    ]
+    for store in [projected_store] + wide_stores:
+        store.start()
 
     last_z().wait()
     last_y().start()
@@ -757,7 +768,7 @@
     last_y().wait()
     half_to_twin(normed_others, 1, 1, last_run).start()
 
-    for store in grad_stores + [projected_store, branch_store]:
+    for store in grad_stores + wide_stores + [projected_store, branch_store]:
         store.wait()
     for copy in (hidden_far_twin, normed_one_twin, quarter_zx()):
         copy.wait()
@@ -803,6 +814,7 @@
             wide,
             jax.ShapeDtypeStruct((row_count, width), BF16),
             jax.ShapeDtypeStruct((row_count, 768), BF16),
+            jax.ShapeDtypeStruct((2, half, 768), F32),
             jax.ShapeDtypeStruct((2, half, width // 2), F32),
             wide,
             jax.ShapeDtypeStruct((row_count, width), BF16),
@@ -812,7 +824,7 @@
             jax.ShapeDtypeStruct((5, half, width), F32),
         ),
         in_specs=[hbm] * 6 + [vmem] * 2 + [hbm] * 3 + [vmem] * 3,
-        out_specs=(hbm,) * 16 + (vmem,) + (hbm,) * 2,
+        out_specs=(hbm,) * 17 + (vmem,) + (hbm,) * 2,
         scratch_shapes=[
             pltpu.VMEM(w_gate.shape, BF16),
             pltpu.VMEM(w_up.shape, BF16),
@@ -850,7 +862,7 @@
     )(
         w_query, w_key, w_value, w_out, tokens, cotangent,
         gain_one.reshape(1, width), gain.reshape(1, width), w_gate, w_up, w_down,
-        segment.reshape(1, row_count), position.reshape(1, row_count), frequency.reshape(1, 128),
+        segment.reshape(1, row_count), position.reshape(1, row_count), jnp.asarray(frequency).reshape(1, 128),
     )
 
 
@@ -869,6 +881,7 @@
     w_up_ref,
     w_down_ref,
     projected_ref,
+    projected_wide_ref,
     branch_ref,
     gain_two_ref,
     w_query_ref,
@@ -1057,7 +1070,6 @@
     for i in range(2):
         for load in piece_load(order[i], i):
             load.start()
-    loads[13].start()
     for load in loads[:4]:
         load.start()
     for load in weight_loads(0, 0):
@@ -1073,6 +1085,10 @@
     for device in [twin_id, y_id] + [(peer, tensor) for peer in peers]:
         pl.semaphore_signal(barrier, inc=1, device_id=device, device_id_type=MESH)
     pl.semaphore_wait(barrier, 9)
+    projected_copy = remote(
+        projected_wide_ref, far_staged, end_send.at[2], end_recv.at[2], far_id
+    )
+    projected_copy.start()
     late_copies = [
         remote(normed_others_ref.at[1, late_normed], normed_late.at[0, late_normed],
                late_send.at[0], late_recv.at[0], x_id),
@@ -1085,18 +1101,6 @@
     ]
     for copy in late_copies:
         copy.start()
-
-    loads[13].wait()
-
-    def widen(r):
-        window = pl.ds(pl.multiple_of(r * ROWS, ROWS), ROWS)
-        for s in range(2):
-            there = pl.ds(pl.multiple_of(s * half + r * ROWS, ROWS), ROWS)
-            proj_part[0, s, window, :] = projected[0, there, :].astype(F32)
-
-    loop(half // ROWS, widen)
-    projected_copy = remote(proj_part.at[0], far_staged, end_send.at[2], end_recv.at[2], far_id)
-    projected_copy.start()
     branch_copy = remote(branch_ref, branch_came, end_send.at[1], end_recv.at[1], y_id)
 
     late_twins = [
@@ -1264,7 +1268,7 @@
         ]
 
     def attention_parts():
-        for load in far_loads + loads[8:13]:
+        for load in far_loads + loads[8:14]:
             load.wait()
         projected_copy.wait()
 
@@ -1345,7 +1349,7 @@
         loop(tiles, lambda j: core_copy(j).wait_send())
 
     feed_forward_tile(0, first=True)
-    for load in loads[4:13] + loads[14:]:
+    for load in loads[4:]:
         load.start()
     far_loads = (
         [
@@ -1511,7 +1515,7 @@
 
 def last(
     normed_others, cot_others, normed, cot, act, gg, gu, w_gate, w_up, w_down,
-    projected, branch, gain_two, w_query, w_key, w_value, heads, grad_attn, grad_attn_far,
+    projected, projected_wide, branch, gain_two, w_query, w_key, w_value, heads, grad_attn, grad_attn_far,
     normed_one, normed_one_far, heads_far, grad_hidden, tokens, gain,
 ):
     row_count, width = tokens.shape
@@ -1538,7 +1542,7 @@
             jax.ShapeDtypeStruct((2, half, width), F32),
             jax.ShapeDtypeStruct((8, 2, TILE), F32),
         ),
-        in_specs=[hbm] * 12 + [vmem] + [hbm] * 11 + [vmem],
+        in_specs=[hbm] * 13 + [vmem] + [hbm] * 11 + [vmem],
         out_specs=(hbm,) * 16 + (vmem,),
         scratch_shapes=[
             pltpu.VMEM((6 * half, width), BF16),
@@ -1579,7 +1583,7 @@
         name="weight_gradients",
     )(
         normed_others, cot_others, normed, cot, act, gg, gu, w_gate, w_up, w_down,
-        projected, branch, gain_two, w_query, w_key, w_value, heads, grad_attn, grad_attn_far,
+        projected, projected_wide, branch, gain_two, w_query, w_key, w_value, heads, grad_attn, grad_attn_far,
         normed_one, normed_one_far, heads_far, grad_hidden, tokens, gain.reshape(1, width),
     )
 
@@ -1676,6 +1680,7 @@
             wide,
             jax.ShapeDtypeStruct((row_count, width), BF16),
             jax.ShapeDtypeStruct((row_count, 768), BF16),
+            jax.ShapeDtypeStruct((2, half, 768), F32),
             jax.ShapeDtypeStruct((2, half, width // 2), F32),
             wide,
             jax.ShapeDtypeStruct((row_count, width), BF16),
@@ -1685,7 +1690,7 @@
             jax.ShapeDtypeStruct((5, half, width), F32),
         ),
         in_specs=[hbm] * 6 + [vmem] * 2 + [hbm] * 3 + [vmem] * 3,
-        out_specs=(hbm,) * 16 + (vmem,) + (hbm,) * 2,
+        out_specs=(hbm,) * 17 + (vmem,) + (hbm,) * 2,
         scratch_shapes=[
             pltpu.VMEM(w_gate.shape, BF16),
             pltpu.VMEM(w_up.shape, BF16),
@@ -1723,7 +1728,7 @@
     )(
         w_query, w_key, w_value, w_out, tokens, cotangent,
         gain_one.reshape(1, width), gain.reshape(1, width), w_gate, w_up, w_down,
-        segment.reshape(1, row_count), position.reshape(1, row_count), frequency.reshape(1, 128),
+        segment.reshape(1, row_count), position.reshape(1, row_count), jnp.asarray(frequency).reshape(1, 128),
     )
 
 
@@ -1742,6 +1747,7 @@
     w_up_ref,
     w_down_ref,
     projected_ref,
+    projected_wide_ref,
     branch_ref,
     gain_two_ref,
     w_query_ref,
@@ -1930,7 +1936,6 @@
     for i in range(2):
         for load in piece_load(order[i], i):
             load.start()
-    loads[13].start()
     for load in loads[:4]:
         load.start()
     for load in weight_loads(0, 0):
@@ -1946,6 +1951,10 @@
     for device in [twin_id, y_id] + [(peer, tensor) for peer in peers]:
         pl.semaphore_signal(barrier, inc=1, device_id=device, device_id_type=MESH)
     pl.semaphore_wait(barrier, 9)
+    projected_copy = remote(
+        projected_wide_ref, far_staged, end_send.at[2], end_recv.at[2], far_id
+    )
+    projected_copy.start()
     late_copies = [
         remote(normed_others_ref.at[1, late_normed], normed_late.at[0, late_normed],
                late_send.at[0], late_recv.at[0], x_id),
@@ -1958,18 +1967,6 @@
     ]
     for copy in late_copies:
         copy.start()
-
-    loads[13].wait()
-
-    def widen(r):
-        window = pl.ds(pl.multiple_of(r * ROWS, ROWS), ROWS)
-        for s in range(2):
-            there = pl.ds(pl.multiple_of(s * half + r * ROWS, ROWS), ROWS)
-            proj_part[0, s, window, :] = projected[0, there, :].astype(F32)
-
-    loop(half // ROWS, widen)
-    projected_copy = remote(proj_part.at[0], far_staged, end_send.at[2], end_recv.at[2], far_id)
-    projected_copy.start()
     branch_copy = remote(branch_ref, branch_came, end_send.at[1], end_recv.at[1], y_id)
 
     late_twins = [
@@ -2137,7 +2134,7 @@
         ]
 
     def attention_parts():
-        for load in far_loads + loads[8:13]:
+        for load in far_loads + loads[8:14]:
             load.wait()
         projected_copy.wait()
 
@@ -2218,7 +2215,7 @@
         loop(tiles, lambda j: core_copy(j).wait_send())
 
     feed_forward_tile(0, first=True)
-    for load in loads[4:13] + loads[14:]:
+    for load in loads[4:]:
         load.start()
     far_loads = (
         [
@@ -2384,7 +2381,7 @@
 
 def last(
     normed_others, cot_others, normed, cot, act, gg, gu, w_gate, w_up, w_down,
-    projected, branch, gain_two, w_query, w_key, w_value, heads, grad_attn, grad_attn_far,
+    projected, projected_wide, branch, gain_two, w_query, w_key, w_value, heads, grad_attn, grad_attn_far,
     normed_one, normed_one_far, heads_far, grad_hidden, tokens, gain,
 ):
     row_count, width = tokens.shape
@@ -2411,7 +2408,7 @@
             jax.ShapeDtypeStruct((2, half, width), F32),
             jax.ShapeDtypeStruct((8, 2, TILE), F32),
         ),
-        in_specs=[hbm] * 12 + [vmem] + [hbm] * 11 + [vmem],
+        in_specs=[hbm] * 13 + [vmem] + [hbm] * 11 + [vmem],
         out_specs=(hbm,) * 16 + (vmem,),
         scratch_shapes=[
             pltpu.VMEM((6 * half, width), BF16),
@@ -2452,7 +2449,7 @@
         name="weight_gradients",
     )(
         normed_others, cot_others, normed, cot, act, gg, gu, w_gate, w_up, w_down,
-        projected, branch, gain_two, w_query, w_key, w_value, heads, grad_attn, grad_attn_far,
+        projected, projected_wide, branch, gain_two, w_query, w_key, w_value, heads, grad_attn, grad_attn_far,
         normed_one, normed_one_far, heads_far, grad_hidden, tokens, gain.reshape(1, width),
     )
 
@@ -2567,8 +2564,8 @@
     row_count, width = tokens.shape
     query_width, kv_width = w_query.shape[1], key_weight.shape[1]
     half_dim = HEAD_SIZE // 2
-    frequency = 500000.0 ** (-(jnp.arange(half_dim).astype(F32) * 2.0 / HEAD_SIZE))
-    frequency = jnp.tile(frequency, 4)
+    steps = np.arange(half_dim, dtype=np.float32) * 2.0 / HEAD_SIZE
+    frequency = np.tile((500000.0 ** -steps).astype(np.float32), 4)
     (
         normed_one,
         head_outputs,
@@ -2580,6 +2577,7 @@
         grad_hidden,
         grad_attn,
         projected,
+        projected_wide,
         grad_attn_far,
         branch,
         normed_two,
@@ -2613,7 +2611,7 @@
         gains,
     ) = last(
         normed_others, cotangent_others, normed_two, cotangent, activation, grad_gate_in,
-        grad_up_in, w_gate, w_up, w_down, projected, branch, gain_two_half, w_query, key_weight,
+        grad_up_in, w_gate, w_up, w_down, projected, projected_wide, branch, gain_two_half, w_query, key_weight,
         value_weight, head_outputs, grad_attn, grad_attn_far, normed_one, normed_one_far,
         heads_far, grad_hidden, tokens, attn_gain,
     )

time: 367 us -> 367 us (level)
  no operation moved by 1% of the time
where the time goes in v9:
time: 367 us; the launch traced here: 366 us
  Pallas kernels  362 us (99%)
    pallas_call x1, Pallas kernels, last(): pl.pallas_call(last_kernel, out_shape=(rows_pair, rows_pair, rows_pair, c...  199 us
    pallas_call x1, Pallas kernels, middle(): pl.pallas_call(middle_kernel, out_shape=(jax.ShapeDtypeStruct((row_count,...  151 us
    pallas_call x1, Pallas kernels, finish(): pl.pallas_call(finish_kernel, grid=(steps,), out_shape=[jax.ShapeDtypeStr...  12.2 us
  transfers between devices with their start and end apart: 1, of which 1 were waited for; matrix products, arithmetic and copies ran while one was open for 0% of the time, Pallas kernels for 3%

profile of v9, /device:TPU:0, one launch (start us, length us, event | category | flops | bytes accessed | tf_op | source)
XLA Modules:
  0.0 366.4 jit_solution(8841135443177264222)
XLA Ops:
  0.6 151.1 %feed_forward.1 = (bf16[512,2048]{1,0:T(8,128)(2,1)}, bf16[512,512]{1,0:T(8,128)(2,1)}, bf16[512,512]{1,0:T(8,128)(2,1)}, bf16[512,512]{1,0:T(8,128)(2,1)}, bf16...) custom-call(bf16[2048,512]{1,0:T(8,128)(2,1)} %w_query_ref.3, ...), custom_call_target="tpu_custom_call" | custom-call | tf_op jit(solution)/shard_map/feed_forward/pallas_call | solution.py:807
  151.7 198.9 %weight_gradients.1 = (f32[2,256,2048]{2,1,0:T(8,128)}, f32[2,256,2048]{2,1,0:T(8,128)}, f32[2,256,2048]{2,1,0:T(8,128)}, f32[2048,256]{1,0:T(8,128)}, f32[2048,...) custom-call(f32[5,256,2048]{2,1,0:T(8,128)} %get-tuple-element.51.no, ...), custom_call_target="tpu_custom_call" | custom-call | tf_op jit(solution)/shard_map/weight_gradients/pallas_call | solution.py:2399
  350.6 1.1 collective-permute-start
  351.8 12.2 %last_sums.1 = (f32[256,2048]{1,0:T(8,128)}, f32[256,2048]{1,0:T(8,128)}, f32[2048,256]{1,0:T(8,128)}, f32[512,256]{1,0:T(8,128)}, f32[256,512]{1,0:T(8,128)}, /...) custom-call(f32[2,256,2048]{2,1,0:T(8,128)} %get-tuple-element.68.ke, ...), custom_call_target="tpu_custom_call" | custom-call | flops 2000000 | bytes 34000000 | tf_op jit(solution)/shard_map/last_sums/pallas_call | solution.py:2492
  364.0 0.3 collective-permute-done
  364.3 2.1 add_dynamic-update-slice_fusion
Async XLA Ops:
  350.6 13.7 %collective-permute-start = (f32[512,256]{1,0:T(8,128)}, f32[512,256]{1,0:T(8,128)}, u32[]{:S(2)}, u32[]{:S(2)}) collective-permute-start(f32[512,256]{1,0:T(8,128)} %get-tuple-element.90), channel_id=1, source_target_pairs={{0,8},{4,12},{8,0},{12,4},{16,24},{20,28},{24,16},{28,20},{1,9},{5... | collective-permute-start | bytes 1572872 | tf_op jit(solution)/shard_map/ppermute | solution.py:2619
